TPU v7x, 32 devices: a whole 2x2x4 slice. The times are simulated.
32 devices in a mesh: batch: 8 (over z, y), tm: 4 (over x, core).
Axes of the slice: x: 2, y: 2, z: 4, core: 2. Of those that a mesh axis runs over, the one named last changes fastest.
Arguments:
- signal: float32 [16, 512, 512], P('batch', None, 'tm'), may hold values from -6 to 6
- quant_cot: float32 [16, 64, 1024], P('batch', 'tm'), may hold values from -6 to 6
- commit_cot: float32 [16, 9, 64], P('batch', None, 'tm'), may hold values from -6 to 6
- lengths: int32 [16], P('batch'), may hold values from 85 to 512, as said below
- codes: int32 [16, 9, 64], P('batch', None, 'tm'), may hold values from 0 to 1023
- wide_weight: bfloat16 [3, 512, 7, 512], replicated, may hold values from -0.09375 to 0.09375
- wide_bias: float32 [3, 512], replicated, may hold values from -1.8 to 1.8
- narrow_weight: bfloat16 [3, 512, 512], replicated, may hold values from -0.25 to 0.25
- narrow_bias: float32 [3, 512], replicated, may hold values from -1.8 to 1.8
- snake_alpha: float32 [7, 512], replicated, may hold values from 0.5 to 1
- down_weight: bfloat16 [1024, 16, 512], replicated, may hold values from -0.0625 to 0.0625
- down_bias: float32 [1024], replicated, may hold values from -1.8 to 1.8
- in_weight: float32 [9, 8, 1024], replicated, may hold values from -0.1875 to 0.1875
- in_bias: float32 [9, 8], replicated, may hold values from -1.8 to 1.8
- codebook: float32 [9, 8, 1024], replicated, may hold values from -6 to 6
- out_weight: float32 [9, 8, 1024], replicated, may hold values from -0.75 to 0.75
- out_bias: float32 [9, 1024], replicated, may hold values from -0.6 to 0.6
Outputs:
- quantized: float32 [16, 64, 1024], P('batch', 'tm')
- commit: float32 [16, 9, 64], P('batch', None, 'tm')
- signal_grad: float32 [16, 512, 512], P('batch', None, 'tm')
- wide_weight_grad: float32 [3, 512, 7, 512], P(None, 'tm')
- wide_bias_grad: float32 [3, 512], P(None, 'tm')
- narrow_weight_grad: float32 [3, 512, 512], P(None, 'tm')
- narrow_bias_grad: float32 [3, 512], P(None, 'tm')
- alpha_grad: float32 [7, 512], P(None, 'tm')
- down_weight_grad: float32 [1024, 16, 512], P('tm')
- down_bias_grad: float32 [1024], P('tm')
- in_weight_grad: float32 [9, 8, 1024], P(None, None, 'tm')
- in_bias_grad: float32 [9, 8], P(None, 'tm')
- codebook_grad: float32 [9, 8, 1024], P(None, None, 'tm')
- out_weight_grad: float32 [9, 8, 1024], P(None, None, 'tm')
- out_bias_grad: float32 [9, 1024], P(None, 'tm')
Inputs may be any that keep to these rules, and one draw needn't show every extreme that they name: `lengths`: in each group of 2 crops that one index of batch holds, one crop has the full length 512; the others are drawn evenly.
All inputs are finite; a program needn't handle non-finite values.
Results may differ from a plain program's by a relative error of at most 0.035.
The roundings to bfloat16 on the way count: a program that leaves them out, or rounds other values in their place, can miss the bound.
Values may be sent and summed in bfloat16 or wider, within the bound.
A program may use at most 320 MiB of HBM per device.

v0:
```python
import math

import jax
import jax.numpy as jnp
from jax import lax
from jax.sharding import PartitionSpec as P

STRIDE = 8


DILATIONS = (1, 3, 9)
SHARD_DIMS = (1, 1, 1, 1, 1, 0, 0, 2, 1, 2, 2, 1)


def with_halo(block, sides, width):
    for axis, dim in sides:
        count = lax.axis_size(axis)
        forward = [(i, i + 1) for i in range(count - 1)]
        backward = [(target, source) for source, target in forward]
        low = lax.ppermute(
            lax.slice_in_dim(block, block.shape[dim] - width, None, axis=dim), axis, forward
        )
        high = lax.ppermute(lax.slice_in_dim(block, 0, width, axis=dim), axis, backward)
        block = jnp.concatenate([low, block, high], axis=dim)
    return block


def snake(values, alphas):
    factor = alphas[None, :, None]
    return values + jnp.square(jnp.sin(factor * values)) / factor


def snake_back(values, alphas, upstream):
    factor = alphas[None, :, None]
    double_sin = jnp.sin(2.0 * factor * values)
    square = jnp.square(jnp.sin(factor * values))
    grad_values = upstream * (1.0 + double_sin)
    grad_alphas = jnp.sum(
        upstream * (values * double_sin / factor - square / jnp.square(factor)), axis=(0, 2)
    )
    return (grad_values, grad_alphas)


def stacked_windows(padded, dilation, extent, backward):
    pieces = []
    for tap_index in range(7):
        offset = (6 - tap_index if backward else tap_index) * dilation
        pieces.append(lax.slice_in_dim(padded, offset, offset + extent, axis=2))
    return jnp.stack(pieces, axis=1)


def wide_conv(padded, weight, bias, dilation, extent):
    windows = stacked_windows(padded, dilation, extent, False)
    return (
        jnp.einsum("oki,bkit->bot", weight, windows, preferred_element_type=jnp.float32)
        + bias[None, :, None]
    )


def narrow_conv(rounded, weight, bias):
    return (
        jnp.einsum("oi,bit->bot", weight, rounded, preferred_element_type=jnp.float32)
        + bias[None, :, None]
    )


def unit_forward(hidden, number, unit_weights):
    wide_weight, wide_bias, narrow_weight, narrow_bias, snake_alpha = unit_weights
    dilation = DILATIONS[number]
    length = hidden.shape[2]
    snaked = snake(hidden, snake_alpha[2 * number]).astype(jnp.bfloat16)
    padded = with_halo(snaked, (("tm", 2),), 3 * dilation)
    conv_out = wide_conv(padded, wide_weight[number], wide_bias[number], dilation, length)
    rounded = snake(conv_out, snake_alpha[2 * number + 1]).astype(jnp.bfloat16)
    return (padded, conv_out, rounded)


def pack_grads(gradients, time_count):
    rows = [
        jnp.moveaxis(gradient, dim_index, 0).reshape(time_count, -1)
        for gradient, dim_index in zip(gradients, SHARD_DIMS)
    ]
    return jnp.concatenate(rows, axis=1)


def unpack_grads(flattened, gradients, time_count):
    pieces = []
    offset = 0
    for gradient, dim_index in zip(gradients, SHARD_DIMS):
        moved = jnp.moveaxis(gradient, dim_index, 0).shape
        layout = (moved[0] // time_count,) + tuple(moved[1:])
        extent = math.prod(layout)
        segment = flattened[offset : offset + extent].reshape(layout)
        pieces.append(jnp.moveaxis(segment, 0, dim_index))
        offset = offset + extent
    return tuple(pieces)


def body(
    signal,
    quant_cot,
    commit_cot,
    lengths,
    codes,
    wide_weight,
    wide_bias,
    narrow_weight,
    narrow_bias,
    snake_alpha,
    down_weight,
    down_bias,
    in_weight,
    in_bias,
    codebook,
    out_weight,
    out_bias,
):
    crop_count, channel_count, length = signal.shape
    places = lax.axis_index("tm") * length + jnp.arange(length, dtype=jnp.int32)
    valid = (places[None, :] < lengths[:, None]).astype(jnp.float32)[:, None, :]
    unit_weights = (wide_weight, wide_bias, narrow_weight, narrow_bias, snake_alpha)
    current = signal * valid
    hiddens = [current]
    for number in range(3):
        padded, conv_out, rounded = unit_forward(current, number, unit_weights)
        current = current + narrow_conv(rounded, narrow_weight[number], narrow_bias[number])
        hiddens.append(current)
    mixed = (snake(current, snake_alpha[6]) * valid).astype(jnp.bfloat16)
    edged = with_halo(mixed, (("tm", 2),), STRIDE // 2)
    frame_count = length // STRIDE
    blocks = edged.reshape(crop_count, channel_count, frame_count + 1, STRIDE)
    frame_windows = jnp.concatenate([blocks[:, :, :frame_count], blocks[:, :, 1:]], axis=3)
    latent = (
        jnp.einsum("cki,bifk->bfc", down_weight, frame_windows, preferred_element_type=jnp.float32)
        + down_bias[None, None, :]
    )
    frame_places = lax.axis_index("tm") * frame_count + jnp.arange(frame_count, dtype=jnp.int32)
    frame_valid = (STRIDE * frame_places[None, :] < lengths[:, None]).astype(jnp.float32)
    code_range = jnp.arange(codebook.shape[2], dtype=jnp.int32)
    phase_count = in_weight.shape[0]
    residual = latent
    quantized = jnp.zeros_like(latent)
    commits = []
    phase_saved = []
    for phase_index in range(phase_count):
        onehot = (codes[:, phase_index, :, None] == code_range).astype(jnp.float32)
        encoded = (
            jnp.einsum(
                "dc,bfc->bfd", in_weight[phase_index], residual, precision=lax.Precision.HIGHEST
            )
            + in_bias[phase_index]
        )
        looked = jnp.einsum(
            "bfn,dn->bfd", onehot, codebook[phase_index], precision=lax.Precision.HIGHEST
        )
        added_term = (
            jnp.einsum(
                "dc,bfd->bfc", out_weight[phase_index], looked, precision=lax.Precision.HIGHEST
            )
            + out_bias[phase_index]
        )
        spread_gap = encoded - looked
        commits.append(jnp.sum(jnp.square(spread_gap), axis=2) * frame_valid)
        phase_saved.append((residual, onehot, looked, spread_gap))
        residual = residual - added_term
        quantized = quantized + added_term
    quantized_out = quantized * frame_valid[:, :, None]
    commit_out = jnp.stack(commits, axis=1)
    quant_grad = quant_cot * frame_valid[:, :, None]
    carried = jnp.zeros_like(latent)
    in_weight_grads = [None] * phase_count
    in_bias_grads = [None] * phase_count
    codebook_grads = [None] * phase_count
    out_weight_grads = [None] * phase_count
    out_bias_grads = [None] * phase_count
    for phase_index in reversed(range(phase_count)):
        phase_input, onehot, looked, spread_gap = phase_saved[phase_index]
        gap_grad = 2.0 * (commit_cot[:, phase_index, :] * frame_valid)[:, :, None] * spread_gap
        push_grad = quant_grad - carried
        out_bias_grads[phase_index] = jnp.sum(push_grad, axis=(0, 1))
        out_weight_grads[phase_index] = jnp.einsum(
            "bfd,bfc->dc", looked, push_grad, precision=lax.Precision.HIGHEST
        )
        looked_grad = (
            jnp.einsum(
                "dc,bfc->bfd", out_weight[phase_index], push_grad, precision=lax.Precision.HIGHEST
            )
            - gap_grad
        )
        codebook_grads[phase_index] = jnp.einsum(
            "bfn,bfd->dn", onehot, looked_grad, precision=lax.Precision.HIGHEST
        )
        in_bias_grads[phase_index] = jnp.sum(gap_grad, axis=(0, 1))
        in_weight_grads[phase_index] = jnp.einsum(
            "bfd,bfc->dc", gap_grad, phase_input, precision=lax.Precision.HIGHEST
        )
        carried = carried + jnp.einsum(
            "dc,bfd->bfc", in_weight[phase_index], gap_grad, precision=lax.Precision.HIGHEST
        )
    latent_low = carried.astype(jnp.bfloat16)
    down_bias_grad = jnp.sum(latent_low, axis=(0, 1), dtype=jnp.float32)
    down_weight_grad = jnp.einsum(
        "bfc,bifk->cki", latent_low, frame_windows, preferred_element_type=jnp.float32
    )
    frame_edges = with_halo(latent_low, (("tm", 1),), 1)
    spread_back = jnp.einsum(
        "cki,bfc->bifk", down_weight, frame_edges, preferred_element_type=jnp.float32
    )
    leading = jnp.pad(spread_back[:, :, :, :STRIDE], ((0, 0), (0, 0), (0, 1), (0, 0)))
    trailing = jnp.pad(spread_back[:, :, :, STRIDE:], ((0, 0), (0, 0), (1, 0), (0, 0)))
    joined = (leading + trailing).reshape(crop_count, channel_count, (frame_count + 3) * STRIDE)
    first_place = STRIDE + STRIDE // 2
    mixed_grad = joined[:, :, first_place : first_place + length]
    upstream, alpha_last = snake_back(current, snake_alpha[6], mixed_grad * valid)
    alpha_rows = [None] * 7
    alpha_rows[6] = alpha_last
    wide_grads = [None] * 3
    wide_bias_grads = [None] * 3
    narrow_grads = [None] * 3
    narrow_bias_grads = [None] * 3
    for number in reversed(range(3)):
        dilation = DILATIONS[number]
        rim_width = 3 * dilation
        hidden_in = hiddens[number]
        padded, conv_out, rounded = unit_forward(hidden_in, number, unit_weights)
        grad_branch = upstream.astype(jnp.bfloat16)
        narrow_bias_grads[number] = jnp.sum(grad_branch, axis=(0, 2), dtype=jnp.float32)
        narrow_grads[number] = jnp.einsum(
            "bot,bit->oi", grad_branch, rounded, preferred_element_type=jnp.float32
        )
        grad_rounded = jnp.einsum(
            "oi,bot->bit", narrow_weight[number], grad_branch, preferred_element_type=jnp.float32
        )
        grad_conv, alpha_rows[2 * number + 1] = snake_back(
            conv_out, snake_alpha[2 * number + 1], grad_rounded
        )
        grad_conv = grad_conv.astype(jnp.bfloat16)
        wide_bias_grads[number] = jnp.sum(grad_conv, axis=(0, 2), dtype=jnp.float32)
        windows = stacked_windows(padded, dilation, length, False)
        wide_grads[number] = jnp.einsum(
            "bot,bkit->oki", grad_conv, windows, preferred_element_type=jnp.float32
        )
        grad_padded = with_halo(grad_conv, (("tm", 2),), rim_width)
        grad_windows = stacked_windows(grad_padded, dilation, length, True)
        grad_snaked = jnp.einsum(
            "oki,bkot->bit", wide_weight[number], grad_windows, preferred_element_type=jnp.float32
        )
        grad_hidden, alpha_rows[2 * number] = snake_back(
            hidden_in, snake_alpha[2 * number], grad_snaked
        )
        upstream = upstream + grad_hidden
    signal_grad = upstream * valid
    gradients = (
        jnp.stack(wide_grads),
        jnp.stack(wide_bias_grads),
        jnp.stack(narrow_grads),
        jnp.stack(narrow_bias_grads),
        jnp.stack(alpha_rows),
        down_weight_grad,
        down_bias_grad,
        jnp.stack(in_weight_grads),
        jnp.stack(in_bias_grads),
        jnp.stack(codebook_grads),
        jnp.stack(out_weight_grads),
        jnp.stack(out_bias_grads),
    )
    time_count = lax.axis_size("tm")
    packed = pack_grads(gradients, time_count)
    shares = lax.psum_scatter(
        packed.astype(jnp.bfloat16), "tm", scatter_dimension=0, tiled=True
    ).astype(jnp.float32)
    summed = lax.psum(shares[0], "batch")
    restored = unpack_grads(summed, gradients, time_count)
    return (
        quantized_out,
        commit_out,
        signal_grad,
        restored[0],
        restored[1],
        restored[2],
        restored[3],
        restored[4],
        restored[5],
        restored[6],
        restored[7],
        restored[8],
        restored[9],
        restored[10],
        restored[11],
    )


def solution(mesh):
    return jax.shard_map(
        body,
        mesh=mesh,
        in_specs=(
            P("batch", None, "tm"),
            P("batch", "tm", None),
            P("batch", None, "tm"),
            P("batch"),
            P("batch", None, "tm"),
            P(),
            P(),
            P(),
            P(),
            P(),
            P(),
            P(),
            P(),
            P(),
            P(),
            P(),
            P(),
        ),
        out_specs=(
            P("batch", "tm", None),
            P("batch", None, "tm"),
            P("batch", None, "tm"),
            P(None, "tm", None, None),
            P(None, "tm"),
            P(None, "tm", None),
            P(None, "tm"),
            P(None, "tm"),
            P("tm", None, None),
            P("tm"),
            P(None, None, "tm"),
            P(None, "tm"),
            P(None, None, "tm"),
            P(None, None, "tm"),
            P(None, "tm"),
        ),
        check_vma=False,
    )
```

profile of v0, /device:TPU:0, one launch (start us, length us, event | category | flops | bytes accessed | tf_op | source)
XLA Modules:
  0.0 1626.2 jit_solution(1594261433658186396)
XLA Ops:
  10.4 1.9 add_convert_fusion.5
  13.6 3.0 collective-permute-start
  28.1 2.0 bitcast_dynamic-update-slice_fusion
  30.4 3.9 fusion.77
  34.3 3.6 add_convert_fusion.3
  37.9 4.5 collective-permute-start.2
  47.5 3.6 add_convert_fusion.1
  51.2 4.5 collective-permute-start.4
  60.5 4.3 multiply_convert_fusion.3
  64.8 4.4 collective-permute-start.6
  72.6 28.7 %fusion.85 = f32[2,16,1024]{2,1,0:T(8,128)S(1)} fusion(bf16[2,512,16,16]{1,2,3,0:T(8,128)(2,1)S(1)} %copy_dynamic-update-slice_fusion, bf16[1024,16,512]{2,1,0:T(8,128)(2,1)} %param.27, f32[1024]{0:T(1024)S(1)} %copy-done.192), kind=kOutput, calls=%fused_computation.90 | convolution fusion | flops 536903680 | bytes 17436672 | tf_op jit(solution)/shard_map/cki,bifk->bfc/dot_general | solution.py:134
  103.5 1.7 subtract_subtract_fusion
  106.9 2.0 convolution_subtract_fusion
  121.2 1.9 fusion.481
  126.2 8.2 fusion
  143.5 4.4 collective-permute-start.8
  154.3 4.6 copy.189
  158.9 4.7 reshape.988
  163.6 4.6 copy.190
  168.2 5.3 reshape.989
  173.5 4.6 copy.187
  178.2 5.3 reshape.986
  183.5 24.3 %copy.186 = bf16[1024,16,512]{2,1,0:T(8,128)(2,1)} copy(bf16[1024,16,512]{0,2,1:T(8,128)(2,1)} %fusion) | data formatting | bytes 33554432 | tf_op jit(solution)/shard_map/bfc,bifk->cki/transpose | solution.py:202
  207.8 26.5 %reshape.984 = bf16[4,2097152]{1,0:T(4,128)(2,1)} reshape(bf16[1024,16,512]{2,1,0:T(8,128)(2,1)} %copy.186) | data formatting | bytes 33554432 | tf_op jit(solution)/shard_map/reshape | solution.py:80
  234.3 12.8 fusion.29
  248.3 1.9 fusion.497
  250.2 2.0 fusion.501
  252.3 3.0 fusion.9
  256.5 3.6 multiply_reduce_fusion.1
  260.2 3.0 fusion.35
  264.3 3.7 collective-permute-start.11
  269.1 6.3 convert_reduce_fusion.1
  275.4 1.9 fusion.500
  277.4 3.0 fusion.8
  281.7 3.6 multiply_reduce_fusion.2
  285.3 3.6 multiply_reduce_fusion.3
  289.0 2.9 fusion.36
  293.6 4.8 collective-permute-start.13
  299.6 5.5 convert_reduce_fusion
  305.1 2.7 fusion.37
  307.8 3.2 fusion.499
  311.6 3.0 fusion.10
  317.2 3.0 reshape.981
  323.9 5.7 maximum_bitcast_fusion
  329.6 30.5 %copy.175 = bf16[512,3,7,512]{3,2,1,0:T(8,128)(2,1)} copy(bf16[512,3,7,512]{3,0,2,1:T(8,128)(2,1)S(1)} %maximum_bitcast_fusion) | data formatting | bytes 22020096 | tf_op jit(solution)/shard_map/transpose | solution.py:80
  360.1 20.5 %reshape.979 = bf16[4,1376256]{1,0:T(4,128)(2,1)} reshape(bf16[512,3,7,512]{3,2,1,0:T(8,128)(2,1)} %copy.175) | data formatting | bytes 22020096 | tf_op jit(solution)/shard_map/reshape | solution.py:80
  380.6 10.2 constant_dynamic-update-slice_fusion.16
  390.8 3.8 multiply_reduce_fusion.4
  394.7 3.6 multiply_reduce_fusion.5
  401.1 5.2 collective-permute-start.15
  409.0 11.2 multiply_reduce_fusion
  421.4 12.1 constant_dynamic-update-slice_fusion.11
  436.1 2.8 dynamic-update-slice.9
  438.9 2.7 dynamic-update-slice.10
  441.6 1.6 dynamic-update-slice.11
  444.5 500.7 %all-reduce.8.cloned.1.call-done = bf16[4,3729554]{1,0:T(4,128)(2,1)} async-done(((bf16[4,3729554]{1,0:T(4,128)(2,1)}), bf16[4,3729554]{1,0:T(4,128)(2,1)}) %all-reduce.8.cloned.1.call-update) | async-done | bytes 29836448
  945.1 161.7 %fusion.5 = f32[3729554]{0:T(1024)} fusion(bf16[4,3729554]{1,0:T(4,128)(2,1)} %all-reduce.8.cloned.1.call-done, u32[]{:T(128)} %bitcast.313), kind=kLoop, calls=%fused_computation.7 | loop fusion | flops 3729554 | bytes 22377328 | tf_op jit(solution)/shard_map/squeeze | solution.py:272
  1108.3 1.7 fusion.84
  1111.0 455.9 %all-reduce.6.cloned.1.call-done = f32[3729554]{0:T(1024)} async-done(((f32[3729554]{0:T(1024)}), f32[3729554]{0:T(1024)}) %all-reduce.6.cloned.1.call-update) | async-done | bytes 14918232 | tf_op jit(solution)/shard_map/psum | solution.py:272
  1582.6 5.7 slice.799
  1588.3 9.3 reshape.996
  1597.6 4.4 slice.794
  1602.0 7.2 reshape.991
  1609.2 8.4 copy.193
  (650 shorter events, 107.4 us)
Async XLA Ops:
  7.2 17.1 %copy-start.66 = (s32[2]{0:T(128)S(1)}, s32[2]{0:T(128)}, u32[]{:S(2)}) copy-start(s32[2]{0:T(128)} %param.20) | copy-start | bytes 28
  7.2 16.4 %copy-start.96 = (f32[9,1024]{1,0:T(8,128)S(1)}, f32[9,1024]{1,0:T(8,128)}, u32[]{:S(2)}) copy-start(f32[9,1024]{1,0:T(8,128)} %param.33) | copy-start | bytes 110596
  7.2 17.0 %copy-start.119 = (f32[2,9,16]{2,0,1:T(2,128)S(1)}, f32[2,9,16]{2,0,1:T(2,128)}, u32[]{:S(2)}) copy-start(f32[2,9,16]{2,0,1:T(2,128)} %param.19) | copy-start | bytes 3460
  7.3 17.7 %copy-start.24 = (f32[9,8,1024]{2,1,0:T(8,128)S(1)}, f32[9,8,1024]{2,1,0:T(8,128)}, u32[]{:S(2)}) copy-start(f32[9,8,1024]{2,1,0:T(8,128)} %param.32) | copy-start | bytes 884740
  7.3 937.9 %all-reduce.8.cloned.1.call-start = ((), (), s32[]{:S(2)}) async-start(), calls=%async_computation.1 | async-start | bytes 59674624
  8.3 19.8 %copy-start.72 = (f32[1,512]{1,0:T(1,128)}, f32[1,512]{1,0:T(1,128)S(1)}, u32[]{:S(2)}) copy-start(f32[1,512]{1,0:T(1,128)S(1)} %get-tuple-element.192) | copy-start | bytes 6148
  8.3 26.0 %copy-start.101 = (f32[1,512]{1,0:T(1,128)}, f32[1,512]{1,0:T(1,128)S(1)}, u32[]{:S(2)}) copy-start(f32[1,512]{1,0:T(1,128)S(1)} %get-tuple-element.191) | copy-start | bytes 6148
  8.3 26.0 %copy-start.104 = (f32[1,512]{1,0:T(1,128)}, f32[1,512]{1,0:T(1,128)S(1)}, u32[]{:S(2)}) copy-start(f32[1,512]{1,0:T(1,128)S(1)} %get-tuple-element.190) | copy-start | bytes 6148
  8.3 39.2 %copy-start.106 = (f32[1,512]{1,0:T(1,128)}, f32[1,512]{1,0:T(1,128)S(1)}, u32[]{:S(2)}) copy-start(f32[1,512]{1,0:T(1,128)S(1)} %get-tuple-element.189) | copy-start | bytes 6148
  8.4 39.2 %copy-start.108 = (f32[1,512]{1,0:T(1,128)}, f32[1,512]{1,0:T(1,128)S(1)}, u32[]{:S(2)}) copy-start(f32[1,512]{1,0:T(1,128)S(1)} %get-tuple-element.188) | copy-start | bytes 6148
  8.4 52.1 %copy-start.110 = (f32[1,512]{1,0:T(1,128)}, f32[1,512]{1,0:T(1,128)S(1)}, u32[]{:S(2)}) copy-start(f32[1,512]{1,0:T(1,128)S(1)} %get-tuple-element.193) | copy-start | bytes 6148
  8.4 52.1 %copy-start.140 = (f32[1,512]{1,0:T(1,128)}, f32[1,512]{1,0:T(1,128)S(1)}, u32[]{:S(2)}) copy-start(f32[1,512]{1,0:T(1,128)S(1)} %get-tuple-element.187) | copy-start | bytes 6148
  10.4 50.1 %copy-start.112 = (f32[2,128]{1,0:T(2,128)}, f32[2,128]{1,0:T(2,128)S(1)}, u32[]{:S(2)}) copy-start(f32[2,128]{1,0:T(2,128)S(1)} %compare_convert_fusion.1) | copy-start | bytes 3076
  12.3 17.8 %collective-permute-start.1 = (bf16[2,512,3]{1,2,0:T(4,128)(2,1)S(1)}, bf16[2,512,3]{1,2,0:T(4,128)(2,1)S(1)}, u32[]{:S(2)}, u32[]{:S(2)}) collective-permute-start(bf16[2,512,3]{1,2,0:T(4,128)(2,1)S(1)} %get-tuple-element.158), channel_id=1, source_target_pairs={{1,0},{2,1},{3,2},{5,4},{6,5},{7,6},{9,8},{10,9},{11,10},{13,12},{... | collective-permute-start | bytes 18440 | tf_op jit(solution)/shard_map/ppermute | solution.py:23
  13.6 14.2 collective-permute-start
  17.3 38.5 %copy-start.68 = (s32[16]{0:T(128)}, s32[16]{0:T(128)S(1)}, u32[]{:S(2)}) copy-start(s32[16]{0:T(128)S(1)} %add_multiply_fusion.2) | copy-start | bytes 196
  20.0 95.4 %copy-start.62 = (f32[2,16,8]{1,2,0:T(8,128)}, f32[2,16,8]{1,2,0:T(8,128)S(1)}, u32[]{:S(2)}) copy-start(f32[2,16,8]{1,2,0:T(8,128)S(1)} %fusion.296) | copy-start | bytes 3076
  20.4 81.0 %copy-start.64 = (f32[2,16,8]{1,2,0:T(8,128)}, f32[2,16,8]{1,2,0:T(8,128)S(1)}, u32[]{:S(2)}) copy-start(f32[2,16,8]{1,2,0:T(8,128)S(1)} %fusion.298) | copy-start | bytes 3076
  20.8 121.7 %copy-start.56 = (f32[2,16,8]{1,2,0:T(8,128)}, f32[2,16,8]{1,2,0:T(8,128)S(1)}, u32[]{:S(2)}) copy-start(f32[2,16,8]{1,2,0:T(8,128)S(1)} %fusion.290) | copy-start | bytes 3076
  25.0 77.7 %copy-start.90 = (f32[2,16]{1,0:T(2,128)}, f32[2,16]{1,0:T(2,128)S(1)}, u32[]{:S(2)}) copy-start(f32[2,16]{1,0:T(2,128)S(1)} %get-tuple-element.201) | copy-start | bytes 388
  25.0 84.0 %copy-start.74 = (f32[2,16]{1,0:T(2,128)}, f32[2,16]{1,0:T(2,128)S(1)}, u32[]{:S(2)}) copy-start(f32[2,16]{1,0:T(2,128)S(1)} %get-tuple-element.200) | copy-start | bytes 388
  25.0 89.1 %copy-start.80 = (f32[2,16]{1,0:T(2,128)}, f32[2,16]{1,0:T(2,128)S(1)}, u32[]{:S(2)}) copy-start(f32[2,16]{1,0:T(2,128)S(1)} %get-tuple-element.196) | copy-start | bytes 388
  26.6 76.9 %copy-start.26 = (f32[2,16,1024]{2,1,0:T(8,128)}, f32[2,16,1024]{2,1,0:T(8,128)S(1)}, u32[]{:S(2)}) copy-start(f32[2,16,1024]{2,1,0:T(8,128)S(1)} %convolution_add_fusion.15) | copy-start | bytes 393220
  26.9 76.6 %copy-start.28 = (f32[2,16,1024]{2,1,0:T(8,128)}, f32[2,16,1024]{2,1,0:T(8,128)S(1)}, u32[]{:S(2)}) copy-start(f32[2,16,1024]{2,1,0:T(8,128)S(1)} %convolution_add_fusion.17) | copy-start | bytes 393220
  27.2 76.3 %copy-start.30 = (f32[2,16,1024]{2,1,0:T(8,128)}, f32[2,16,1024]{2,1,0:T(8,128)S(1)}, u32[]{:S(2)}) copy-start(f32[2,16,1024]{2,1,0:T(8,128)S(1)} %convolution_add_fusion.19) | copy-start | bytes 393220
  27.9 18.4 %slice-start = ((s8[11010048]{0:T(1024)(128)(4,1)}), s8[2621440]{0:T(1024)(128)(4,1)S(1)}, s32[]{:S(2)}) async-start(s8[11010048]{0:T(1024)(128)(4,1)} %bitcast.1158), calls=%async_computation.2 | async-start | bytes 5242880
  30.4 16.0 slice-start.1
  37.9 6.6 collective-permute-start.2
  43.0 3.1 collective-permute-start.3
  51.2 5.9 collective-permute-start.4
  55.9 51.0 %copy-start.92 = (f32[2,16]{1,0:T(2,128)}, f32[2,16]{1,0:T(2,128)S(1)}, u32[]{:S(2)}) copy-start(f32[2,16]{1,0:T(2,128)S(1)} %compare_convert_fusion) | copy-start | bytes 388
  55.9 3.1 collective-permute-start.5
  64.8 6.0 collective-permute-start.6
  69.2 3.1 collective-permute-start.7
  72.5 28.8 %copy-start.15 = (f32[9,8,1024]{2,1,0:T(8,128)S(1)}, f32[9,8,1024]{2,1,0:T(8,128)}, u32[]{:S(2)}) copy-start(f32[9,8,1024]{2,1,0:T(8,128)} %param.29) | copy-start | bytes 884740
  135.8 15.4 copy-start.142
  135.8 15.4 copy-start.173
  136.0 15.4 copy-start.160
  136.0 15.4 copy-start.161
  136.1 15.4 copy-start.162
  136.1 16.1 copy-start.138
  136.1 16.1 copy-start.137
  136.2 16.1 copy-start.136
  136.2 16.2 copy-start.135
  136.2 16.2 copy-start.134
  136.2 16.2 copy-start.133
  136.2 16.2 copy-start.132
  136.2 16.2 copy-start.131
  136.2 16.2 copy-start.130
  136.2 16.2 copy-start.139
  143.5 90.8 %collective-permute-start.8 = (bf16[2,1,1024]{2,1,0:T(2,128)(2,1)}, bf16[2,1,1024]{2,1,0:T(2,128)(2,1)}, u32[]{:S(2)}, u32[]{:S(2)}) collective-permute-start(bf16[2,1,1024]{2,1,0:T(2,128)(2,1)} %get-tuple-element.176), channel_id=1, source_target_pairs={{0,1},{1,2},{2,3},{4,5},{5,6},{6,7},{8,9},{9,10},{10,11},{12,13},{... | collective-permute-start | bytes 12296 | tf_op jit(solution)/shard_map/ppermute | solution.py:20
  147.8 86.4 %collective-permute-start.9 = (bf16[2,1,1024]{2,1,0:T(2,128)(2,1)}, bf16[2,1,1024]{2,1,0:T(2,128)(2,1)}, u32[]{:S(2)}, u32[]{:S(2)}) collective-permute-start(bf16[2,1,1024]{2,1,0:T(2,128)(2,1)} %get-tuple-element.177), channel_id=1, source_target_pairs={{1,0},{2,1},{3,2},{5,4},{6,5},{7,6},{9,8},{10,9},{11,10},{13,12},{... | collective-permute-start | bytes 12296 | tf_op jit(solution)/shard_map/ppermute | solution.py:23
  207.8 26.5 %copy-start.49 = (bf16[2,16,1024]{2,1,0:T(8,128)(2,1)S(1)}, bf16[2,16,1024]{2,1,0:T(8,128)(2,1)}, u32[]{:S(2)}) copy-start(bf16[2,16,1024]{2,1,0:T(8,128)(2,1)} %copy-done.48) | copy-start | bytes 196612
  247.9 21.2 %copy-start.3 = (f32[2,512,19,8]{1,3,2,0:T(8,128)}, f32[2,512,19,8]{1,3,2,0:T(8,128)S(1)}, u32[]{:S(2)}) copy-start(f32[2,512,19,8]{1,3,2,0:T(8,128)S(1)} %copy.247) | copy-start | bytes 1867780
  255.2 12.7 collective-permute-start.10
  264.3 4.5 collective-permute-start.11
  280.4 18.1 %collective-permute-start.12 = (bf16[2,512,9]{1,2,0:T(8,128)(2,1)S(1)}, bf16[2,512,9]{1,2,0:T(8,128)(2,1)S(1)}, u32[]{:S(2)}, u32[]{:S(2)}) collective-permute-start(bf16[2,512,9]{1,2,0:T(8,128)(2,1)S(1)} %get-tuple-element.149), channel_id=1, source_target_pairs={{1,0},{2,1},{3,2},{5,4},{6,5},{7,6},{9,8},{10,9},{11,10},{13,12},{... | collective-permute-start | bytes 55304 | tf_op jit(solution)/shard_map/ppermute | solution.py:23
  293.6 5.7 collective-permute-start.13
  320.9 85.4 %collective-permute-start.14 = (bf16[2,512,3]{1,2,0:T(4,128)(2,1)}, bf16[2,512,3]{1,2,0:T(4,128)(2,1)}, u32[]{:S(2)}, u32[]{:S(2)}) collective-permute-start(bf16[2,512,3]{1,2,0:T(4,128)(2,1)} %get-tuple-element.147), channel_id=1, source_target_pairs={{1,0},{2,1},{3,2},{5,4},{6,5},{7,6},{9,8},{10,9},{11,10},{13,12},{... | collective-permute-start | bytes 18440 | tf_op jit(solution)/shard_map/ppermute | solution.py:23
  401.1 7.6 collective-permute-start.15
  421.3 17.5 %copy-start.32 = (bf16[4,18432]{1,0:T(4,128)(2,1)S(1)}, bf16[4,18432]{1,0:T(4,128)(2,1)}, u32[]{:S(2)}) copy-start(bf16[4,18432]{1,0:T(4,128)(2,1)} %reshape.989) | copy-start | bytes 442372
  421.4 20.3 %copy-start.58 = (bf16[4,2304]{1,0:T(4,128)(2,1)S(1)}, bf16[4,2304]{1,0:T(4,128)(2,1)}, u32[]{:S(2)}) copy-start(bf16[4,2304]{1,0:T(4,128)(2,1)} %reshape.990) | copy-start | bytes 55300
  443.2 1123.7 %all-reduce.6.cloned.1.call-start = ((), (), s32[]{:S(2)}) async-start(), calls=%async_computation | async-start | bytes 29843456 | tf_op jit(solution)/shard_map/psum | solution.py:272
  1108.2 466.8 %copy-start.190 = (f32[2,9,16]{2,0,1:T(2,128)}, f32[2,9,16]{2,0,1:T(2,128)S(1)}, u32[]{:S(2)}) copy-start(f32[2,9,16]{2,0,1:T(2,128)S(1)} %constant_dynamic-update-slice_fusion) | copy-start | bytes 3460
  (151 other events, 1061.4 us)
Sparse Core Ops, SparseCore 0:
  443.4 501.7 all-reduce.7
  1107.2 459.7 all-reduce.5
where the time goes:
time: 1640 us; the launch traced here: 1630 us
  waiting for transfers between devices  962 us (59%)
  local copies, waits for them, and re-layouts  241 us (15%)
  other arithmetic  204 us (12%)
  matrix products  156 us (10%)
  starting transfers between devices  45.2 us (3%)
  between operations  17.9 us (1%)
    unnamed x3, waiting for transfers between devices  501 us
    psum x1, waiting for transfers between devices, body(): summed = lax.psum(shares[0], 'batch')  456 us
    squeeze x1, other arithmetic, body(): summed = lax.psum(shares[0], 'batch')  162 us
    reshape x12, local copies, waits for them, and re-layouts, pack_grads(): jnp.moveaxis(gradient, dim_index, 0).reshape(time_count, -1)  69.3 us
    unnamed x423, local copies, waits for them, and re-layouts  55.8 us
    transpose x10, local copies, waits for them, and re-layouts, pack_grads(): jnp.moveaxis(gradient, dim_index, 0).reshape(time_count, -1)  46.5 us
    ppermute x8, starting transfers between devices, with_halo(): lax.ppermute(lax.slice_in_dim(block, block.shape[dim] - width, None, axis...  34.4 us
  transfers between devices with their start and end apart: 18, of which 7 were waited for; matrix products, arithmetic and copies ran while one was open for 13% of the time, Pallas kernels for 0%

commit v1 on v0

--- a/solution.py
+++ b/solution.py
@@ -1,15 +1,18 @@
-import math
+import functools
 
 import jax
 import jax.numpy as jnp
 from jax import lax
+from jax.experimental import pallas as pl
+from jax.experimental.pallas import tpu as pltpu
 from jax.sharding import PartitionSpec as P
 
 STRIDE = 8
 
 
 DILATIONS = (1, 3, 9)
-SHARD_DIMS = (1, 1, 1, 1, 1, 0, 0, 2, 1, 2, 2, 1)
+MESH = pl.DeviceIdType.MESH
+BLOCK = 64
 
 
 def with_halo(block, sides, width):
@@ -75,25 +78,196 @@
     return (padded, conv_out, rounded)
 
 
-def pack_grads(gradients, time_count):
-    rows = [
-        jnp.moveaxis(gradient, dim_index, 0).reshape(time_count, -1)
-        for gradient, dim_index in zip(gradients, SHARD_DIMS)
-    ]
-    return jnp.concatenate(rows, axis=1)
-
-
-def unpack_grads(flattened, gradients, time_count):
-    pieces = []
-    offset = 0
-    for gradient, dim_index in zip(gradients, SHARD_DIMS):
-        moved = jnp.moveaxis(gradient, dim_index, 0).shape
-        layout = (moved[0] // time_count,) + tuple(moved[1:])
-        extent = math.prod(layout)
-        segment = flattened[offset : offset + extent].reshape(layout)
-        pieces.append(jnp.moveaxis(segment, 0, dim_index))
-        offset = offset + extent
-    return tuple(pieces)
+def add_rows(rows, sources, target):
+    def step(index, carry):
+        at = index * BLOCK
+        total = None
+        for ref, start in sources:
+            block = ref[pl.ds(start + at, BLOCK), :].astype(jnp.float32)
+            total = block if total is None else total + block
+        ref, start = target
+        ref[pl.ds(start + at, BLOCK), :] = total.astype(ref.dtype)
+        return carry
+
+    lax.fori_loop(0, rows // BLOCK, step, 0)
+
+
+def reduce_kernel(pieces, batch_size, packed, final, own, from_core, to_x, from_x, to_y, from_y, to_z, from_z, local_sems, send_sems, recv_sems):
+    members = batch_size // 2
+    batch = lax.axis_index("batch")
+    time = lax.axis_index("tm")
+    low, high = lax.rem(time, 2), time // 2
+    core = 2 * high + 1 - low
+    across = 2 * (1 - high) + low
+    half = lax.rem(batch, 2)
+    place = batch // 2
+    pair = 2 * place + 1 - half
+
+    def member(step):
+        return 2 * lax.rem(place + step, members) + half
+
+    barrier = pltpu.get_barrier_semaphore()
+    peers = [(batch, core), (batch, across), (pair, time)]
+    peers += [(member(step), time) for step in range(1, members)]
+    for peer in peers:
+        pl.semaphore_signal(barrier, inc=1, device_id=peer, device_id_type=MESH)
+    pl.semaphore_wait(barrier, len(peers))
+
+    def send(source, target, number, slot, device):
+        return pltpu.make_async_remote_copy(
+            src_ref=source,
+            dst_ref=target,
+            send_sem=send_sems.at[number, slot],
+            recv_sem=recv_sems.at[number, slot],
+            device_id=device,
+            device_id_type=MESH,
+        )
+
+    spread = members - 1
+    slot_y, slot_z, slot_back, slot_last = 3, 4, 4 + spread, 4 + 2 * spread
+    copies = {}
+    for number, (start, rows) in enumerate(pieces):
+        here = pl.ds(start, rows)
+        copies[number, 0] = send(
+            packed.at[core, here], from_core.at[0, here], number, 0, (batch, core)
+        )
+        far = 2 * (1 - high) + 1 - low
+        copies[number, 1] = send(
+            packed.at[far, here], from_core.at[1, here], number, 1, (batch, core)
+        )
+        copies[number, 1].start()
+        copies[number, 0].start()
+    locals_ = []
+    for number, (start, rows) in enumerate(pieces):
+        here = pl.ds(start, rows)
+        first = pltpu.make_async_copy(packed.at[across, here], own.at[1, here], local_sems.at[number, 1])
+        second = pltpu.make_async_copy(packed.at[time, here], own.at[0, here], local_sems.at[number, 0])
+        first.start()
+        second.start()
+        locals_.append((second, first))
+
+    def stage_core(number):
+        start, rows = pieces[number]
+        locals_[number][1].wait()
+        copies[number, 1].wait_recv()
+        add_rows(rows, [(own.at[1], start), (from_core.at[1], start)], (to_x, start))
+        here = pl.ds(start, rows)
+        copies[number, 2] = send(to_x.at[here], from_x.at[here], number, 2, (batch, across))
+        copies[number, 2].start()
+
+    def stage_x(number):
+        start, rows = pieces[number]
+        locals_[number][0].wait()
+        copies[number, 0].wait_recv()
+        copies[number, 2].wait_recv()
+        add_rows(
+            rows, [(own.at[0], start), (from_core.at[0], start), (from_x, start)], (to_y, start)
+        )
+        other = pl.ds(start + (1 - half) * (rows // 2), rows // 2)
+        copies[number, slot_y] = send(
+            to_y.at[other], from_y.at[pl.ds(start // 2, rows // 2)], number, slot_y, (pair, time)
+        )
+        copies[number, slot_y].start()
+
+    def stage_y(number):
+        start, rows = pieces[number]
+        copies[number, slot_y].wait_recv()
+        add_rows(
+            rows // 2,
+            [(to_y, start + half * (rows // 2)), (from_y, start // 2)],
+            (to_z, start // 2),
+        )
+        chunk = rows // batch_size
+        for step in range(1, members):
+            target = lax.rem(place + step, members)
+            copies[number, slot_z + step - 1] = send(
+                to_z.at[pl.ds(start // 2 + target * chunk, chunk)],
+                from_z.at[step - 1, pl.ds(start // batch_size, chunk)],
+                number,
+                slot_z + step - 1,
+                (member(step), time),
+            )
+            copies[number, slot_z + step - 1].start()
+
+    def stage_z(number):
+        start, rows = pieces[number]
+        chunk = rows // batch_size
+        for step in range(1, members):
+            copies[number, slot_z + step - 1].wait_recv()
+        mine = start + half * (rows // 2) + place * chunk
+        sources = [(to_z, start // 2 + place * chunk)]
+        sources += [(from_z.at[step], start // batch_size) for step in range(members - 1)]
+        total = None
+        for ref, at in sources:
+            block = ref[pl.ds(at, chunk), :].astype(jnp.float32)
+            total = block if total is None else total + block
+        final[pl.ds(mine, chunk), :] = total.astype(final.dtype)
+        for step in range(1, members):
+            copies[number, slot_back + step - 1] = send(
+                final.at[pl.ds(mine, chunk)],
+                final.at[pl.ds(mine, chunk)],
+                number,
+                slot_back + step - 1,
+                (member(step), time),
+            )
+            copies[number, slot_back + step - 1].start()
+
+    def stage_back(number):
+        start, rows = pieces[number]
+        for step in range(1, members):
+            copies[number, slot_back + step - 1].wait_recv()
+        mine = pl.ds(start + half * (rows // 2), rows // 2)
+        copies[number, slot_last] = send(
+            final.at[mine], final.at[mine], number, slot_last, (pair, time)
+        )
+        copies[number, slot_last].start()
+
+    def stage_last(number):
+        copies[number, slot_last].wait_recv()
+
+    stages = [stage_core, stage_x, stage_y, stage_z, stage_back, stage_last]
+    for wave in range(len(pieces) + len(stages) - 1):
+        for depth in range(len(stages)):
+            number = wave - depth
+            if 0 <= number < len(pieces):
+                stages[depth](number)
+    for copy in copies.values():
+        copy.wait_send()
+
+
+def reduce_all(packed, pieces, batch_size):
+    rows, width = packed.shape[1:]
+    members = batch_size // 2
+    slots = 5 + 2 * (members - 1)
+    kind = packed.dtype
+    return pl.pallas_call(
+        functools.partial(reduce_kernel, pieces, batch_size),
+        out_shape=jax.ShapeDtypeStruct((rows, width), kind),
+        in_specs=[pl.BlockSpec(memory_space=pl.ANY)],
+        out_specs=pl.BlockSpec(memory_space=pltpu.VMEM),
+        scratch_shapes=[
+            pltpu.VMEM((2, rows, width), kind),
+            pltpu.VMEM((2, rows, width), kind),
+            pltpu.VMEM((rows, width), kind),
+            pltpu.VMEM((rows, width), kind),
+            pltpu.VMEM((rows, width), kind),
+            pltpu.VMEM((rows // 2, width), kind),
+            pltpu.VMEM((rows // 2, width), kind),
+            pltpu.VMEM((members - 1, rows // batch_size, width), kind),
+            pltpu.SemaphoreType.DMA((len(pieces), 2)),
+            pltpu.SemaphoreType.DMA((len(pieces), slots)),
+            pltpu.SemaphoreType.DMA((len(pieces), slots)),
+        ],
+        compiler_params=pltpu.CompilerParams(
+            collective_id=0, has_side_effects=True, vmem_limit_bytes=56 * 2**20
+        ),
+    )(packed)
+
+
+def by_share(array, dim, time_count):
+    extent = array.shape[-1] // time_count
+    flat = array.reshape(-1, time_count, extent)
+    return jnp.swapaxes(flat, 0, 1)
 
 
 def body(
@@ -126,6 +300,7 @@
         current = current + narrow_conv(rounded, narrow_weight[number], narrow_bias[number])
         hiddens.append(current)
     mixed = (snake(current, snake_alpha[6]) * valid).astype(jnp.bfloat16)
+    mixed_all = lax.all_gather(jnp.swapaxes(mixed, 1, 2), ("batch", "tm"), axis=0, tiled=False)
     edged = with_halo(mixed, (("tm", 2),), STRIDE // 2)
     frame_count = length // STRIDE
     blocks = edged.reshape(crop_count, channel_count, frame_count + 1, STRIDE)
@@ -199,9 +374,13 @@
         )
     latent_low = carried.astype(jnp.bfloat16)
     down_bias_grad = jnp.sum(latent_low, axis=(0, 1), dtype=jnp.float32)
-    down_weight_grad = jnp.einsum(
-        "bfc,bifk->cki", latent_low, frame_windows, preferred_element_type=jnp.float32
-    )
+    time_count = lax.axis_size("tm")
+    batch_count = lax.axis_size("batch")
+    crops_all = batch_count * crop_count
+    latent_all = lax.all_gather(latent_low, "tm", axis=1, tiled=True)
+    latent_all = lax.all_gather(latent_all, "batch", axis=0, tiled=True)
+    share = latent_low.shape[2] // time_count
+    latent_mine = lax.dynamic_slice_in_dim(latent_all, lax.axis_index("tm") * share, share, axis=2)
     frame_edges = with_halo(latent_low, (("tm", 1),), 1)
     spread_back = jnp.einsum(
         "cki,bfc->bifk", down_weight, frame_edges, preferred_element_type=jnp.float32
@@ -250,43 +429,95 @@
         )
         upstream = upstream + grad_hidden
     signal_grad = upstream * valid
-    gradients = (
-        jnp.stack(wide_grads),
-        jnp.stack(wide_bias_grads),
-        jnp.stack(narrow_grads),
-        jnp.stack(narrow_bias_grads),
-        jnp.stack(alpha_rows),
-        down_weight_grad,
-        down_bias_grad,
-        jnp.stack(in_weight_grads),
-        jnp.stack(in_bias_grads),
-        jnp.stack(codebook_grads),
-        jnp.stack(out_weight_grads),
-        jnp.stack(out_bias_grads),
-    )
-    time_count = lax.axis_size("tm")
-    packed = pack_grads(gradients, time_count)
-    shares = lax.psum_scatter(
-        packed.astype(jnp.bfloat16), "tm", scatter_dimension=0, tiled=True
+
+    unit_rows = []
+    for number in reversed(range(3)):
+        wide = wide_grads[number].reshape(time_count, -1, 7, channel_count)
+        wide = jnp.swapaxes(wide, 1, 2).reshape(time_count, -1, channel_count)
+        narrow = narrow_grads[number].reshape(time_count, -1, channel_count)
+        unit_rows += [wide.astype(jnp.bfloat16), narrow.astype(jnp.bfloat16)]
+    by_latent = [
+        by_share(jnp.stack(rows), 2, time_count)
+        for rows in (in_weight_grads, codebook_grads, out_weight_grads, out_bias_grads)
+    ]
+    by_latent.append(by_share(down_bias_grad, 0, time_count))
+    by_channel = [
+        by_share(jnp.stack(rows), 1, time_count)
+        for rows in (wide_bias_grads, narrow_bias_grads, alpha_rows)
+    ]
+    by_channel = jnp.concatenate(by_channel, axis=1)
+    in_bias_rows = by_share(jnp.stack(in_bias_grads), 1, time_count).reshape(time_count, 1, -1)
+    wide_of = by_latent[0].shape[2]
+
+    def widened(rows):
+        return jnp.pad(rows, ((0, 0), (0, 0), (0, wide_of - rows.shape[2])))
+
+    small = jnp.concatenate(by_latent + [widened(by_channel), widened(in_bias_rows)], axis=1)
+    fold = channel_count // wide_of
+    quantum = max(16 * batch_count, 2 * BLOCK)
+    small_rows = -(-small.shape[1] // (fold * quantum)) * quantum
+    small = jnp.pad(small, ((0, 0), (0, fold * small_rows - small.shape[1]), (0, 0)))
+    small = jnp.concatenate(
+        [small[:, part * small_rows : (part + 1) * small_rows] for part in range(fold)], axis=2
+    )
+    packed = jnp.concatenate([small.astype(jnp.bfloat16)] + unit_rows, axis=1)
+    unit_extent = (packed.shape[1] - small_rows) // 3
+    piece = max(unit_extent // 2, 16 * batch_count)
+    pieces = [(0, small_rows)]
+    pieces += [(at, piece) for at in range(small_rows, packed.shape[1], piece)]
+    summed = reduce_all(packed, tuple(pieces), batch_count)
+
+    small = summed[:small_rows]
+    small = jnp.concatenate(
+        [small[:, part * wide_of : (part + 1) * wide_of] for part in range(fold)], axis=0
     ).astype(jnp.float32)
-    summed = lax.psum(shares[0], "batch")
-    restored = unpack_grads(summed, gradients, time_count)
+    phases, dims = in_weight.shape[:2]
+    count = phases * dims
+    offset = 3 * count
+    in_weight_out = small[:count].reshape(phases, dims, -1)
+    codebook_out = small[count : 2 * count].reshape(phases, dims, -1)
+    out_weight_out = small[2 * count : offset].reshape(phases, dims, -1)
+    out_bias_out = small[offset : offset + phases]
+    down_bias_out = small[offset + phases]
+    offset = offset + phases + 1
+    narrow_of = channel_count // time_count
+    wide_bias_out = small[offset : offset + 3, :narrow_of]
+    narrow_bias_out = small[offset + 3 : offset + 6, :narrow_of]
+    alpha_out = small[offset + 6 : offset + 13, :narrow_of]
+    in_bias_out = small[offset + 13, : count // time_count].reshape(phases, -1)
+    units = summed[small_rows:].reshape(3, unit_extent, channel_count)[::-1].astype(jnp.float32)
+    wide_out = units[:, : 7 * narrow_of].reshape(3, 7, narrow_of, channel_count)
+    wide_out = jnp.swapaxes(wide_out, 1, 2)
+    narrow_out = units[:, 7 * narrow_of :]
+
+    mixed_all = mixed_all.reshape(batch_count, time_count, crop_count, length, channel_count)
+    mixed_all = jnp.swapaxes(mixed_all, 1, 2).reshape(crops_all, time_count * length, channel_count)
+    half = STRIDE // 2
+    padded_all = jnp.pad(mixed_all, ((0, 0), (half, half), (0, 0)))
+    grouped = padded_all.reshape(crops_all, -1, STRIDE, channel_count)
+    early = jnp.einsum(
+        "bfc,bfki->cki", latent_mine, grouped[:, :-1], preferred_element_type=jnp.float32
+    )
+    late = jnp.einsum(
+        "bfc,bfki->cki", latent_mine, grouped[:, 1:], preferred_element_type=jnp.float32
+    )
+    down_weight_out = jnp.concatenate([early, late], axis=1)
     return (
         quantized_out,
         commit_out,
         signal_grad,
-        restored[0],
-        restored[1],
-        restored[2],
-        restored[3],
-        restored[4],
-        restored[5],
-        restored[6],
-        restored[7],
-        restored[8],
-        restored[9],
-        restored[10],
-        restored[11],
+        wide_out,
+        wide_bias_out,
+        narrow_out,
+        narrow_bias_out,
+        alpha_out,
+        down_weight_out,
+        down_bias_out,
+        in_weight_out,
+        in_bias_out,
+        codebook_out,
+        out_weight_out,
+        out_bias_out,
     )
 
 

time: 1640 us -> 519 us (0.32)
  the two profiles are of different devices: /device:TPU:0 before, /device:TPU:24 now
where the time goes in v1:
time: 519 us; the launch traced here: 510 us
  matrix products  183 us (35%)
  Pallas kernels  120 us (23%)
  local copies, waits for them, and re-layouts  85.3 us (16%)
  other arithmetic  49.7 us (10%)
  starting transfers between devices  42.7 us (8%)
  between operations  17.5 us (3%)
  blocking collectives  7.15 us (1%)
    pallas_call x1, Pallas kernels, reduce_all(): pl.pallas_call(functools.partial(reduce_kernel, pieces, batch_size), out_...  120 us
    ppermute x8, starting transfers between devices, with_halo(): lax.ppermute(lax.slice_in_dim(block, block.shape[dim] - width, None, axis...  31.9 us
    dot_general x1, matrix products, body(): jnp.einsum('cki,bifk->bfc', down_weight, frame_windows, preferred_element...  29 us
    unnamed x366, local copies, waits for them, and re-layouts  26.6 us
    reduce_sum x5, other arithmetic, snake_back(): jnp.sum(upstream * (values * double_sin / factor - square / jnp.square(fa...  18.9 us
    dot_general x3, matrix products, body(): jnp.einsum('oki,bkot->bit', wide_weight[number], grad_windows, preferred_...  17.3 us
    dot_general x1, matrix products, body(): jnp.einsum('cki,bfc->bifk', down_weight, frame_edges, preferred_element_t...  13.4 us
    dot_general x9, matrix products, body(): jnp.einsum('dc,bfc->bfd', out_weight[phase_index], push_grad, precision=l...  13.3 us
  transfers between devices with their start and end apart: 18, of which 2 were waited for; matrix products, arithmetic and copies ran while one was open for 51% of the time, Pallas kernels for 24%

profile of v1, /device:TPU:24, one launch (start us, length us, event | category | flops | bytes accessed | tf_op | source)
XLA Modules:
  0.0 509.6 jit_solution(13710813860485865698)
XLA Ops:
  10.4 1.9 add_convert_fusion.5
  12.4 1.7 collective-permute-start
  29.2 2.0 bitcast_dynamic-update-slice_fusion
  31.5 3.9 fusion.79
  35.5 3.6 add_convert_fusion.3
  39.1 4.3 collective-permute-start.2
  44.0 1.7 collective-permute-start.3
  46.0 2.3 collective-permute-done.3
  49.8 3.6 add_convert_fusion.1
  53.5 4.5 collective-permute-start.4
  60.2 1.6 collective-permute-done.5
  63.3 4.3 multiply_convert_fusion.3
  68.9 5.0 collective-permute-start.6
  76.2 29.0 %fusion.87 = f32[2,16,1024]{2,1,0:T(8,128)S(1)} fusion(bf16[1024,16,512]{2,1,0:T(8,128)(2,1)} %param.27, bf16[2,512,16,8]{1,2,3,0:T(8,128)(2,1)S(1)} %copy.302, bf16[2,512,16,8]{1,2,3,0:T(8,128)(2,1)S(1)} %copy.301, f32[1024]{0:T(1024)} %param.28), kind=kOutput, calls=%fused_computation.87 | convolution fusion | flops 537165824 | bytes 17436672 | tf_op jit(solution)/shard_map/cki,bifk->bfc/dot_general | solution.py:309
  105.5 1.7 subtract_subtract_fusion
  115.8 2.0 multiply_reduce_fusion.22
  126.4 4.9 collective-permute-start.8
  138.9 1.7 reshape.1054
  140.6 1.5 convolution_subtract_fusion.8
  142.1 1.5 fusion.99
  145.1 1.5 fusion.98
  148.2 1.5 fusion.97
  151.1 1.5 fusion.96
  157.1 1.5 fusion.94
  166.1 1.7 reshape.1065
  183.5 1.7 copy_bitcast_fusion.1
  185.2 2.1 fusion.86
  187.3 7.2 %all_gather.12 = bf16[2,64,1024]{2,1,0:T(8,128)(2,1)} all-gather(bf16[2,16,1024]{2,1,0:T(8,128)(2,1)S(1)} %copy-done.41), channel_id=1, replica_groups=mesh['batch'=8,'tm'=4] {'tm'}, dimensions={1}, use_global_device_ids=true | all-gather | bytes 327680 | tf_op jit(solution)/shard_map/all_gather | solution.py:380
  199.4 13.4 %fusion.34 = f32[2,512,18,16]{1,2,3,0:T(8,128)S(1)} fusion(bf16[1024,16,512]{2,1,0:T(8,128)(2,1)} %param.27, bf16[2,1,1024]{2,1,0:T(2,128)(2,1)} %collective-permute-done.9, bf16[2,16,1024]{2,1,0:T(8,128)(2,1)S(1)} %copy-done.42, bf16[2,1,1024]{2,1,0:T(2,128)(2,1)} %collective-permute-done.8), kind=kOutput, calls=%fused_computation.36 | convolution fusion | flops 604200960 | bytes 18030592 | tf_op jit(solution)/shard_map/cki,bfc->bifk/dot_general | solution.py:385
  214.0 1.9 fusion.466
  215.9 2.0 fusion.465
  219.1 2.9 fusion.37
  223.4 3.0 collective-permute-start.11
  226.4 3.8 multiply_reduce_fusion.1
  230.2 2.1 copy.255
  233.4 4.5 convert_reduce_fusion.2
  237.9 1.9 fusion.464
  241.1 2.9 fusion.38
  245.3 4.1 collective-permute-start.13
  249.4 3.8 multiply_reduce_fusion.3
  253.3 3.6 multiply_reduce_fusion.2
  256.9 2.1 copy.260
  260.0 4.0 convert_reduce_fusion.1
  264.0 1.9 fusion.463
  267.2 3.0 fusion.39
  271.4 4.3 collective-permute-start.15
  275.7 4.0 multiply_reduce_fusion.5
  279.8 3.6 multiply_reduce_fusion.4
  283.4 2.1 copy.265
  286.2 8.9 %multiply_reduce_fusion = (bf16[512]{0:T(512)(128)(2,1)S(1)}, bf16[512]{0:T(512)(128)(2,1)S(1)}, f32[2,512,128]{1,2,0:T(8,128)}) fusion(f32[2,512,128]{1,2,0:T(8,128)S(1)} %copy-done.36, f32[2,512,152]{1,2,0:T(8,128)S(1)} %bitcast.975, f32[512]{0:T(512)S(1)} %copy-done.135, f32[512]{0:T(512)S(1)} %copy-done.110, f32[512]{0:T(512)S(1)} %bitcast.1017, ...), kind=kOutput, calls=%fused_computation.206 | convolution fusion | flops 942668800 | bytes 8141824 | tf_op jit(solution)/shard_map/oki,bkot->bit/dot_general | solution.py:424
  296.8 4.3 constant_dynamic-update-slice_fusion.14
  302.0 2.1 constant_dynamic-update-slice_fusion.12
  305.7 2.1 constant_dynamic-update-slice_fusion.10
  308.7 120.4 %shard_map.280 = bf16[3200,512]{1,0:T(8,128)(2,1)} custom-call(bf16[4,3200,512]{2,1,0:T(8,128)(2,1)} %constant_dynamic-update-slice_fusion.9.packed), custom_call_target="tpu_custom_call" | custom-call | tf_op jit(solution)/shard_map/pallas_call | solution.py:243
  429.0 1.9 slice-done
  431.8 3.1 slice.825
  435.8 2.0 copy.271
  441.7 7.8 %copy.268 = bf16[8,2,4,128,512]{4,3,2,1,0:T(8,128)(2,1)} copy(bf16[8,2,4,128,512]{4,3,1,2,0:T(8,128)(2,1)} %bitcast.970) | data formatting | bytes 16777216 | tf_op jit(solution)/shard_map/transpose | solution.py:494
  449.5 10.2 %pad_bitcast_fusion = bf16[16,65,8,512]{3,2,1,0:T(8,128)(2,1)} fusion(bf16[16,512,512]{2,1,0:T(8,128)(2,1)} %bitcast.963), kind=kLoop, calls=%fused_computation.6 | loop fusion | bytes 16908288 | tf_op jit(solution)/shard_map/reshape | solution.py:497
  459.6 11.7 %fusion.484 = (bf16[16,64,8,512]{3,2,1,0:T(8,128)(2,1)}, bf16[16,64,8,512]{3,2,1,0:T(8,128)(2,1)}) fusion(bf16[16,65,8,512]{3,2,1,0:T(8,128)(2,1)} %pad_bitcast_fusion), kind=kLoop, calls=%fused_computation.736 | loop fusion | bytes 33554432 | tf_op jit(solution)/shard_map/slice | solution.py:499
  471.4 9.4 %fusion.31 = f32[256,8,512]{2,0,1:T(8,128)S(1)} fusion(bf16[16,64,8,512]{3,2,1,0:T(8,128)(2,1)} %get-tuple-element.137, bf16[16,64,1024]{2,1,0:T(8,128)(2,1)} %all-gather.4.cloned.1.call-done, s32[]{:T(128)S(6)} %select_n.3), kind=kOutput, calls=%fused_computation.35 | convolution fusion | flops 2147483648 | bytes 13107204 | tf_op jit(solution)/shard_map/bfc,bfki->cki/dot_general | solution.py:501
  480.8 9.2 %fusion.28 = f32[256,8,512]{2,0,1:T(8,128)} fusion(bf16[16,64,8,512]{3,2,1,0:T(8,128)(2,1)S(1)} %copy-done.3, bf16[16,64,1024]{2,1,0:T(8,128)(2,1)} %all-gather.4.cloned.1.call-done, s32[]{:T(128)S(6)} %select_n.3), kind=kOutput, calls=%fused_computation.34 | convolution fusion | flops 2147483648 | bytes 13107204 | tf_op jit(solution)/shard_map/bfc,bfki->cki/dot_general | solution.py:498
  489.9 4.1 pad_maximum_fusion
  494.1 8.3 %copy.272 = f32[256,16,512]{2,1,0:T(8,128)} copy(f32[256,16,512]{2,0,1:T(8,128)S(1)} %pad_maximum_fusion) | data formatting | bytes 16777216
  (602 shorter events, 110.5 us)
Async XLA Ops:
  7.2 16.9 %copy-start.25 = (f32[9,8,1024]{2,1,0:T(8,128)S(1)}, f32[9,8,1024]{2,1,0:T(8,128)}, u32[]{:S(2)}) copy-start(f32[9,8,1024]{2,1,0:T(8,128)} %param.32) | copy-start | bytes 884740
  7.2 434.4 %all-gather.6.cloned.1.call-start = ((), (), s32[]{:S(2)}) async-start(), calls=%async_computation.1 | async-start | bytes 8650752 | tf_op jit(solution)/shard_map/all_gather | solution.py:303
  8.3 16.5 %copy-start.128 = (f32[1,512]{1,0:T(1,128)}, f32[1,512]{1,0:T(1,128)S(1)}, u32[]{:S(2)}) copy-start(f32[1,512]{1,0:T(1,128)S(1)} %get-tuple-element.191) | copy-start | bytes 6148
  8.3 20.9 %copy-start.75 = (f32[1,512]{1,0:T(1,128)}, f32[1,512]{1,0:T(1,128)S(1)}, u32[]{:S(2)}) copy-start(f32[1,512]{1,0:T(1,128)S(1)} %get-tuple-element.196) | copy-start | bytes 6148
  8.3 27.1 %copy-start.93 = (f32[1,512]{1,0:T(1,128)}, f32[1,512]{1,0:T(1,128)S(1)}, u32[]{:S(2)}) copy-start(f32[1,512]{1,0:T(1,128)S(1)} %get-tuple-element.194) | copy-start | bytes 6148
  8.3 27.1 %copy-start.95 = (f32[1,512]{1,0:T(1,128)}, f32[1,512]{1,0:T(1,128)S(1)}, u32[]{:S(2)}) copy-start(f32[1,512]{1,0:T(1,128)S(1)} %get-tuple-element.195) | copy-start | bytes 6148
  8.3 41.4 %copy-start.97 = (f32[1,512]{1,0:T(1,128)}, f32[1,512]{1,0:T(1,128)S(1)}, u32[]{:S(2)}) copy-start(f32[1,512]{1,0:T(1,128)S(1)} %get-tuple-element.192) | copy-start | bytes 6148
  8.3 41.4 %copy-start.99 = (f32[1,512]{1,0:T(1,128)}, f32[1,512]{1,0:T(1,128)S(1)}, u32[]{:S(2)}) copy-start(f32[1,512]{1,0:T(1,128)S(1)} %get-tuple-element.193) | copy-start | bytes 6148
  8.3 54.9 %copy-start.101 = (f32[1,512]{1,0:T(1,128)}, f32[1,512]{1,0:T(1,128)S(1)}, u32[]{:S(2)}) copy-start(f32[1,512]{1,0:T(1,128)S(1)} %get-tuple-element.197) | copy-start | bytes 6148
  8.4 19.4 %copy-start.71 = (s32[2]{0:T(128)S(1)}, s32[2]{0:T(128)}, u32[]{:S(2)}) copy-start(s32[2]{0:T(128)} %param.20) | copy-start | bytes 28
  8.4 19.3 %copy-start.109 = (f32[2,9,16]{2,0,1:T(2,128)S(1)}, f32[2,9,16]{2,0,1:T(2,128)}, u32[]{:S(2)}) copy-start(f32[2,9,16]{2,0,1:T(2,128)} %param.19) | copy-start | bytes 3460
  10.4 52.9 %copy-start.103 = (f32[2,128]{1,0:T(2,128)}, f32[2,128]{1,0:T(2,128)S(1)}, u32[]{:S(2)}) copy-start(f32[2,128]{1,0:T(2,128)S(1)} %compare_convert_fusion.1) | copy-start | bytes 3076
  12.4 16.6 %collective-permute-start = (bf16[2,512,3]{1,2,0:T(4,128)(2,1)S(1)}, bf16[2,512,3]{1,2,0:T(4,128)(2,1)S(1)}, u32[]{:S(2)}, u32[]{:S(2)}) collective-permute-start(bf16[2,512,3]{1,2,0:T(4,128)(2,1)S(1)} %get-tuple-element.161), channel_id=1, source_target_pairs={{0,1},{1,2},{2,3},{4,5},{5,6},{6,7},{8,9},{9,10},{10,11},{12,13},{... | collective-permute-start | bytes 18440 | tf_op jit(solution)/shard_map/ppermute | solution.py:23
  14.1 17.2 %collective-permute-start.1 = (bf16[2,512,3]{1,2,0:T(4,128)(2,1)S(1)}, bf16[2,512,3]{1,2,0:T(4,128)(2,1)S(1)}, u32[]{:S(2)}, u32[]{:S(2)}) collective-permute-start(bf16[2,512,3]{1,2,0:T(4,128)(2,1)S(1)} %get-tuple-element.160), channel_id=1, source_target_pairs={{1,0},{2,1},{3,2},{5,4},{6,5},{7,6},{9,8},{10,9},{11,10},{13,12},{... | collective-permute-start | bytes 18440 | tf_op jit(solution)/shard_map/ppermute | solution.py:26
  16.5 90.8 %copy-start.53 = (f32[2,16,8]{1,2,0:T(8,128)}, f32[2,16,8]{1,2,0:T(8,128)S(1)}, u32[]{:S(2)}) copy-start(f32[2,16,8]{1,2,0:T(8,128)S(1)} %fusion.265) | copy-start | bytes 3076
  21.7 83.7 %copy-start.55 = (f32[2,16,8]{1,2,0:T(8,128)}, f32[2,16,8]{1,2,0:T(8,128)S(1)}, u32[]{:S(2)}) copy-start(f32[2,16,8]{1,2,0:T(8,128)S(1)} %fusion.267) | copy-start | bytes 3076
  21.7 36.3 %copy-start.72 = (s32[16]{0:T(128)}, s32[16]{0:T(128)S(1)}, u32[]{:S(2)}) copy-start(s32[16]{0:T(128)S(1)} %add_multiply_fusion.2) | copy-start | bytes 196
  25.1 80.3 %copy-start.26 = (f32[2,16,1024]{2,1,0:T(8,128)}, f32[2,16,1024]{2,1,0:T(8,128)S(1)}, u32[]{:S(2)}) copy-start(f32[2,16,1024]{2,1,0:T(8,128)S(1)} %convolution_add_fusion.15) | copy-start | bytes 393220
  29.1 19.5 %slice-start.1 = ((s8[11010048]{0:T(1024)(128)(4,1)}), s8[4194304]{0:T(1024)(128)(4,1)S(1)}, s32[]{:S(2)}) async-start(s8[11010048]{0:T(1024)(128)(4,1)} %bitcast.1039), calls=%async_computation.3 | async-start | bytes 8388608
  31.5 17.0 %slice-start.2 = ((s8[11010048]{0:T(1024)(128)(4,1)}), s8[4194304]{0:T(1024)(128)(4,1)S(1)}, s32[]{:S(2)}) async-start(s8[11010048]{0:T(1024)(128)(4,1)} %bitcast.1039), calls=%async_computation.4 | async-start | bytes 8388608
  39.1 6.7 %collective-permute-start.2 = (bf16[2,512,9]{1,2,0:T(8,128)(2,1)S(1)}, bf16[2,512,9]{1,2,0:T(8,128)(2,1)S(1)}, u32[]{:S(2)}, u32[]{:S(2)}) collective-permute-start(bf16[2,512,9]{1,2,0:T(8,128)(2,1)S(1)} %get-tuple-element.159), channel_id=1, source_target_pairs={{0,1},{1,2},{2,3},{4,5},{5,6},{6,7},{8,9},{9,10},{10,11},{12,13},{... | collective-permute-start | bytes 55304 | tf_op jit(solution)/shard_map/ppermute | solution.py:23
  44.0 4.3 collective-permute-start.3
  53.5 6.5 %collective-permute-start.4 = (bf16[2,512,27]{1,2,0:T(8,128)(2,1)S(1)}, bf16[2,512,27]{1,2,0:T(8,128)(2,1)S(1)}, u32[]{:S(2)}, u32[]{:S(2)}) collective-permute-start(bf16[2,512,27]{1,2,0:T(8,128)(2,1)S(1)} %get-tuple-element.157), channel_id=1, source_target_pairs={{0,1},{1,2},{2,3},{4,5},{5,6},{6,7},{8,9},{9,10},{10,11},{12,13},{... | collective-permute-start | bytes 165896 | tf_op jit(solution)/shard_map/ppermute | solution.py:23
  58.6 3.1 collective-permute-start.5
  67.6 7.3 %collective-permute-start.7 = (bf16[2,512,4]{1,2,0:T(4,128)(2,1)S(1)}, bf16[2,512,4]{1,2,0:T(4,128)(2,1)S(1)}, u32[]{:S(2)}, u32[]{:S(2)}) collective-permute-start(bf16[2,512,4]{1,2,0:T(4,128)(2,1)S(1)} %get-tuple-element.155), channel_id=1, source_target_pairs={{1,0},{2,1},{3,2},{5,4},{6,5},{7,6},{9,8},{10,9},{11,10},{13,12},{... | collective-permute-start | bytes 24584 | tf_op jit(solution)/shard_map/ppermute | solution.py:26
  68.9 6.0 %collective-permute-start.6 = (bf16[2,512,4]{1,2,0:T(4,128)(2,1)S(1)}, bf16[2,512,4]{1,2,0:T(4,128)(2,1)S(1)}, u32[]{:S(2)}, u32[]{:S(2)}) collective-permute-start(bf16[2,512,4]{1,2,0:T(4,128)(2,1)S(1)} %get-tuple-element.154), channel_id=1, source_target_pairs={{0,1},{1,2},{2,3},{4,5},{5,6},{6,7},{8,9},{9,10},{10,11},{12,13},{... | collective-permute-start | bytes 24584 | tf_op jit(solution)/shard_map/ppermute | solution.py:23
  74.8 396.5 %all-gather.4.cloned.1.call-start = ((), (), s32[]{:S(2)}) async-start(), calls=%async_computation | async-start | bytes 2359296 | tf_op jit(solution)/shard_map/all_gather | solution.py:381
  76.2 29.3 %copy-start.27 = (f32[2,16,1024]{2,1,0:T(8,128)S(1)}, f32[2,16,1024]{2,1,0:T(8,128)}, u32[]{:S(2)}) copy-start(f32[2,16,1024]{2,1,0:T(8,128)} %convolution_add_fusion.17) | copy-start | bytes 393220
  76.2 29.3 %copy-start.28 = (f32[2,16,1024]{2,1,0:T(8,128)S(1)}, f32[2,16,1024]{2,1,0:T(8,128)}, u32[]{:S(2)}) copy-start(f32[2,16,1024]{2,1,0:T(8,128)} %convolution_add_fusion.19) | copy-start | bytes 393220
  76.2 29.3 %copy-start.105 = (f32[1,1024]{1,0:T(1,128)S(1)}, f32[1,1024]{1,0:T(1,128)}, u32[]{:S(2)}) copy-start(f32[1,1024]{1,0:T(1,128)} %get-tuple-element.183) | copy-start | bytes 12292
  76.2 31.1 %copy-start.14 = (f32[9,8,1024]{2,1,0:T(8,128)S(1)}, f32[9,8,1024]{2,1,0:T(8,128)}, u32[]{:S(2)}) copy-start(f32[9,8,1024]{2,1,0:T(8,128)} %param.29) | copy-start | bytes 884740
  76.2 31.1 %copy-start.77 = (f32[2,16]{1,0:T(2,128)S(1)}, f32[2,16]{1,0:T(2,128)}, u32[]{:S(2)}) copy-start(f32[2,16]{1,0:T(2,128)} %get-tuple-element.198) | copy-start | bytes 388
  76.2 31.1 %copy-start.144 = (f32[8]{0:T(128)S(1)}, f32[8]{0:T(128)}, u32[]{:S(2)}) copy-start(f32[8]{0:T(128)} %get-tuple-element.93) | copy-start | bytes 100
  125.1 74.2 %collective-permute-start.9 = (bf16[2,1,1024]{2,1,0:T(2,128)(2,1)}, bf16[2,1,1024]{2,1,0:T(2,128)(2,1)}, u32[]{:S(2)}, u32[]{:S(2)}) collective-permute-start(bf16[2,1,1024]{2,1,0:T(2,128)(2,1)} %get-tuple-element.181), channel_id=1, source_target_pairs={{1,0},{2,1},{3,2},{5,4},{6,5},{7,6},{9,8},{10,9},{11,10},{13,12},{... | collective-permute-start | bytes 12296 | tf_op jit(solution)/shard_map/ppermute | solution.py:26
  126.4 72.9 %collective-permute-start.8 = (bf16[2,1,1024]{2,1,0:T(2,128)(2,1)}, bf16[2,1,1024]{2,1,0:T(2,128)(2,1)}, u32[]{:S(2)}, u32[]{:S(2)}) collective-permute-start(bf16[2,1,1024]{2,1,0:T(2,128)(2,1)} %get-tuple-element.180), channel_id=1, source_target_pairs={{0,1},{1,2},{2,3},{4,5},{5,6},{6,7},{8,9},{9,10},{10,11},{12,13},{... | collective-permute-start | bytes 12296 | tf_op jit(solution)/shard_map/ppermute | solution.py:23
  140.6 22.4 %copy-start.150 = (s32[2,16]{1,0:T(2,128)S(1)}, s32[2,16]{1,0:T(2,128)}, u32[]{:S(2)}) copy-start(s32[2,16]{1,0:T(2,128)} %copy-done.149) | copy-start | bytes 388
  140.6 23.3 %copy-start.48 = (f32[2,16,8]{1,2,0:T(8,128)S(1)}, f32[2,16,8]{1,2,0:T(8,128)}, u32[]{:S(2)}) copy-start(f32[2,16,8]{1,2,0:T(8,128)} %copy-done.47) | copy-start | bytes 3076
  140.6 23.3 %copy-start.78 = (f32[2,16]{1,0:T(2,128)S(1)}, f32[2,16]{1,0:T(2,128)}, u32[]{:S(2)}) copy-start(f32[2,16]{1,0:T(2,128)} %get-tuple-element.198) | copy-start | bytes 388
  140.6 23.3 %copy-start.88 = (f32[2,16]{1,0:T(2,128)S(1)}, f32[2,16]{1,0:T(2,128)}, u32[]{:S(2)}) copy-start(f32[2,16]{1,0:T(2,128)} %compare_convert_fusion) | copy-start | bytes 388
  140.6 24.7 %copy-start.148 = (s32[2,16]{1,0:T(2,128)S(1)}, s32[2,16]{1,0:T(2,128)}, u32[]{:S(2)}) copy-start(s32[2,16]{1,0:T(2,128)} %copy-done.147) | copy-start | bytes 388
  179.6 15.9 %copy-start.127 = (bf16[1024]{0:T(1024)(128)(2,1)S(1)}, bf16[1024]{0:T(1024)(128)(2,1)}, u32[]{:S(2)}) copy-start(bf16[1024]{0:T(1024)(128)(2,1)} %get-tuple-element.176) | copy-start | bytes 6148
  179.6 15.9 %copy-start.126 = (bf16[1024]{0:T(1024)(128)(2,1)S(1)}, bf16[1024]{0:T(1024)(128)(2,1)}, u32[]{:S(2)}) copy-start(bf16[1024]{0:T(1024)(128)(2,1)} %get-tuple-element.164) | copy-start | bytes 6148
  179.6 15.9 %copy-start.124 = (bf16[1024]{0:T(1024)(128)(2,1)S(1)}, bf16[1024]{0:T(1024)(128)(2,1)}, u32[]{:S(2)}) copy-start(bf16[1024]{0:T(1024)(128)(2,1)} %get-tuple-element.166) | copy-start | bytes 6148
  179.6 16.0 %copy-start.123 = (bf16[1024]{0:T(1024)(128)(2,1)S(1)}, bf16[1024]{0:T(1024)(128)(2,1)}, u32[]{:S(2)}) copy-start(bf16[1024]{0:T(1024)(128)(2,1)} %get-tuple-element.168) | copy-start | bytes 6148
  179.6 16.0 %copy-start.122 = (bf16[1024]{0:T(1024)(128)(2,1)S(1)}, bf16[1024]{0:T(1024)(128)(2,1)}, u32[]{:S(2)}) copy-start(bf16[1024]{0:T(1024)(128)(2,1)} %get-tuple-element.170) | copy-start | bytes 6148
  179.6 16.0 %copy-start.121 = (bf16[1024]{0:T(1024)(128)(2,1)S(1)}, bf16[1024]{0:T(1024)(128)(2,1)}, u32[]{:S(2)}) copy-start(bf16[1024]{0:T(1024)(128)(2,1)} %get-tuple-element.172) | copy-start | bytes 6148
  179.6 16.0 %copy-start.120 = (bf16[1024]{0:T(1024)(128)(2,1)S(1)}, bf16[1024]{0:T(1024)(128)(2,1)}, u32[]{:S(2)}) copy-start(bf16[1024]{0:T(1024)(128)(2,1)} %get-tuple-element.174) | copy-start | bytes 6148
  179.6 16.0 %copy-start.119 = (bf16[1024]{0:T(1024)(128)(2,1)S(1)}, bf16[1024]{0:T(1024)(128)(2,1)}, u32[]{:S(2)}) copy-start(bf16[1024]{0:T(1024)(128)(2,1)} %get-tuple-element.116) | copy-start | bytes 6148
  180.6 16.1 %copy-start.166 = (bf16[8]{0:T(256)(128)(2,1)S(1)}, bf16[8]{0:T(256)(128)(2,1)}, u32[]{:S(2)}) copy-start(bf16[8]{0:T(256)(128)(2,1)} %get-tuple-element.87) | copy-start | bytes 52
  180.6 16.3 %copy-start.163 = (bf16[8]{0:T(256)(128)(2,1)S(1)}, bf16[8]{0:T(256)(128)(2,1)}, u32[]{:S(2)}) copy-start(bf16[8]{0:T(256)(128)(2,1)} %get-tuple-element.85) | copy-start | bytes 52
  180.7 16.5 %copy-start.165 = (bf16[8]{0:T(256)(128)(2,1)S(1)}, bf16[8]{0:T(256)(128)(2,1)}, u32[]{:S(2)}) copy-start(bf16[8]{0:T(256)(128)(2,1)} %get-tuple-element.83) | copy-start | bytes 52
  180.7 16.7 %copy-start.160 = (bf16[8]{0:T(256)(128)(2,1)S(1)}, bf16[8]{0:T(256)(128)(2,1)}, u32[]{:S(2)}) copy-start(bf16[8]{0:T(256)(128)(2,1)} %get-tuple-element.81) | copy-start | bytes 52
  180.7 16.9 %copy-start.161 = (bf16[8]{0:T(256)(128)(2,1)S(1)}, bf16[8]{0:T(256)(128)(2,1)}, u32[]{:S(2)}) copy-start(bf16[8]{0:T(256)(128)(2,1)} %get-tuple-element.79) | copy-start | bytes 52
  180.7 17.1 %copy-start.159 = (bf16[8]{0:T(256)(128)(2,1)S(1)}, bf16[8]{0:T(256)(128)(2,1)}, u32[]{:S(2)}) copy-start(bf16[8]{0:T(256)(128)(2,1)} %get-tuple-element.77) | copy-start | bytes 52
  180.7 17.3 %copy-start.158 = (bf16[8]{0:T(256)(128)(2,1)S(1)}, bf16[8]{0:T(256)(128)(2,1)}, u32[]{:S(2)}) copy-start(bf16[8]{0:T(256)(128)(2,1)} %get-tuple-element.75) | copy-start | bytes 52
  181.6 17.8 %copy-start.42 = (bf16[2,16,1024]{2,1,0:T(8,128)(2,1)S(1)}, bf16[2,16,1024]{2,1,0:T(8,128)(2,1)}, u32[]{:S(2)}) copy-start(bf16[2,16,1024]{2,1,0:T(8,128)(2,1)} %copy-done.40) | copy-start | bytes 196612
  199.3 33.5 %slice-start.4 = ((s8[11010048]{0:T(1024)(128)(4,1)}), s8[2621440]{0:T(1024)(128)(4,1)S(1)}, s32[]{:S(2)}) async-start(s8[11010048]{0:T(1024)(128)(4,1)} %bitcast.1041), calls=%async_computation.6 | async-start | bytes 5242880
  199.4 33.5 %slice-start.5 = ((s8[11010048]{0:T(1024)(128)(4,1)}), s8[4194304]{0:T(1024)(128)(4,1)S(1)}, s32[]{:S(2)}) async-start(s8[11010048]{0:T(1024)(128)(4,1)} %bitcast.1041), calls=%async_computation.7 | async-start | bytes 8388608
  222.1 10.2 %collective-permute-start.10 = (bf16[2,512,27]{1,2,0:T(8,128)(2,1)S(1)}, bf16[2,512,27]{1,2,0:T(8,128)(2,1)S(1)}, u32[]{:S(2)}, u32[]{:S(2)}) collective-permute-start(bf16[2,512,27]{1,2,0:T(8,128)(2,1)S(1)} %get-tuple-element.153), channel_id=1, source_target_pairs={{1,0},{2,1},{3,2},{5,4},{6,5},{7,6},{9,8},{10,9},{11,10},{13,12},{... | collective-permute-start | bytes 165896 | tf_op jit(solution)/shard_map/ppermute | solution.py:26
  223.4 9.2 %collective-permute-start.11 = (bf16[2,512,27]{1,2,0:T(8,128)(2,1)S(1)}, bf16[2,512,27]{1,2,0:T(8,128)(2,1)S(1)}, u32[]{:S(2)}, u32[]{:S(2)}) collective-permute-start(bf16[2,512,27]{1,2,0:T(8,128)(2,1)S(1)} %get-tuple-element.152), channel_id=1, source_target_pairs={{0,1},{1,2},{2,3},{4,5},{5,6},{6,7},{8,9},{9,10},{10,11},{12,13},{... | collective-permute-start | bytes 165896 | tf_op jit(solution)/shard_map/ppermute | solution.py:23
  244.0 15.0 %collective-permute-start.12 = (bf16[2,512,9]{1,2,0:T(8,128)(2,1)S(1)}, bf16[2,512,9]{1,2,0:T(8,128)(2,1)S(1)}, u32[]{:S(2)}, u32[]{:S(2)}) collective-permute-start(bf16[2,512,9]{1,2,0:T(8,128)(2,1)S(1)} %get-tuple-element.151), channel_id=1, source_target_pairs={{1,0},{2,1},{3,2},{5,4},{6,5},{7,6},{9,8},{10,9},{11,10},{13,12},{... | collective-permute-start | bytes 55304 | tf_op jit(solution)/shard_map/ppermute | solution.py:26
  245.3 14.0 %collective-permute-start.13 = (bf16[2,512,9]{1,2,0:T(8,128)(2,1)S(1)}, bf16[2,512,9]{1,2,0:T(8,128)(2,1)S(1)}, u32[]{:S(2)}, u32[]{:S(2)}) collective-permute-start(bf16[2,512,9]{1,2,0:T(8,128)(2,1)S(1)} %get-tuple-element.150), channel_id=1, source_target_pairs={{0,1},{1,2},{2,3},{4,5},{5,6},{6,7},{8,9},{9,10},{10,11},{12,13},{... | collective-permute-start | bytes 55304 | tf_op jit(solution)/shard_map/ppermute | solution.py:23
  270.1 15.4 %collective-permute-start.14 = (bf16[2,512,3]{1,2,0:T(4,128)(2,1)S(1)}, bf16[2,512,3]{1,2,0:T(4,128)(2,1)S(1)}, u32[]{:S(2)}, u32[]{:S(2)}) collective-permute-start(bf16[2,512,3]{1,2,0:T(4,128)(2,1)S(1)} %get-tuple-element.149), channel_id=1, source_target_pairs={{1,0},{2,1},{3,2},{5,4},{6,5},{7,6},{9,8},{10,9},{11,10},{13,12},{... | collective-permute-start | bytes 18440 | tf_op jit(solution)/shard_map/ppermute | solution.py:26
  271.4 14.4 %collective-permute-start.15 = (bf16[2,512,3]{1,2,0:T(4,128)(2,1)S(1)}, bf16[2,512,3]{1,2,0:T(4,128)(2,1)S(1)}, u32[]{:S(2)}, u32[]{:S(2)}) collective-permute-start(bf16[2,512,3]{1,2,0:T(4,128)(2,1)S(1)} %get-tuple-element.148), channel_id=1, source_target_pairs={{0,1},{1,2},{2,3},{4,5},{5,6},{6,7},{8,9},{9,10},{10,11},{12,13},{... | collective-permute-start | bytes 18440 | tf_op jit(solution)/shard_map/ppermute | solution.py:23
  (130 other events, 1002.2 us)
Sparse Core Ops, SparseCore 0:
  75.0 77.5 all-gather.5
  199.4 48.7 all-gather.3

commit v2 on v1

v2 whole, which is shorter than its diff:
```python
import functools

import jax
import jax.numpy as jnp
from jax import lax
from jax.experimental import pallas as pl
from jax.experimental.pallas import tpu as pltpu
from jax.sharding import PartitionSpec as P

STRIDE = 8


DILATIONS = (1, 3, 9)
MESH = pl.DeviceIdType.MESH
BLOCK = 64


TAPS = 7
RIM = 32
ROWS = 32


def dot(left, right, left_dim, right_dim, precision=None):
    return lax.dot_general(
        left,
        right,
        (((left_dim,), (right_dim,)), ((), ())),
        precision=precision,
        preferred_element_type=jnp.float32,
    )


def exact(left, right, left_dim, right_dim):
    return dot(left, right, left_dim, right_dim, lax.Precision.HIGHEST)


def reduced_angle(angle):
    turns = jnp.floor(angle * 0.3183098861837907 + 0.5)
    rest = angle - turns * 3.140625
    rest = rest - turns * 9.67502593994140625e-4
    return rest - turns * 1.509957990978376432e-7


def sine(rest, square):
    series = -1.0 / 5040.0 + square * (1.0 / 362880.0 - square * (1.0 / 39916800.0))
    return rest + rest * square * (-1.0 / 6.0 + square * (1.0 / 120.0 + square * series))


def cosine(square):
    series = 1.0 / 40320.0 + square * (-1.0 / 3628800.0 + square * (1.0 / 479001600.0))
    return 1.0 + square * (-0.5 + square * (1.0 / 24.0 + square * (-1.0 / 720.0 + square * series)))


def snake_of(values, alpha, inverse):
    rest = reduced_angle(alpha * values)
    wave = sine(rest, rest * rest)
    return values + wave * wave * inverse


def snake_slopes(values, alpha, inverse):
    rest = reduced_angle(alpha * values)
    square = rest * rest
    wave = sine(rest, square)
    double = 2.0 * wave * cosine(square)
    return 1.0 + double, (values * double - wave * wave * inverse) * inverse


def split_three(values):
    first = values.astype(jnp.bfloat16)
    rest = values - first.astype(jnp.float32)
    second = rest.astype(jnp.bfloat16)
    third = (rest - second.astype(jnp.float32)).astype(jnp.bfloat16)
    return first, second, third


def folded(values):
    return jnp.sum(values.reshape(values.shape[0] // 8, 8, values.shape[1]), axis=0)


def block_kernel(
    time_count,
    small_rows,
    lengths,
    signal,
    quant_cot,
    commit_cot,
    codes,
    wide_hbm,
    wide_bias,
    narrow_hbm,
    narrow_bias,
    snake_alpha,
    down_hbm,
    down_bias,
    in_weight,
    in_bias,
    codebook,
    out_weight,
    out_bias,
    quantized,
    commit,
    signal_grad,
    packed,
    phases_out,
    latent_low,
    wide,
    narrow,
    down,
    down_raw,
    hidden,
    conv,
    windows,
    rounded,
    pad,
    grad,
    work,
    branch,
    moved,
    mixed_pad,
    frames,
    latent,
    latent_pad,
    spread,
    looked,
    gap_grad,
    correction,
    units,
    small,
    small_low,
    halo_out,
    halo_in,
    latent_in,
    weight_sems,
    out_sems,
    send_sems,
    recv_sems,
):
    f32, bf16 = jnp.float32, jnp.bfloat16
    batch = lax.axis_index("batch")
    time = lax.axis_index("tm")
    left = lax.rem(time + time_count - 1, time_count)
    right = lax.rem(time + 1, time_count)
    crops, channels, length = signal.shape
    latents = down_bias.shape[1]
    per_crop = length // ROWS
    blocks = crops * per_crop
    frame_count = length // STRIDE
    frames_all = crops * frame_count
    phases = codes.shape[1]
    dims = in_weight.shape[0] // phases
    count = phases * dims
    share = channels // time_count
    wide_of = latents // time_count

    barrier = pltpu.get_barrier_semaphore()
    for peer in (left, right):
        pl.semaphore_signal(barrier, inc=1, device_id=(batch, peer), device_id_type=MESH)

    wide_copies = [
        pltpu.make_async_copy(wide_hbm.at[unit], wide.at[unit], weight_sems.at[unit])
        for unit in range(3)
    ]
    narrow_copy = pltpu.make_async_copy(narrow_hbm, narrow, weight_sems.at[3])
    raw_rows = down_raw.shape[1]
    parts = down_hbm.shape[0] // raw_rows

    def raw_copy(part):
        return pltpu.make_async_copy(
            down_hbm.at[pl.ds(part * raw_rows, raw_rows)],
            down_raw.at[part % 2],
            weight_sems.at[4 + part % 2],
        )

    wide_copies[0].start()
    narrow_copy.start()
    raw_copy(0).start()
    raw_copy(1).start()
    wide_copies[1].start()
    wide_copies[2].start()

    def halo_copies(number, source_rows, target):
        made = []
        for side, peer in ((0, left), (1, right)):
            made.append(
                pltpu.make_async_remote_copy(
                    src_ref=source_rows(side),
                    dst_ref=target(1 - side),
                    send_sem=send_sems.at[number, side],
                    recv_sem=recv_sems.at[number, 1 - side],
                    device_id=(batch, peer),
                    device_id_type=MESH,
                )
            )
        return made

    sent = []

    def start_halo(number, width):
        made = halo_copies(
            number,
            lambda side: halo_out.at[number, side, :, pl.ds(RIM - width if side else 0, width)],
            lambda side: halo_in.at[number, side, :, pl.ds(RIM - width if side == 0 else 0, width)],
        )
        for copy in made:
            copy.start()
        sent.extend(made)
        return made

    def fill_rims(made, number, width):
        made[1].wait_recv()
        made[0].wait_recv()
        low = jnp.where(time > 0, 1.0, 0.0)
        high = jnp.where(time < time_count - 1, 1.0, 0.0)
        for crop in range(crops):
            start = RIM - width
            pad[crop, start:RIM, :] = halo_in[number, 0, crop, start:RIM, :].astype(f32) * low
            pad[crop, RIM + length : RIM + length + width, :] = (
                halo_in[number, 1, crop, 0:width, :].astype(f32) * high
            )

    def each_block(step, carry, edges_then=None):
        def edge(index, carry):
            side = lax.rem(index, 2)
            return step(index // 2, side * (per_crop - 1), carry, side)

        def inside(index, carry):
            return step(index // (per_crop - 2), 1 + lax.rem(index, per_crop - 2), carry, None)

        carry = lax.fori_loop(0, 2 * crops, edge, carry)
        made = edges_then() if edges_then is not None else None
        return lax.fori_loop(0, crops * (per_crop - 2), inside, carry), made

    def keep_edge(number, crop, side, rows):
        if side is not None:
            halo_out[number, side, crop] = rows

    def row_of(ref, row):
        return ref[row : row + 1, :]

    def valid_rows(crop, place):
        places = time * length + place * ROWS + lax.broadcasted_iota(jnp.int32, (ROWS, 1), 0)
        return jnp.where(places < lengths[crop], 1.0, 0.0)

    def reorder(part):
        raw_copy(part).wait()
        taps = down.shape[0]
        size = taps * 16
        rows = lax.broadcasted_iota(jnp.int32, (size, size), 0)
        columns = lax.broadcasted_iota(jnp.int32, (size, size), 1)
        swap = jnp.where(columns == lax.rem(rows, 16) * taps + rows // 16, 1.0, 0.0).astype(bf16)

        def step(index, carry):
            source = down_raw[part % 2, pl.ds(pl.multiple_of(index * size, size), size), :]
            swapped = dot(swap, source, 1, 0).astype(bf16)
            at = pl.multiple_of(part * (raw_rows // taps) + index * 16, 16)
            for tap in range(taps):
                down[tap, pl.ds(at, 16), :] = swapped[tap * 16 : (tap + 1) * 16, :]
            return carry

        lax.fori_loop(0, raw_rows // size, step, 0, unroll=4)
        if part + 2 < parts:
            raw_copy(part + 2).start()

    frame_rows = lax.broadcasted_iota(jnp.int32, (frames_all, 1), 0)
    frame_place = time * frame_count + lax.rem(frame_rows, frame_count)
    frame_length = jnp.where(frame_rows < frame_count, lengths[0], lengths[crops - 1])
    frame_valid = jnp.where(STRIDE * frame_place < frame_length, 1.0, 0.0)
    code_lanes = lax.broadcasted_iota(jnp.int32, (frames_all, codebook.shape[1]), 1)

    def onehot(phase):
        return jnp.where(codes[:, phase : phase + 1] == code_lanes, 1.0, 0.0).astype(bf16)

    for phase in range(phases):
        rows = codebook[phase * dims : (phase + 1) * dims, :]
        three = jnp.concatenate([part.astype(f32) for part in split_three(rows)], axis=0)
        found = dot(three.astype(bf16), onehot(phase), 1, 1)
        looked[phase * dims : (phase + 1) * dims, :] = (
            found[:dims] + found[dims : 2 * dims] + found[2 * dims :]
        )
    looked_rows = looked[...].T
    quantized[...] = (
        (exact(looked_rows, out_weight[...], 1, 0) + jnp.sum(out_bias[...], axis=0, keepdims=True))
        * frame_valid
    ).reshape(quantized.shape)
    phase_of_row = lax.broadcasted_iota(jnp.int32, (count, count), 0) // dims
    phase_of_column = lax.broadcasted_iota(jnp.int32, (count, count), 1) // dims
    earlier = jnp.where(phase_of_row < phase_of_column, 1.0, 0.0)
    later = jnp.where(phase_of_row > phase_of_column, 1.0, 0.0)
    crossing = exact(out_weight[...], in_weight[...], 1, 1) * earlier
    bias_terms = exact(out_bias[...], in_weight[...], 1, 1)
    nine_rows = lax.broadcasted_iota(jnp.int32, (phases, count), 0)
    nine_columns = lax.broadcasted_iota(jnp.int32, (phases, count), 1) // dims
    bias_terms = jnp.sum(jnp.where(nine_rows < nine_columns, bias_terms, 0.0), axis=0, keepdims=True)
    correction[...] = exact(looked_rows, crossing, 1, 0) + bias_terms - in_bias[...]

    for crop in range(crops):
        places = time * length + lax.broadcasted_iota(jnp.int32, (length, 1), 0)
        keep = jnp.where(places < lengths[crop], 1.0, 0.0)
        hidden[0, crop * length : (crop + 1) * length, :] = signal[crop].T * keep

    pl.semaphore_wait(barrier, 2)

    def block_rows(crop, place):
        return pl.ds(pl.multiple_of((crop * per_crop + place) * ROWS, ROWS), ROWS)

    def pad_rows(place):
        return pl.ds(pl.multiple_of(RIM + place * ROWS, ROWS), ROWS)

    for unit in range(3):
        dilation = DILATIONS[unit]
        width = 16 if 3 * dilation <= 16 else 32
        alpha = row_of(snake_alpha, 2 * unit)
        inverse = 1.0 / alpha

        def first_snake(crop, place, carry, side):
            low = snake_of(hidden[unit, block_rows(crop, place), :], alpha, inverse).astype(bf16)
            pad[crop, pad_rows(place), :] = low.astype(f32)
            keep_edge(unit, crop, side, low)
            return carry

        _, made = each_block(first_snake, 0, lambda: start_halo(unit, width))
        for part in range(unit * parts // 4, (unit + 1) * parts // 4):
            reorder(part)
        fill_rims(made, unit, width)
        for tap in range(TAPS):
            for crop in range(crops):
                start = RIM + (tap - 3) * dilation
                windows[unit, tap, crop * length : (crop + 1) * length, :] = pad[
                    crop, start : start + length, :
                ].astype(bf16)
        wide_copies[unit].wait()
        total = None
        for tap in range(TAPS):
            term = dot(windows[unit, tap], wide[unit, tap], 1, 1)
            total = term if total is None else total + term
        conv[unit] = total + row_of(wide_bias, unit)
        alpha = row_of(snake_alpha, 2 * unit + 1)
        inverse = 1.0 / alpha

        def second_snake(index, carry):
            at = pl.ds(pl.multiple_of(index * ROWS, ROWS), ROWS)
            rounded[unit, at, :] = snake_of(conv[unit, at, :], alpha, inverse).astype(bf16)
            return carry

        lax.fori_loop(0, blocks, second_snake, 0)
        if unit == 0:
            narrow_copy.wait()
        hidden[unit + 1] = (
            hidden[unit] + dot(rounded[unit], narrow[unit], 1, 1) + row_of(narrow_bias, unit)
        )

    lane_tiles = channels // 128
    stretch = length + 16
    alpha = row_of(snake_alpha, 6)
    inverse = 1.0 / alpha

    def last_snake(crop, place, carry, side):
        values = snake_of(hidden[3, block_rows(crop, place), :], alpha, inverse)
        low = (values * valid_rows(crop, place)).astype(bf16)
        keep_edge(3, crop, side, low)
        wider = low.astype(f32)
        for tile in range(lane_tiles):
            at = pl.multiple_of((tile * crops + crop) * stretch + 8 + place * ROWS, 8)
            mixed_pad[pl.ds(at, ROWS), :] = wider[:, tile * 128 : (tile + 1) * 128]
        return carry

    _, made = each_block(last_snake, 0, lambda: start_halo(3, 16))
    for part in range(3 * parts // 4, parts):
        reorder(part)
    made[1].wait_recv()
    made[0].wait_recv()
    low = jnp.where(time > 0, 1.0, 0.0)
    high = jnp.where(time < time_count - 1, 1.0, 0.0)
    for crop in range(crops):
        before = halo_in[3, 0, crop, RIM - 16 : RIM, :].astype(f32)[8:] * low
        after = halo_in[3, 1, crop, 0:16, :].astype(f32)[:8] * high
        for tile in range(lane_tiles):
            base = (tile * crops + crop) * stretch
            lanes = slice(tile * 128, (tile + 1) * 128)
            mixed_pad[base : base + 8, :] = before[:, lanes]
            mixed_pad[base + 8 + length : base + 16 + length, :] = after[:, lanes]
    taps = frames.shape[0]
    for tap in range(taps):
        for crop in range(crops):
            for tile in range(lane_tiles):
                base = (tile * crops + crop) * stretch + tap + 4
                frames[
                    tap,
                    crop * frame_count : (crop + 1) * frame_count,
                    tile * 128 : (tile + 1) * 128,
                ] = mixed_pad[pl.ds(base, frame_count, stride=STRIDE), :].astype(bf16)
    phases_out[...] = frames[taps // 2 - STRIDE // 2 : taps // 2 + STRIDE // 2]
    total = None
    for tap in range(taps):
        term = dot(frames[tap], down[tap], 1, 1)
        total = term if total is None else total + term
    latent[...] = total + down_bias[...]

    gap = exact(latent[...], in_weight[...], 1, 1) - correction[...] - looked_rows
    grouping = jnp.where(
        lax.broadcasted_iota(jnp.int32, (count, phases), 0) // dims
        == lax.broadcasted_iota(jnp.int32, (count, phases), 1),
        1.0,
        0.0,
    )
    commit[...] = exact(gap * gap, grouping, 1, 0) * frame_valid
    gap_back = 2.0 * (exact(commit_cot[...] * frame_valid, grouping, 1, 1) * gap)
    gap_grad[...] = gap_back
    lowered = exact(gap_back, in_weight[...], 1, 0).astype(bf16)
    latent_low[...] = lowered.reshape(latent_low.shape)

    made = halo_copies(4, lambda side: latent_low, lambda side: latent_in.at[side])
    for copy in made:
        copy.start()
    sent.extend(made)

    push = quant_cot[...].reshape(frames_all, latents) * frame_valid
    gap_back = gap_grad[...]
    looked_rows = looked[...].T
    between = exact(looked_rows, gap_back, 0, 0)
    small[...] = jnp.zeros_like(small)

    def keep_small(row, rows):
        for index in range(time_count):
            columns = rows[:, index * wide_of : (index + 1) * wide_of]
            done = 0
            while done < rows.shape[0]:
                fold, at = divmod(row + done, 128)
                size = min(rows.shape[0] - done, 128 - at)
                small[index, at : at + size, fold * wide_of : (fold + 1) * wide_of] = columns[
                    done : done + size
                ]
                done += size

    def keep_channels(row, rows):
        fold, at = divmod(row, 128)
        for index in range(time_count):
            small[index, at : at + rows.shape[0], fold * wide_of : fold * wide_of + share] = rows[
                :, index * share : (index + 1) * share
            ]

    earlier_rows = jnp.where(
        lax.broadcasted_iota(jnp.int32, (count, phases), 0) // dims
        > lax.broadcasted_iota(jnp.int32, (count, phases), 1),
        1.0,
        0.0,
    )
    ones = jnp.ones((frames_all, phases), f32)
    keep_small(
        0,
        exact(gap_back, latent[...], 0, 0)
        - exact(exact(gap_back, looked_rows, 0, 0) * later, out_weight[...], 1, 0)
        - exact(exact(gap_back, ones, 0, 0) * earlier_rows, out_bias[...], 1, 0),
    )
    looked_back = exact(push, out_weight[...], 1, 1) - gap_back
    crossing = exact(out_weight[...], in_weight[...], 1, 1) * earlier
    looked_back = (looked_back - exact(gap_back, crossing, 1, 1)).T
    for phase in range(phases):
        rows = looked_back[phase * dims : (phase + 1) * dims, :]
        three = jnp.concatenate([part.astype(f32) for part in split_three(rows)], axis=0)
        found = dot(three.astype(bf16), onehot(phase), 1, 0)
        keep_small(
            count + phase * dims, found[:dims] + found[dims : 2 * dims] + found[2 * dims :]
        )
    keep_small(
        2 * count,
        exact(looked_rows, push, 0, 0) - exact(between * earlier, in_weight[...], 1, 0),
    )
    gap_sum = jnp.sum(gap_back, axis=0, keepdims=True)
    keep_small(
        3 * count,
        jnp.sum(push, axis=0, keepdims=True)
        - exact(jnp.where(nine_rows < nine_columns, gap_sum, 0.0), in_weight[...], 1, 0),
    )
    lowered = latent_low[...].reshape(frames_all, latents).astype(f32)
    row = 3 * count + phases
    keep_small(row, jnp.sum(lowered, axis=0, keepdims=True))
    wide_bias_row, narrow_bias_row, alpha_row, in_bias_row = row + 1, row + 4, row + 7, row + 14
    fold, at = divmod(in_bias_row, 128)
    for index in range(time_count):
        small[index, at : at + 1, fold * wide_of : fold * wide_of + count] = gap_sum

    made[1].wait_recv()
    made[0].wait_recv()
    latent_pad[...] = jnp.zeros_like(latent_pad)
    for crop in range(crops):
        own = lowered[crop * frame_count : (crop + 1) * frame_count, :]
        latent_pad[crop, 8 : 8 + frame_count, :] = own
        before = latent_in[0, crop].astype(f32)[frame_count - 1 :, :] * low
        after = latent_in[1, crop].astype(f32)[:1, :] * high
        latent_pad[crop, 7:8, :] = before
        latent_pad[crop, 8 + frame_count : 9 + frame_count, :] = after
    reach = frame_count + 8
    same = jnp.concatenate([latent_pad[crop, 8 : 8 + reach, :] for crop in range(crops)], axis=0)
    previous = jnp.concatenate([latent_pad[crop, 7 : 7 + reach, :] for crop in range(crops)], axis=0)
    same, previous = same.astype(bf16), previous.astype(bf16)
    run = reach * STRIDE
    for step in range(STRIDE):
        both = dot(same, down[step], 1, 0) + dot(previous, down[step + STRIDE], 1, 0)
        for crop in range(crops):
            for tile in range(lane_tiles):
                base = (tile * crops + crop) * run + step
                spread[pl.ds(base, reach, stride=STRIDE), :] = both[
                    crop * reach : (crop + 1) * reach, tile * 128 : (tile + 1) * 128
                ]

    alpha = row_of(snake_alpha, 6)
    inverse = 1.0 / alpha
    zero = jnp.zeros((8, channels), f32)

    def mixed_back(crop, place, carry, side):
        pieces = []
        for tile in range(lane_tiles):
            at = (tile * crops + crop) * run + STRIDE // 2 + place * ROWS
            pieces.append(spread[pl.ds(at, ROWS), :])
        upstream = jnp.concatenate(pieces, axis=1) * valid_rows(crop, place)
        at = block_rows(crop, place)
        slope, alpha_slope = snake_slopes(hidden[3, at, :], alpha, inverse)
        following = upstream * slope
        grad[at, :] = following
        branch[at, :] = following.astype(bf16)
        return (
            carry[0] + folded(upstream * alpha_slope),
            carry[1] + folded(following.astype(bf16).astype(f32)),
        )

    (alpha_sum, bias_sum), _ = each_block(mixed_back, (zero, zero))
    keep_channels(alpha_row + 6, jnp.sum(alpha_sum, axis=0, keepdims=True))

    unit_rows = units.shape[2]
    out_copies = []
    for unit in (2, 1, 0):
        dilation = DILATIONS[unit]
        width = 16 if 3 * dilation <= 16 else 32
        slot = unit % 2
        number = 5 + unit
        keep_channels(narrow_bias_row + unit, jnp.sum(bias_sum, axis=0, keepdims=True))
        work[...] = dot(branch[...], narrow[unit], 1, 0)
        alpha = row_of(snake_alpha, 2 * unit + 1)
        inverse = 1.0 / alpha

        def conv_back(crop, place, carry, side):
            at = block_rows(crop, place)
            upstream = work[at, :]
            slope, alpha_slope = snake_slopes(conv[unit, at, :], alpha, inverse)
            lowered = (upstream * slope).astype(bf16)
            moved[at, :] = lowered
            wider = lowered.astype(f32)
            pad[crop, pad_rows(place), :] = wider
            keep_edge(number, crop, side, lowered)
            return carry[0] + folded(upstream * alpha_slope), carry[1] + folded(wider)

        (alpha_sum, bias_sum), made = each_block(
            conv_back, (zero, zero), lambda: start_halo(number, width)
        )
        keep_channels(alpha_row + 2 * unit + 1, jnp.sum(alpha_sum, axis=0, keepdims=True))
        keep_channels(wide_bias_row + unit, jnp.sum(bias_sum, axis=0, keepdims=True))
        if unit == 0:
            out_copies[0].wait()

        def keep_unit(row, rows):
            rows = rows.astype(bf16)
            for index in range(time_count):
                units[slot, index, row : row + share, :] = rows[index * share : (index + 1) * share]

        for tap in range(TAPS):
            keep_unit(tap * share, dot(moved[...], windows[unit, tap], 0, 0))
        keep_unit(TAPS * share, dot(branch[...], rounded[unit], 0, 0))
        copy = pltpu.make_async_copy(
            units.at[slot],
            packed.at[:, pl.ds(small_rows + (2 - unit) * unit_rows, unit_rows)],
            out_sems.at[unit],
        )
        copy.start()
        out_copies.append(copy)
        fill_rims(made, number, width)
        total = None
        for tap in range(TAPS):
            start = RIM - (tap - 3) * dilation
            shifted = jnp.concatenate(
                [pad[crop, start : start + length, :].astype(bf16) for crop in range(crops)], axis=0
            )
            term = dot(shifted, wide[unit, tap], 1, 0)
            total = term if total is None else total + term
        work[...] = total
        alpha = row_of(snake_alpha, 2 * unit)
        inverse = 1.0 / alpha

        def hidden_back(crop, place, carry, side):
            at = block_rows(crop, place)
            upstream = work[at, :]
            slope, alpha_slope = snake_slopes(hidden[unit, at, :], alpha, inverse)
            following = grad[at, :] + upstream * slope
            if unit == 0:
                following = following * valid_rows(crop, place)
            grad[at, :] = following
            lowered = following.astype(bf16)
            branch[at, :] = lowered
            return (
                carry[0] + folded(upstream * alpha_slope),
                carry[1] + folded(lowered.astype(f32)),
            )

        (alpha_sum, bias_sum), _ = each_block(hidden_back, (zero, zero))
        keep_channels(alpha_row + 2 * unit, jnp.sum(alpha_sum, axis=0, keepdims=True))

    small_low[...] = small[...].astype(bf16)
    for start in range(0, small_rows, 128):
        copy = pltpu.make_async_copy(
            small_low, packed.at[:, pl.ds(start, 128)], out_sems.at[3 + start // 128]
        )
        copy.start()
        out_copies.append(copy)
    for crop in range(crops):
        signal_grad[crop] = grad[crop * length : (crop + 1) * length, :].T
    for copy in out_copies[1:]:
        copy.wait()
    for copy in sent:
        copy.wait_send()


def run_block(time_count, small_rows, lengths, *arrays):
    (signal, quant_cot, commit_cot, codes, wide, _, narrow, _, _, down, down_bias) = arrays[:11]
    f32, bf16 = jnp.float32, jnp.bfloat16
    crops, channels, length = signal.shape
    latents = down_bias.shape[1]
    taps = down.shape[0] // latents
    frames = crops * (length // STRIDE)
    rows = crops * length
    phases = codes.shape[1]
    count = arrays[11].shape[0]
    unit_rows = (TAPS + 1) * (channels // time_count)
    vmem = pl.BlockSpec(memory_space=pltpu.VMEM)
    hbm = pl.BlockSpec(memory_space=pl.ANY)
    in_specs = [pl.BlockSpec(memory_space=pltpu.SMEM)] + [vmem] * len(arrays)
    for place in (4, 6, 9):
        in_specs[1 + place] = hbm
    lane_tiles = channels // 128
    dma = pltpu.SemaphoreType.DMA
    return pl.pallas_call(
        functools.partial(block_kernel, time_count, small_rows),
        out_shape=(
            jax.ShapeDtypeStruct(quant_cot.shape, f32),
            jax.ShapeDtypeStruct((frames, phases), f32),
            jax.ShapeDtypeStruct(signal.shape, f32),
            jax.ShapeDtypeStruct((time_count, small_rows + 3 * unit_rows, channels), bf16),
            jax.ShapeDtypeStruct((STRIDE, frames, channels), bf16),
            jax.ShapeDtypeStruct(quant_cot.shape, bf16),
        ),
        in_specs=in_specs,
        out_specs=(vmem, vmem, vmem, hbm, vmem, vmem),
        scratch_shapes=[
            pltpu.VMEM(wide.shape, bf16),
            pltpu.VMEM(narrow.shape, bf16),
            pltpu.VMEM((taps, latents, channels), bf16),
            pltpu.VMEM((2, down.shape[0] // 16, channels), bf16),
            pltpu.VMEM((4, rows, channels), f32),
            pltpu.VMEM((3, rows, channels), f32),
            pltpu.VMEM((3, TAPS, rows, channels), bf16),
            pltpu.VMEM((3, rows, channels), bf16),
            pltpu.VMEM((crops, length + 2 * RIM, channels), f32),
            pltpu.VMEM((rows, channels), f32),
            pltpu.VMEM((rows, channels), f32),
            pltpu.VMEM((rows, channels), bf16),
            pltpu.VMEM((rows, channels), bf16),
            pltpu.VMEM((lane_tiles * crops * (length + 16), 128), f32),
            pltpu.VMEM((taps, frames, channels), bf16),
            pltpu.VMEM((frames, latents), f32),
            pltpu.VMEM((crops, 16 + length // STRIDE, latents), f32),
            pltpu.VMEM((lane_tiles * crops * (length + 8 * STRIDE), 128), f32),
            pltpu.VMEM((count, frames), f32),
            pltpu.VMEM((frames, count), f32),
            pltpu.VMEM((frames, count), f32),
            pltpu.VMEM((2, time_count, unit_rows, channels), bf16),
            pltpu.VMEM((time_count, 128, channels), f32),
            pltpu.VMEM((time_count, 128, channels), bf16),
            pltpu.VMEM((8, 2, crops, RIM, channels), bf16),
            pltpu.VMEM((8, 2, crops, RIM, channels), bf16),
            pltpu.VMEM((2,) + quant_cot.shape, bf16),
            dma((6,)),
            dma((3 + small_rows // 128,)),
            dma((8, 2)),
            dma((8, 2)),
        ],
        compiler_params=pltpu.CompilerParams(
            collective_id=1, has_side_effects=True, vmem_limit_bytes=60 * 2**20
        ),
    )(lengths, *arrays)


def add_rows(rows, sources, target):
    def step(index, carry):
        at = index * BLOCK
        total = None
        for ref, start in sources:
            block = ref[pl.ds(start + at, BLOCK), :].astype(jnp.float32)
            total = block if total is None else total + block
        ref, start = target
        ref[pl.ds(start + at, BLOCK), :] = total.astype(ref.dtype)
        return carry

    lax.fori_loop(0, rows // BLOCK, step, 0)


def reduce_kernel(pieces, batch_size, packed, final, own, from_core, to_x, from_x, to_y, from_y, to_z, from_z, local_sems, send_sems, recv_sems):
    members = batch_size // 2
    batch = lax.axis_index("batch")
    time = lax.axis_index("tm")
    low, high = lax.rem(time, 2), time // 2
    core = 2 * high + 1 - low
    across = 2 * (1 - high) + low
    half = lax.rem(batch, 2)
    place = batch // 2
    pair = 2 * place + 1 - half

    def member(step):
        return 2 * lax.rem(place + step, members) + half

    barrier = pltpu.get_barrier_semaphore()
    peers = [(batch, core), (batch, across), (pair, time)]
    peers += [(member(step), time) for step in range(1, members)]
    for peer in peers:
        pl.semaphore_signal(barrier, inc=1, device_id=peer, device_id_type=MESH)
    pl.semaphore_wait(barrier, len(peers))

    def send(source, target, number, slot, device):
        return pltpu.make_async_remote_copy(
            src_ref=source,
            dst_ref=target,
            send_sem=send_sems.at[number, slot],
            recv_sem=recv_sems.at[number, slot],
            device_id=device,
            device_id_type=MESH,
        )

    spread = members - 1
    slot_y, slot_z, slot_back, slot_last = 3, 4, 4 + spread, 4 + 2 * spread
    copies = {}
    for number, (start, rows) in enumerate(pieces):
        here = pl.ds(start, rows)
        copies[number, 0] = send(
            packed.at[core, here], from_core.at[0, here], number, 0, (batch, core)
        )
        far = 2 * (1 - high) + 1 - low
        copies[number, 1] = send(
            packed.at[far, here], from_core.at[1, here], number, 1, (batch, core)
        )
        copies[number, 1].start()
        copies[number, 0].start()
    locals_ = []
    for number, (start, rows) in enumerate(pieces):
        here = pl.ds(start, rows)
        first = pltpu.make_async_copy(packed.at[across, here], own.at[1, here], local_sems.at[number, 1])
        second = pltpu.make_async_copy(packed.at[time, here], own.at[0, here], local_sems.at[number, 0])
        first.start()
        second.start()
        locals_.append((second, first))

    def stage_core(number):
        start, rows = pieces[number]
        locals_[number][1].wait()
        copies[number, 1].wait_recv()
        add_rows(rows, [(own.at[1], start), (from_core.at[1], start)], (to_x, start))
        here = pl.ds(start, rows)
        copies[number, 2] = send(to_x.at[here], from_x.at[here], number, 2, (batch, across))
        copies[number, 2].start()

    def stage_x(number):
        start, rows = pieces[number]
        locals_[number][0].wait()
        copies[number, 0].wait_recv()
        copies[number, 2].wait_recv()
        add_rows(
            rows, [(own.at[0], start), (from_core.at[0], start), (from_x, start)], (to_y, start)
        )
        other = pl.ds(start + (1 - half) * (rows // 2), rows // 2)
        copies[number, slot_y] = send(
            to_y.at[other], from_y.at[pl.ds(start // 2, rows // 2)], number, slot_y, (pair, time)
        )
        copies[number, slot_y].start()

    def stage_y(number):
        start, rows = pieces[number]
        copies[number, slot_y].wait_recv()
        add_rows(
            rows // 2,
            [(to_y, start + half * (rows // 2)), (from_y, start // 2)],
            (to_z, start // 2),
        )
        chunk = rows // batch_size
        for step in range(1, members):
            target = lax.rem(place + step, members)
            copies[number, slot_z + step - 1] = send(
                to_z.at[pl.ds(start // 2 + target * chunk, chunk)],
                from_z.at[step - 1, pl.ds(start // batch_size, chunk)],
                number,
                slot_z + step - 1,
                (member(step), time),
            )
            copies[number, slot_z + step - 1].start()

    def stage_z(number):
        start, rows = pieces[number]
        chunk = rows // batch_size
        for step in range(1, members):
            copies[number, slot_z + step - 1].wait_recv()
        mine = start + half * (rows // 2) + place * chunk
        sources = [(to_z, start // 2 + place * chunk)]
        sources += [(from_z.at[step], start // batch_size) for step in range(members - 1)]
        total = None
        for ref, at in sources:
            block = ref[pl.ds(at, chunk), :].astype(jnp.float32)
            total = block if total is None else total + block
        final[pl.ds(mine, chunk), :] = total.astype(final.dtype)
        for step in range(1, members):
            copies[number, slot_back + step - 1] = send(
                final.at[pl.ds(mine, chunk)],
                final.at[pl.ds(mine, chunk)],
                number,
                slot_back + step - 1,
                (member(step), time),
            )
            copies[number, slot_back + step - 1].start()

    def stage_back(number):
        start, rows = pieces[number]
        for step in range(1, members):
            copies[number, slot_back + step - 1].wait_recv()
        mine = pl.ds(start + half * (rows // 2), rows // 2)
        copies[number, slot_last] = send(
            final.at[mine], final.at[mine], number, slot_last, (pair, time)
        )
        copies[number, slot_last].start()

    def stage_last(number):
        copies[number, slot_last].wait_recv()

    stages = [stage_core, stage_x, stage_y, stage_z, stage_back, stage_last]
    for wave in range(len(pieces) + len(stages) - 1):
        for depth in range(len(stages)):
            number = wave - depth
            if 0 <= number < len(pieces):
                stages[depth](number)
    for copy in copies.values():
        copy.wait_send()


def reduce_all(packed, pieces, batch_size):
    rows, width = packed.shape[1:]
    members = batch_size // 2
    slots = 5 + 2 * (members - 1)
    kind = packed.dtype
    return pl.pallas_call(
        functools.partial(reduce_kernel, pieces, batch_size),
        out_shape=jax.ShapeDtypeStruct((rows, width), kind),
        in_specs=[pl.BlockSpec(memory_space=pl.ANY)],
        out_specs=pl.BlockSpec(memory_space=pltpu.VMEM),
        scratch_shapes=[
            pltpu.VMEM((2, rows, width), kind),
            pltpu.VMEM((2, rows, width), kind),
            pltpu.VMEM((rows, width), kind),
            pltpu.VMEM((rows, width), kind),
            pltpu.VMEM((rows, width), kind),
            pltpu.VMEM((rows // 2, width), kind),
            pltpu.VMEM((rows // 2, width), kind),
            pltpu.VMEM((members - 1, rows // batch_size, width), kind),
            pltpu.SemaphoreType.DMA((len(pieces), 2)),
            pltpu.SemaphoreType.DMA((len(pieces), slots)),
            pltpu.SemaphoreType.DMA((len(pieces), slots)),
        ],
        compiler_params=pltpu.CompilerParams(
            collective_id=0, has_side_effects=True, vmem_limit_bytes=56 * 2**20
        ),
    )(packed)


def down_kernel(lows, phases, out, held, columns, in_sems, out_sems):
    count = lows.shape[2]
    group, lanes = held.shape[1], held.shape[4]
    rows = group * held.shape[3]
    tiles = lanes // 128
    groups = phases.shape[0] // group
    items = [(part, at) for part in range(phases.shape[3] // lanes) for at in range(groups)]
    loads = [
        pltpu.make_async_copy(
            phases.at[pl.ds(at * group, group), :, :, pl.ds(part * lanes, lanes)],
            held.at[index % 2],
            in_sems.at[index % 2],
        )
        for index, (part, at) in enumerate(items)
    ]
    for load in loads[:2]:
        load.start()
    stores = []
    after = before = None
    for index, (part, at) in enumerate(items):
        if after is None or groups > 1:
            turned = [lows[kind, at * rows : (at + 1) * rows].T for kind in range(3)]
            after = jnp.concatenate([turned[0], turned[1]], axis=0)
            before = jnp.concatenate([turned[0], turned[2]], axis=0)
        loads[index].wait()
        for step in range(STRIDE):
            block = held[index % 2, :, step].reshape(rows, lanes)
            late = step >= STRIDE // 2
            both = dot(after if late else before, block, 1, 0)
            middle = step + STRIDE // 2
            for tap, row in ((middle, 0), (middle - STRIDE if late else middle + STRIDE, count)):
                for tile in range(tiles):
                    place = pl.ds(tap, count, stride=2 * STRIDE)
                    value = both[row : row + count, tile * 128 : (tile + 1) * 128]
                    if at > 0:
                        value = value + columns[part * tiles + tile, place, :]
                    columns[part * tiles + tile, place, :] = value
        if index + 2 < len(items):
            loads[index + 2].start()
        if at == groups - 1:
            for tile in range(part * tiles, (part + 1) * tiles):
                stores.append(
                    pltpu.make_async_copy(
                        columns.at[tile], out.at[:, pl.ds(tile * 128, 128)], out_sems.at[tile]
                    )
                )
                stores[-1].start()
    for store in stores:
        store.wait()


def down_gradient(lows, phases):
    devices, _, rows, channels = phases.shape
    count = lows.shape[2]
    lanes = 256
    hbm = pl.BlockSpec(memory_space=pl.ANY)
    return pl.pallas_call(
        down_kernel,
        out_shape=jax.ShapeDtypeStruct((count * 2 * STRIDE, channels), jnp.float32),
        in_specs=[pl.BlockSpec(memory_space=pltpu.VMEM), hbm],
        out_specs=hbm,
        scratch_shapes=[
            pltpu.VMEM((2, min(devices, 32), STRIDE, rows, lanes), phases.dtype),
            pltpu.VMEM((channels // 128, count * 2 * STRIDE, 128), jnp.float32),
            pltpu.SemaphoreType.DMA((2,)),
            pltpu.SemaphoreType.DMA((channels // 128,)),
        ],
        compiler_params=pltpu.CompilerParams(vmem_limit_bytes=60 * 2**20),
    )(lows, phases)


def body(
    signal,
    quant_cot,
    commit_cot,
    lengths,
    codes,
    wide_weight,
    wide_bias,
    narrow_weight,
    narrow_bias,
    snake_alpha,
    down_weight,
    down_bias,
    in_weight,
    in_bias,
    codebook,
    out_weight,
    out_bias,
):
    time_count = lax.axis_size("tm")
    batch_count = lax.axis_size("batch")
    crop_count, channel_count, length = signal.shape
    latent_count, tap_count, _ = down_weight.shape
    phases, dims = in_weight.shape[:2]
    count = phases * dims
    frame_count = length // STRIDE
    small_rows = 16 * batch_count
    quantized, commit, signal_grad, packed, own_phases, latent_low = run_block(
        time_count,
        small_rows,
        lengths,
        signal,
        quant_cot,
        jnp.swapaxes(commit_cot, 1, 2).reshape(-1, phases),
        jnp.swapaxes(codes, 1, 2).reshape(-1, phases),
        jnp.swapaxes(wide_weight, 1, 2),
        wide_bias,
        narrow_weight,
        narrow_bias,
        snake_alpha,
        down_weight.reshape(-1, channel_count),
        down_bias.reshape(1, -1),
        in_weight.reshape(count, -1),
        in_bias.reshape(1, -1),
        codebook.reshape(count, -1),
        out_weight.reshape(count, -1),
        out_bias,
    )
    commit = jnp.swapaxes(commit.reshape(crop_count, frame_count, phases), 1, 2)

    all_phases = lax.all_gather(own_phases, ("batch", "tm"))
    all_low = lax.all_gather(latent_low, ("batch", "tm"))
    share = latent_count // time_count
    mine = lax.dynamic_slice_in_dim(all_low, lax.axis_index("tm") * share, share, axis=3)
    mine = mine.reshape(batch_count, time_count, crop_count, frame_count, share)
    line = jnp.swapaxes(mine, 1, 2).reshape(-1, time_count * frame_count, share)
    after = jnp.pad(line[:, 1:], ((0, 0), (0, 1), (0, 0)))
    before = jnp.pad(line[:, :-1], ((0, 0), (1, 0), (0, 0)))
    lows = jnp.stack([line, after, before])
    lows = lows.reshape(3, batch_count, crop_count, time_count, frame_count, share)
    lows = jnp.swapaxes(lows, 2, 3).reshape(3, -1, share)

    unit_extent = (packed.shape[1] - small_rows) // 3
    piece = max(unit_extent // 2, 16 * batch_count)
    pieces = [(0, small_rows)]
    pieces += [(at, piece) for at in range(small_rows, packed.shape[1], piece)]
    summed = reduce_all(packed, tuple(pieces), batch_count)

    wide_of = latent_count // time_count
    small = summed[:128].astype(jnp.float32)
    small = jnp.concatenate([small[:, :wide_of], small[:, wide_of : 2 * wide_of]], axis=0)
    in_weight_out = small[:count].reshape(phases, dims, -1)
    codebook_out = small[count : 2 * count].reshape(phases, dims, -1)
    out_weight_out = small[2 * count : 3 * count].reshape(phases, dims, -1)
    row = 3 * count + phases
    out_bias_out = small[3 * count : row]
    down_bias_out = small[row]
    narrow_of = channel_count // time_count
    wide_bias_out = small[row + 1 : row + 4, :narrow_of]
    narrow_bias_out = small[row + 4 : row + 7, :narrow_of]
    alpha_out = small[row + 7 : row + 14, :narrow_of]
    in_bias_all = small[row + 14, :count].reshape(phases, dims)
    part = dims // time_count
    in_bias_out = lax.dynamic_slice_in_dim(in_bias_all, lax.axis_index("tm") * part, part, axis=1)
    units = summed[small_rows:].reshape(3, unit_extent, channel_count)[::-1].astype(jnp.float32)
    wide_out = units[:, : TAPS * narrow_of].reshape(3, TAPS, narrow_of, channel_count)
    wide_out = jnp.swapaxes(wide_out, 1, 2)
    narrow_out = units[:, TAPS * narrow_of :]
    down_out = down_gradient(lows, all_phases).reshape(share, tap_count, channel_count)
    return (
        quantized,
        commit,
        signal_grad,
        wide_out,
        wide_bias_out,
        narrow_out,
        narrow_bias_out,
        alpha_out,
        down_out,
        down_bias_out,
        in_weight_out,
        in_bias_out,
        codebook_out,
        out_weight_out,
        out_bias_out,
    )


def solution(mesh):
    return jax.shard_map(
        body,
        mesh=mesh,
        in_specs=(
            P("batch", None, "tm"),
            P("batch", "tm", None),
            P("batch", None, "tm"),
            P("batch"),
            P("batch", None, "tm"),
            P(),
            P(),
            P(),
            P(),
            P(),
            P(),
            P(),
            P(),
            P(),
            P(),
            P(),
            P(),
        ),
        out_specs=(
            P("batch", "tm", None),
            P("batch", None, "tm"),
            P("batch", None, "tm"),
            P(None, "tm", None, None),
            P(None, "tm"),
            P(None, "tm", None),
            P(None, "tm"),
            P(None, "tm"),
            P("tm", None, None),
            P("tm"),
            P(None, None, "tm"),
            P(None, "tm"),
            P(None, None, "tm"),
            P(None, None, "tm"),
            P(None, "tm"),
        ),
        check_vma=False,
    )
```

time: 519 us -> 261 us (0.50)
  the two profiles are of different devices: /device:TPU:24 before, /device:TPU:0 now
where the time goes in v2:
time: 261 us; the launch traced here: 257 us
  Pallas kernels  222 us (85%)
  local copies, waits for them, and re-layouts  17 us (7%)
  between operations  14.2 us (5%)
  other arithmetic  2.93 us (1%)
    pallas_call x1, Pallas kernels, reduce_all(): pl.pallas_call(functools.partial(reduce_kernel, pieces, batch_size), out_...  151 us
    pallas_call x1, Pallas kernels, run_block(): pl.pallas_call(functools.partial(block_kernel, time_count, small_rows), o...  59.1 us
    pallas_call x1, Pallas kernels, down_gradient(): pl.pallas_call(down_kernel, out_shape=jax.ShapeDtypeStruct((count * 2 * S...  12.2 us
  transfers between devices with their start and end apart: 2, of which 0 were waited for; matrix products, arithmetic and copies ran while one was open for 5% of the time, Pallas kernels for 59%

profile of v2, /device:TPU:0, one launch (start us, length us, event | category | flops | bytes accessed | tf_op | source)
XLA Modules:
  0.0 257.0 jit_solution(12013955673820412526)
XLA Ops:
  7.2 0.0 all-gather.5.cloned.1.call-start
  7.2 1.4 copy.51
  8.6 1.4 copy.52
  10.0 0.8 copy.53
  10.8 0.6 reshape.96.in_bias
  11.4 59.1 %shard_map.280 = (f32[2,16,1024]{2,1,0:T(8,128)}, f32[32,9]{1,0:T(8,128)}, f32[2,512,128]{2,1,0:T(8,128)}, bf16[4,3200,512]{2,1,0:T(8,128)(2,1)}, bf16[8,32,512]...) custom-call(s32[2]{0:T(128)} %lengths.1, f32[2,512,128]{2,1,0:T(8,128)} %signal.1, f32[2,16,1024]{2,1,0:T(8,128)} %quant_cot.1, ...), custom_call_target="tpu_custom_call" | custom-call | tf_op jit(solution)/shard_map/pallas_call | solution.py:640
  70.5 0.0 all-gather.5.cloned.1.call-update
  70.5 0.0 all-gather.7.cloned.1.call-start
  70.5 0.7 all-gather.7.cloned.1.call-update
  71.2 150.8 %shard_map.281 = bf16[3200,512]{1,0:T(8,128)(2,1)} custom-call(bf16[4,3200,512]{2,1,0:T(8,128)(2,1)} %get-tuple-element.24.packed), custom_call_target="tpu_custom_call" | custom-call | tf_op jit(solution)/shard_map/pallas_call | solution.py:853
  222.1 0.0 slice-start
  222.1 1.9 slice-done
  224.0 0.9 reverse_convert_fusion
  224.8 0.0 copy-start
  224.9 0.0 copy-start.3
  224.9 3.1 %slice.76 = f32[3,896,512]{2,1,0:T(8,128)} slice(f32[3,1024,512]{2,1,0:T(8,128)S(1)} %reverse_convert_fusion), slice={[0:3], [0:896], [0:512]} | slice | bytes 11010048 | tf_op jit(solution)/shard_map/slice | solution.py:1033
  227.9 0.9 slice.78
  228.9 0.0 copy-done
  228.9 0.6 slice.80
  229.5 0.6 slice.83
  230.1 0.6 slice.89
  230.7 0.0 copy-done.3
  230.7 0.7 copy.54
  231.4 0.1 reshape_squeeze.3
  231.4 0.1 constant_dynamic-slice_fusion
  231.5 0.7 copy.58
  232.2 0.6 fusion.3
  232.8 0.7 slice_bitcast_fusion
  233.5 0.0 all-gather.5.cloned.1.call-done
  233.5 1.1 constant_dynamic-slice_fusion.1
  234.6 0.2 fusion.1
  234.9 0.1 pad.8
  234.9 0.2 pad.9
  235.1 1.3 pad_maximum_fusion
  236.5 0.0 all-gather.7.cloned.1.call-done
  236.5 0.0 copy-start.2
  236.5 0.0 copy-start.1
  236.5 12.2 %shard_map.282 = f32[4096,512]{1,0:T(8,128)} custom-call(bf16[3,1024,256]{2,1,0:T(8,128)(2,1)} %bitcast.42, bf16[32,8,32,512]{3,2,1,0:T(8,128)(2,1)} %bitcast.40), custom_call_target="tpu_custom_call" | custom-call | tf_op jit(solution)/shard_map/pallas_call | solution.py:933
  248.7 0.0 copy-done.2
  248.7 0.7 copy.65
  249.3 0.0 copy-done.1
  249.3 0.8 copy.66
  (4 shorter events, 0.1 us)
Async XLA Ops:
  7.2 226.3 %all-gather.5.cloned.1.call-start = ((), (), s32[]{:S(2)}) async-start(), calls=%async_computation | async-start | bytes 2162688 | tf_op jit(solution)/shard_map/all_gather | solution.py:999
  70.5 166.0 %all-gather.7.cloned.1.call-start = ((), (), s32[]{:S(2)}) async-start(), calls=%async_computation.1 | async-start | bytes 8650752 | tf_op jit(solution)/shard_map/all_gather | solution.py:998
  222.1 1.9 slice-start
  224.8 4.0 %copy-start = (bf16[3200,512]{1,0:T(8,128)(2,1)S(1)}, bf16[3200,512]{1,0:T(8,128)(2,1)}, u32[]{:S(2)}) copy-start(bf16[3200,512]{1,0:T(8,128)(2,1)} %shard_map.281) | copy-start | bytes 9830404
  224.9 5.8 %copy-start.3 = (f32[32,9]{1,0:T(8,128)S(1)}, f32[32,9]{1,0:T(8,128)}, u32[]{:S(2)}) copy-start(f32[32,9]{1,0:T(8,128)} %get-tuple-element.22) | copy-start | bytes 3460
  236.5 12.2 %copy-start.2 = (f32[2,16,1024]{2,1,0:T(8,128)S(1)}, f32[2,16,1024]{2,1,0:T(8,128)}, u32[]{:S(2)}) copy-start(f32[2,16,1024]{2,1,0:T(8,128)} %get-tuple-element.111) | copy-start | bytes 393220
  236.5 12.9 %copy-start.1 = (f32[2,512,128]{2,1,0:T(8,128)S(1)}, f32[2,512,128]{2,1,0:T(8,128)}, u32[]{:S(2)}) copy-start(f32[2,512,128]{2,1,0:T(8,128)} %get-tuple-element.113) | copy-start | bytes 1572868
Sparse Core Ops, SparseCore 0:
  70.6 64.0 all-gather.4
  137.6 98.5 all-gather.6

commit v3 on v2

v3 whole, which is shorter than its diff:
```python
import functools

import jax
import jax.numpy as jnp
from jax import lax
from jax.experimental import pallas as pl
from jax.experimental.pallas import tpu as pltpu
from jax.sharding import PartitionSpec as P

STRIDE = 8


DILATIONS = (1, 3, 9)
MESH = pl.DeviceIdType.MESH
BLOCK = 64


TAPS = 7
RIM = 32
ROWS = 32


def dot(left, right, left_dim, right_dim, precision=None):
    return lax.dot_general(
        left,
        right,
        (((left_dim,), (right_dim,)), ((), ())),
        precision=precision,
        preferred_element_type=jnp.float32,
    )


def exact(left, right, left_dim, right_dim):
    return dot(left, right, left_dim, right_dim, lax.Precision.HIGHEST)


def reduced_angle(angle):
    turns = jnp.floor(angle * 0.3183098861837907 + 0.5)
    rest = angle - turns * 3.140625
    rest = rest - turns * 9.67502593994140625e-4
    return rest - turns * 1.509957990978376432e-7


def sine(rest, square):
    series = -1.0 / 5040.0 + square * (1.0 / 362880.0 - square * (1.0 / 39916800.0))
    return rest + rest * square * (-1.0 / 6.0 + square * (1.0 / 120.0 + square * series))


def cosine(square):
    series = 1.0 / 40320.0 + square * (-1.0 / 3628800.0 + square * (1.0 / 479001600.0))
    return 1.0 + square * (-0.5 + square * (1.0 / 24.0 + square * (-1.0 / 720.0 + square * series)))


def snake_of(values, alpha, inverse):
    rest = reduced_angle(alpha * values)
    wave = sine(rest, rest * rest)
    return values + wave * wave * inverse


def snake_slopes(values, alpha, inverse):
    rest = reduced_angle(alpha * values)
    square = rest * rest
    wave = sine(rest, square)
    double = 2.0 * wave * cosine(square)
    return 1.0 + double, (values * double - wave * wave * inverse) * inverse


def split_three(values):
    first = values.astype(jnp.bfloat16)
    rest = values - first.astype(jnp.float32)
    second = rest.astype(jnp.bfloat16)
    third = (rest - second.astype(jnp.float32)).astype(jnp.bfloat16)
    return first, second, third


def folded(values):
    return jnp.sum(values.reshape(values.shape[0] // 8, 8, values.shape[1]), axis=0)


def block_kernel(
    time_count,
    batch_count,
    pieces,
    lengths,
    signal,
    quant_cot,
    coded,
    wide_hbm,
    wide_bias,
    narrow_hbm,
    narrow_bias,
    snake_alpha,
    down_hbm,
    down_bias,
    in_weight,
    in_bias,
    codebook,
    out_weight,
    out_bias,
    quantized,
    commit,
    signal_grad,
    final,
    all_phases,
    all_lows,
    wide,
    narrow,
    down,
    hidden,
    conv,
    gathered,
    pad,
    grad,
    work,
    branch,
    shares,
    share_all,
    share_pad,
    mixed_pad,
    frames,
    latent,
    latent_pad,
    spread,
    looked,
    gap_grad,
    correction,
    small,
    small_low,
    small_in,
    alpha_out,
    alpha_in,
    low_shares,
    low_all,
    halo_out,
    halo_in,
    latent_low,
    latent_in,
    signal_in,
    quant_in,
    coded_in,
    commit_out,
    signal_out,
    signal_back,
    swap_local,
    swap_send,
    swap_recv,
    from_pair,
    from_members,
    weight_sems,
    local_sems,
    send_sems,
    recv_sems,
    gather_send,
    gather_recv,
    relay_send,
    relay_recv,
    share_send,
    share_recv,
    small_send,
    small_recv,
    low_send,
    low_recv,
    block_send,
    block_recv,
    piece_send,
    piece_recv,
):
    f32, bf16 = jnp.float32, jnp.bfloat16
    sent = []
    batch = lax.axis_index("batch")
    time = lax.axis_index("tm")
    crops, channels, length = signal.shape
    latents = down_bias.shape[1]
    mine = time // crops
    side = lax.rem(time, crops)
    rows_all = crops * length
    blocks = rows_all // ROWS
    frame_count = length // STRIDE
    frames_all = crops * frame_count
    phases = out_bias.shape[0]
    dims = in_weight.shape[0] // phases
    count = phases * dims
    share = channels // time_count
    wide_of = latents // time_count

    core = crops * mine + 1 - side
    across = lax.rem(time + crops, time_count)
    members = batch_count // 2
    half = lax.rem(batch, 2)
    place_z = batch // 2
    pair = 2 * place_z + 1 - half

    def member(step):
        return 2 * lax.rem(place_z + step, members) + half

    def sibling(step):
        return lax.rem(time + step, time_count)

    peers = [(batch, sibling(step)) for step in range(1, time_count)]
    peers += [(pair, time)] + [(member(step), time) for step in range(1, members)]
    barrier = pltpu.get_barrier_semaphore()
    for peer in peers:
        pl.semaphore_signal(barrier, inc=1, device_id=peer, device_id_type=MESH)

    def remote(source, target, send_sem, recv_sem, device):
        copy = pltpu.make_async_remote_copy(
            src_ref=source,
            dst_ref=target,
            send_sem=send_sem,
            recv_sem=recv_sem,
            device_id=device,
            device_id_type=MESH,
        )
        copy.start()
        sent.append(copy)
        return copy

    wide_copies = [
        pltpu.make_async_copy(wide_hbm.at[unit], wide.at[unit], weight_sems.at[unit])
        for unit in range(3)
    ]
    narrow_copy = pltpu.make_async_copy(narrow_hbm, narrow, weight_sems.at[3])
    taps = frames.shape[0]
    group = 16 * taps
    quarter = down.shape[0] // 4
    down_copies = [
        pltpu.make_async_copy(
            down_hbm.at[pl.ds(part * quarter, quarter)],
            down.at[pl.ds(part * quarter, quarter)],
            weight_sems.at[4 + part],
        )
        for part in range(4)
    ]
    first, last = jnp.where(side == 0, 1.0, 0.0), jnp.where(side == 1, 1.0, 0.0)

    def swap(number, source, target, slot, back):
        made = []
        for part in range(crops):
            peer = crops * side + part if back else crops * part + mine
            origin = crops * part + mine if back else crops * side + part
            away = pltpu.make_async_remote_copy(
                src_ref=source(part),
                dst_ref=target(slot),
                send_sem=swap_send.at[number, part],
                recv_sem=swap_recv.at[number, slot],
                device_id=(batch, peer),
                device_id_type=MESH,
            )
            here = pltpu.make_async_copy(source(part), target(slot), swap_local.at[number])
            arrived = pltpu.make_async_remote_copy(
                src_ref=source(part),
                dst_ref=target(part),
                send_sem=swap_send.at[number, part],
                recv_sem=swap_recv.at[number, part],
                device_id=(batch, peer),
                device_id_type=MESH,
            )

            @pl.when(peer != time)
            def _():
                away.start()

            @pl.when(peer == time)
            def _():
                here.start()

            made.append((peer, origin, away, here, arrived))
        swaps.append(made)
        return made

    def swapped_in(made):
        for peer, origin, away, here, arrived in made:

            @pl.when(origin != time)
            def _():
                arrived.wait_recv()

            @pl.when(origin == time)
            def _():
                here.wait()

    swaps = []

    halo_rows = (16, 16, 32, 16, 0, 16, 16, 32)
    halo_start = [sum(halo_rows[:number]) for number in range(len(halo_rows))]

    def start_halo(number):
        rows = pl.ds(halo_start[number], halo_rows[number])
        return remote(
            halo_out.at[rows],
            halo_in.at[rows],
            send_sems.at[number],
            recv_sems.at[number],
            (batch, core),
        )

    def fill_rims(made, number):
        width, begin = halo_rows[number], halo_start[number]
        made.wait_recv()
        rim = halo_in[begin : begin + width, :].astype(f32)
        pad[RIM - width : RIM, :] = rim * last
        pad[RIM + rows_all : RIM + rows_all + width, :] = rim * first

    def each_block(step, carry, edge_then=None):
        carry = step((1 - side) * (blocks - 1), carry, True)
        made = edge_then() if edge_then is not None else None

        def inside(index, carry):
            return step(index + side, carry, False)

        return lax.fori_loop(0, blocks - 1, inside, carry), made

    def keep_edge(number, edge, rows):
        if edge:
            width, begin = halo_rows[number], halo_start[number]
            ahead, behind = rows[ROWS - width :].astype(f32), rows[:width].astype(f32)
            halo_out[begin : begin + width, :] = (ahead * first + behind * last).astype(bf16)

    def row_of(ref, row):
        return ref[row : row + 1, :]

    def valid_rows(place):
        places = side * rows_all + place * ROWS + lax.broadcasted_iota(jnp.int32, (ROWS, 1), 0)
        return jnp.where(places < lengths[mine], 1.0, 0.0)

    def reorder(part):
        rows = lax.broadcasted_iota(jnp.int32, (group, group), 0)
        columns = lax.broadcasted_iota(jnp.int32, (group, group), 1)
        turn = jnp.where(columns == lax.rem(rows, 16) * taps + rows // 16, 1.0, 0.0).astype(bf16)
        down_copies[part].wait()

        def step(index, carry):
            places = [
                pl.ds(pl.multiple_of(part * quarter + (4 * index + which) * group, group), group)
                for which in range(4)
            ]
            turned = [dot(turn, down[at, :], 1, 0).astype(bf16) for at in places]
            for at, rows in zip(places, turned):
                down[at, :] = rows
            return carry

        lax.fori_loop(0, quarter // group // 4, step, 0)

    def down_tap(tap):
        tiles = down.reshape(latents // 16, taps, 16, channels)
        return tiles[:, tap].reshape(latents, channels)

    pl.semaphore_wait(barrier, len(peers))
    swap_signal = swap(0, lambda part: signal.at[part], lambda slot: signal_in.at[slot], side, False)
    swap_quant = swap(1, lambda part: quant_cot.at[part], lambda slot: quant_in.at[slot], side, False)
    swap_coded = swap(2, lambda part: coded.at[part], lambda slot: coded_in.at[slot], side, False)
    wide_copies[0].start()
    narrow_copy.start()
    for copy in down_copies:
        copy.start()
    wide_copies[1].start()
    wide_copies[2].start()

    code_lanes = lax.broadcasted_iota(jnp.int32, (frames_all, codebook.shape[1]), 1).astype(f32)
    frame_rows = lax.broadcasted_iota(jnp.int32, (frames_all, 1), 0)

    def onehot(codes, phase):
        return jnp.where(codes[:, phase : phase + 1] == code_lanes, 1.0, 0.0).astype(bf16)

    def look_up(codes):
        found = []
        for phase in range(phases):
            rows = codebook[phase * dims : (phase + 1) * dims, :]
            three = jnp.concatenate([part.astype(f32) for part in split_three(rows)], axis=0)
            all_three = dot(three.astype(bf16), onehot(codes, phase), 1, 1)
            found.append(all_three[:dims] + all_three[dims : 2 * dims] + all_three[2 * dims :])
        return jnp.concatenate(found, axis=0).T

    looked_rows = look_up(coded[...].reshape(frames_all, -1))
    frame_place = time * frame_count + lax.rem(frame_rows, frame_count)
    frame_length = jnp.where(frame_rows < frame_count, lengths[0], lengths[crops - 1])
    frame_valid = jnp.where(STRIDE * frame_place < frame_length, 1.0, 0.0)
    quantized[...] = (
        (exact(looked_rows, out_weight[...], 1, 0) + jnp.sum(out_bias[...], axis=0, keepdims=True))
        * frame_valid
    ).reshape(quantized.shape)
    swapped_in(swap_coded)
    codes = coded_in[...].reshape(frames_all, -1)
    looked[...] = look_up(codes)
    looked_rows = looked[...]
    frame_place = side * frames_all + frame_rows
    frame_valid = jnp.where(STRIDE * frame_place < lengths[mine], 1.0, 0.0)
    phase_of_row = lax.broadcasted_iota(jnp.int32, (count, count), 0) // dims
    phase_of_column = lax.broadcasted_iota(jnp.int32, (count, count), 1) // dims
    earlier = jnp.where(phase_of_row < phase_of_column, 1.0, 0.0)
    later = jnp.where(phase_of_row > phase_of_column, 1.0, 0.0)
    crossing = exact(out_weight[...], in_weight[...], 1, 1) * earlier
    bias_terms = exact(out_bias[...], in_weight[...], 1, 1)
    nine_rows = lax.broadcasted_iota(jnp.int32, (phases, count), 0)
    nine_columns = lax.broadcasted_iota(jnp.int32, (phases, count), 1) // dims
    bias_terms = jnp.sum(jnp.where(nine_rows < nine_columns, bias_terms, 0.0), axis=0, keepdims=True)
    correction[...] = exact(looked_rows, crossing, 1, 0) + bias_terms - in_bias[...]

    for part in range(4):
        reorder(part)

    swapped_in(swap_signal)
    for part in range(crops):
        places = side * rows_all + part * length + lax.broadcasted_iota(jnp.int32, (length, 1), 0)
        keep = jnp.where(places < lengths[mine], 1.0, 0.0)
        hidden[0, part * length : (part + 1) * length, :] = signal_in[part].T * keep

    def block_rows(place):
        return pl.ds(pl.multiple_of(place * ROWS, ROWS), ROWS)

    def own_rows(place):
        return pl.ds(pl.multiple_of(side * rows_all + place * ROWS, ROWS), ROWS)

    own = pl.ds(pl.multiple_of(side * rows_all, rows_all), rows_all)

    def pad_rows(place):
        return pl.ds(pl.multiple_of(RIM + place * ROWS, ROWS), ROWS)

    def shifted(offset):
        start = RIM + offset
        return pad[start : start + rows_all, :].astype(bf16)

    gather_across, gather_core = {}, {}

    def gather(unit):
        slot = gathered.at[unit, :, mine, own]
        gather_across[unit] = remote(
            slot, slot, gather_send.at[unit, 0], gather_recv.at[unit, 0], (batch, across)
        )
        gather_core[unit] = remote(
            slot, slot, gather_send.at[unit, 1], gather_recv.at[unit, 1], (batch, core)
        )

    for unit in range(3):
        dilation = DILATIONS[unit]
        alpha = row_of(snake_alpha, 2 * unit)
        inverse = 1.0 / alpha

        def first_snake(place, carry, edge):
            low = snake_of(hidden[unit, block_rows(place), :], alpha, inverse).astype(bf16)
            gathered[unit, 0, mine, own_rows(place), :] = low
            pad[pad_rows(place), :] = low.astype(f32)
            keep_edge(unit, edge, low)
            return carry

        _, made = each_block(first_snake, 0, lambda: start_halo(unit))
        fill_rims(made, unit)
        wide_copies[unit].wait()
        result = None
        for tap in range(TAPS):
            term = dot(shifted((tap - 3) * dilation), wide[unit, tap], 1, 1)
            result = term if result is None else result + term
        conv[unit] = result + row_of(wide_bias, unit)
        alpha = row_of(snake_alpha, 2 * unit + 1)
        inverse = 1.0 / alpha

        def second_snake(place, carry, edge):
            values = snake_of(conv[unit, block_rows(place), :], alpha, inverse)
            gathered[unit, 1, mine, own_rows(place), :] = values.astype(bf16)
            return carry

        each_block(second_snake, 0)
        if unit == 0:
            narrow_copy.wait()
        if unit != 1:
            gather(unit)
        rounded = gathered[unit, 1, mine, own, :]
        hidden[unit + 1] = (
            hidden[unit] + dot(rounded, narrow[unit], 1, 1) + row_of(narrow_bias, unit)
        )

    lane_tiles = channels // 128
    stretch = rows_all + 16
    alpha = row_of(snake_alpha, 6)
    inverse = 1.0 / alpha

    def last_snake(place, carry, edge):
        values = snake_of(hidden[3, block_rows(place), :], alpha, inverse)
        low = (values * valid_rows(place)).astype(bf16)
        keep_edge(3, edge, low)
        wider = low.astype(f32)
        for tile in range(lane_tiles):
            at = pl.multiple_of(tile * stretch + 8 + place * ROWS, 8)
            mixed_pad[pl.ds(at, ROWS), :] = wider[:, tile * 128 : (tile + 1) * 128]
        return carry

    _, made = each_block(last_snake, 0, lambda: start_halo(3))
    made.wait_recv()
    begin = halo_start[3]
    rim = halo_in[begin : begin + 16, :].astype(f32)
    before, after = rim[8:] * last, rim[:8] * first
    for tile in range(lane_tiles):
        base = tile * stretch
        lanes = slice(tile * 128, (tile + 1) * 128)
        mixed_pad[base : base + 8, :] = before[:, lanes]
        mixed_pad[base + 8 + rows_all : base + 16 + rows_all, :] = after[:, lanes]
    for tap in range(taps):
        for tile in range(lane_tiles):
            base = tile * stretch + tap + 4
            frames[tap, :, tile * 128 : (tile + 1) * 128] = mixed_pad[
                pl.ds(base, frames_all, stride=STRIDE), :
            ].astype(bf16)
    local_copies = []

    def local(source, target, number):
        copy = pltpu.make_async_copy(source, target, local_sems.at[number])
        copy.start()
        local_copies.append(copy)

    own_phases = frames.at[pl.ds(taps // 2 - STRIDE // 2, STRIDE)]
    local(own_phases, all_phases.at[batch, time], 0)
    pair_blocks = {
        0: remote(
            own_phases,
            all_phases.at[batch, time],
            block_send.at[members],
            block_recv.at[members],
            (pair, time),
        )
    }
    near_first = sorted(range(1, members), key=lambda step: min(step, members - step))
    z_blocks = {
        step: remote(
            own_phases,
            all_phases.at[batch, time],
            block_send.at[step],
            block_recv.at[step],
            (member(step), time),
        )
        for step in near_first
    }

    result = None
    for tap in range(taps):
        term = dot(frames[tap], down_tap(tap), 1, 1)
        result = term if result is None else result + term
    latent[...] = result + down_bias[...]

    gap = exact(latent[...], in_weight[...], 1, 1) - correction[...] - looked_rows
    grouping = jnp.where(
        lax.broadcasted_iota(jnp.int32, (count, phases), 0) // dims
        == lax.broadcasted_iota(jnp.int32, (count, phases), 1),
        1.0,
        0.0,
    )
    squares = exact(gap * gap, grouping, 1, 0) * frame_valid
    commit_out[...] = jnp.concatenate(
        [squares, jnp.zeros((frames_all, 128 - phases), f32)], axis=1
    ).reshape(commit_out.shape)
    swap_commit = swap(3, lambda part: commit_out.at[part], lambda slot: commit.at[slot], mine, True)
    commit_cot = codes[:, phases : 2 * phases]
    gap_back = 2.0 * (exact(commit_cot * frame_valid, grouping, 1, 1) * gap)
    gap_grad[...] = gap_back
    lowered = exact(gap_back, in_weight[...], 1, 0).astype(bf16)
    latent_low[...] = lowered
    for index in range(time_count):
        low_shares[index] = lowered[:, index * wide_of : (index + 1) * wide_of]

    edge_frames = pl.ds(pl.multiple_of((1 - side) * (frames_all - 16), 16), 16)
    made = remote(
        latent_low.at[edge_frames], latent_in, send_sems.at[4], recv_sems.at[4], (batch, core)
    )

    low_all[time] = low_shares[time]
    lows_in = [
        remote(
            low_shares.at[sibling(step)],
            low_all.at[time],
            low_send.at[step - 1],
            low_recv.at[step - 1],
            (batch, sibling(step)),
        )
        for step in range(1, time_count)
    ]

    across_blocks, low_blocks, core_blocks = [], [], []

    def block_of(step, half):
        return 2 * lax.rem(place_z - step + members, members) + half

    def forward_pair(step):
        z_blocks[step].wait_recv()
        slot = all_phases.at[block_of(step, half), time]
        sems = members + step
        pair_blocks[step] = remote(
            slot, slot, block_send.at[sems], block_recv.at[sems], (pair, time)
        )

    def forward_across(step):
        pair_blocks[step].wait_recv()
        for order, which in enumerate((half, 1 - half)):
            slot = all_phases.at[block_of(step, which), time]
            sems = 2 * members + 2 * step + order
            if step == 0 and order == 0:
                local_copies.pop(0).wait()
            across_blocks.append(
                remote(slot, slot, block_send.at[sems], block_recv.at[sems], (batch, across))
            )

    def forward_core(which):
        sems = 4 * members + which
        if which == 0:
            slot = all_phases.at[:, time]
        else:
            for copy in across_blocks:
                copy.wait_recv()
            slot = all_phases.at[:, across]
        core_blocks.append(
            remote(slot, slot, block_send.at[sems], block_recv.at[sems], (batch, core))
        )

    lowered = latent_low[...].astype(f32)

    def keep_alpha(row, rows):
        for index in range(time_count):
            alpha_out[index, row : row + 1, :] = rows[:, index * share : (index + 1) * share]

    def quantizer_gradient():
        swapped_in(swap_quant)
        push = quant_in[...].reshape(frames_all, latents) * frame_valid
        gap_back = gap_grad[...]
        looked_rows = looked[...]
        between = exact(looked_rows, gap_back, 0, 0)
        small[...] = jnp.zeros_like(small)

        def keep_small(row, rows):
            for index in range(time_count):
                columns = rows[:, index * wide_of : (index + 1) * wide_of]
                done = 0
                while done < rows.shape[0]:
                    fold, at = divmod(row + done, 128)
                    size = min(rows.shape[0] - done, 128 - at)
                    small[index, at : at + size, fold * wide_of : (fold + 1) * wide_of] = columns[
                        done : done + size
                    ]
                    done += size

        earlier_rows = jnp.where(
            lax.broadcasted_iota(jnp.int32, (count, phases), 0) // dims
            > lax.broadcasted_iota(jnp.int32, (count, phases), 1),
            1.0,
            0.0,
        )
        ones = jnp.ones((frames_all, phases), f32)
        keep_small(
            0,
            exact(gap_back, latent[...], 0, 0)
            - exact(exact(gap_back, looked_rows, 0, 0) * later, out_weight[...], 1, 0)
            - exact(exact(gap_back, ones, 0, 0) * earlier_rows, out_bias[...], 1, 0),
        )
        looked_back = exact(push, out_weight[...], 1, 1) - gap_back
        crossing = exact(out_weight[...], in_weight[...], 1, 1) * earlier
        looked_back = (looked_back - exact(gap_back, crossing, 1, 1)).T
        for phase in range(phases):
            rows = looked_back[phase * dims : (phase + 1) * dims, :]
            three = jnp.concatenate([part.astype(f32) for part in split_three(rows)], axis=0)
            found = dot(three.astype(bf16), onehot(codes, phase), 1, 0)
            keep_small(
                count + phase * dims, found[:dims] + found[dims : 2 * dims] + found[2 * dims :]
            )
        keep_small(
            2 * count,
            exact(looked_rows, push, 0, 0) - exact(between * earlier, in_weight[...], 1, 0),
        )
        gap_sum = jnp.sum(gap_back, axis=0, keepdims=True)
        keep_small(
            3 * count,
            jnp.sum(push, axis=0, keepdims=True)
            - exact(jnp.where(nine_rows < nine_columns, gap_sum, 0.0), in_weight[...], 1, 0),
        )
        row = 3 * count + phases
        keep_small(row, jnp.sum(lowered, axis=0, keepdims=True))
        fold, at = divmod(row + 1, 128)
        for index in range(time_count):
            small[index, at : at + 1, fold * wide_of : fold * wide_of + count] = gap_sum
        small_low[...] = small[...].astype(bf16)
        smalls_in = [
            remote(
                small_low.at[sibling(step)],
                small_in.at[step - 1],
                small_send.at[step - 1],
                small_recv.at[step - 1],
                (batch, sibling(step)),
            )
            for step in range(1, time_count)
        ]
        return smalls_in

    forward_pair(near_first[0])

    made.wait_recv()
    latent_pad[...] = jnp.zeros_like(latent_pad)
    latent_pad[8 : 8 + frames_all, :] = lowered
    neighbour = latent_in[...].astype(f32)
    latent_pad[7:8, :] = neighbour[15:, :] * last
    latent_pad[8 + frames_all : 9 + frames_all, :] = neighbour[:1, :] * first
    reach = frames_all + 8
    same = latent_pad[8 : 8 + reach, :].astype(bf16)
    previous = latent_pad[7 : 7 + reach, :].astype(bf16)
    run = reach * STRIDE
    for step in range(STRIDE):
        both = dot(same, down_tap(step), 1, 0) + dot(previous, down_tap(step + STRIDE), 1, 0)
        for tile in range(lane_tiles):
            spread[pl.ds(tile * run + step, reach, stride=STRIDE), :] = both[
                :, tile * 128 : (tile + 1) * 128
            ]

    alpha = row_of(snake_alpha, 6)
    inverse = 1.0 / alpha
    zero = jnp.zeros((8, channels), f32)

    def mixed_back(place, carry, edge):
        tiles = []
        for tile in range(lane_tiles):
            at = tile * run + STRIDE // 2 + place * ROWS
            tiles.append(spread[pl.ds(at, ROWS), :])
        upstream = jnp.concatenate(tiles, axis=1) * valid_rows(place)
        at = block_rows(place)
        slope, alpha_slope = snake_slopes(hidden[3, at, :], alpha, inverse)
        following = upstream * slope
        grad[at, :] = following
        keep_branch(2, place, following.astype(bf16))
        return carry + folded(upstream * alpha_slope)

    def keep_branch(unit, place, rows):
        branch[block_rows(place), :] = rows
        for index in range(time_count):
            shares[unit, index, 1, block_rows(place), :] = rows[
                :, index * share : (index + 1) * share
            ]

    alpha_sum, _ = each_block(mixed_back, zero)
    alpha_out[...] = jnp.zeros_like(alpha_out)
    keep_alpha(6, jnp.sum(alpha_sum, axis=0, keepdims=True))

    total = down.at[pl.ds(0, pieces[-1][0] + pieces[-1][1])]

    chunk_of = {start: rows // batch_count for start, rows in pieces}
    spread_z = members - 1
    copies = {}

    def add_into(target, start, sources, rows):
        def step(index, carry):
            at = index * 16
            block = target[pl.ds(pl.multiple_of(start + at, 16), 16), :].astype(f32)
            for ref, begin in sources:
                block += ref[pl.ds(pl.multiple_of(begin + at, 16), 16), :].astype(f32)
            target[pl.ds(pl.multiple_of(start + at, 16), 16), :] = block.astype(bf16)
            return carry

        lax.fori_loop(0, rows // 16, step, 0, unroll=min(4, rows // 16))

    def send_pair(number):
        start, rows = pieces[number]
        other = pl.ds(pl.multiple_of(start + (1 - half) * (rows // 2), 16), rows // 2)
        copies[number, 0] = remote(
            total.at[other],
            from_pair.at[pl.ds(start // 2, rows // 2)],
            piece_send.at[number, 0],
            piece_recv.at[number, 0],
            (pair, time),
        )

    def send_members(number):
        start, rows = pieces[number]
        copies[number, 0].wait_recv()
        mine = pl.multiple_of(start + half * (rows // 2), 16)
        add_into(total, mine, [(from_pair, start // 2)], rows // 2)
        chunk = rows // batch_count
        for step in range(1, members):
            at = mine + lax.rem(place_z + step, members) * chunk
            copies[number, step] = remote(
                total.at[pl.ds(pl.multiple_of(at, 16), chunk)],
                from_members.at[step - 1, pl.ds(start // batch_count, chunk)],
                piece_send.at[number, step],
                piece_recv.at[number, step],
                (member(step), time),
            )

    def send_back(number):
        start, rows = pieces[number]
        chunk = rows // batch_count
        for step in range(1, members):
            copies[number, step].wait_recv()
        mine = pl.multiple_of(start + half * (rows // 2) + place_z * chunk, 16)
        sources = [(from_members.at[step], start // batch_count) for step in range(spread_z)]
        block = total[pl.ds(mine, chunk), :].astype(f32)
        for ref, begin in sources:
            block += ref[pl.ds(begin, chunk), :].astype(f32)
        final[pl.ds(mine, chunk), :] = block.astype(bf16)
        for step in range(1, members):
            copies[number, spread_z + step] = remote(
                final.at[pl.ds(mine, chunk)],
                final.at[pl.ds(mine, chunk)],
                piece_send.at[number, spread_z + step],
                piece_recv.at[number, spread_z + step],
                (member(step), time),
            )

    def send_last(number):
        start, rows = pieces[number]
        for step in range(1, members):
            copies[number, spread_z + step].wait_recv()
        mine = pl.ds(pl.multiple_of(start + half * (rows // 2), 16), rows // 2)
        copies[number, 1 + 2 * spread_z] = remote(
            final.at[mine],
            final.at[mine],
            piece_send.at[number, 1 + 2 * spread_z],
            piece_recv.at[number, 1 + 2 * spread_z],
            (pair, time),
        )

    def finish(number):
        copies[number, 1 + 2 * spread_z].wait_recv()

    relays = {}

    def relay(unit):
        gather_across[unit].wait_recv()
        slot = gathered.at[unit, :, crops - 1 - mine, own]
        relays[unit] = remote(
            slot, slot, relay_send.at[unit], relay_recv.at[unit], (batch, core)
        )

    unit_rows = (TAPS + 1) * share
    unit_start = {unit: pieces[0][1] + unit * unit_rows for unit in range(3)}
    numbers = {
        unit: [
            number
            for number, (start, rows) in enumerate(pieces)
            if unit_start[unit] <= start < unit_start[unit] + unit_rows
        ]
        for unit in range(3)
    }
    everywhere = crops * rows_all
    shifted_start = down.shape[0] // 2
    share_pad[...] = jnp.zeros_like(share_pad)
    shares_in = {}
    bias_rows = {}

    def unit_gradient(unit):
        dilation = DILATIONS[unit]
        for copy in shares_in[unit]:
            copy.wait_recv()
        for crop in range(crops):
            share_pad[crop, RIM : RIM + everywhere, :] = share_all[unit, 0, crop].astype(f32)
        bias_rows[unit] = [
            jnp.sum(
                folded(
                    jnp.concatenate(
                        [share_all[unit, kind, crop].astype(f32) for crop in range(crops)], axis=0
                    )
                ),
                axis=0,
                keepdims=True,
            )
            for kind in range(2)
        ]
        for tap in range(TAPS):
            start = RIM - (tap - 3) * dilation
            for crop in range(crops):
                bank, lane = divmod(tap, time_count)
                begin = shifted_start + (bank * crops + crop) * everywhere
                down[begin : begin + everywhere, lane * share : (lane + 1) * share] = share_pad[
                    crop, start : start + everywhere, :
                ].astype(bf16)
        gather_core[unit].wait_recv()
        relays[unit].wait_recv()
        taken = gathered[unit, 0].reshape(crops * everywhere, channels)
        at = unit_start[unit]
        for bank in range(-(-TAPS // time_count)):
            begin = shifted_start + bank * crops * everywhere
            columns = min(TAPS - bank * time_count, time_count) * share
            moved = down[begin : begin + crops * everywhere, :columns]
            row = at + bank * channels
            total[row : row + columns, :] = dot(moved, taken, 0, 0).astype(bf16)
        taken = gathered[unit, 1].reshape(crops * everywhere, channels)
        narrow_share = share_all[unit, 1].reshape(crops * everywhere, share)
        total[at + TAPS * share : at + unit_rows, :] = dot(narrow_share, taken, 0, 0).astype(bf16)
        for number in numbers[unit]:
            send_pair(number)

    def small_gradient(smalls_in):
        for copy in smalls_in:
            copy.wait_recv()
        block = small[time]
        for step in range(time_count - 1):
            block += small_in[step].astype(f32)
        small[0] = block

    def lows_members():
        for copy in lows_in:
            copy.wait_recv()
        local(low_all, all_lows.at[batch], 1)
        for step in range(1, members):
            low_blocks.append(
                remote(
                    low_all,
                    all_lows.at[batch],
                    low_send.at[2 + step],
                    low_recv.at[2 + step],
                    (member(step), time),
                )
            )
        low_blocks.append(
            remote(
                low_all,
                all_lows.at[batch],
                low_send.at[2 + members],
                low_recv.at[2 + members],
                (pair, time),
            )
        )

    def lows_pair():
        for step in range(1, members):
            low_blocks[step - 1].wait_recv()
            slot = all_lows.at[block_of(step, half)]
            sems = 2 + members + step
            low_blocks.append(
                remote(slot, slot, low_send.at[sems], low_recv.at[sems], (pair, time))
            )

    def between_units(unit):
        if unit == 2:
            lows_members()
            for step in near_first[2:]:
                forward_pair(step)
        else:
            relay(unit + 1)
            if unit == 1:
                lows_pair()
            unit_gradient(unit + 1)

    def finish_all():
        order = numbers[2] + numbers[1] + numbers[0] + [0]
        stages = [send_members, send_back, send_last]
        for wave in range(len(order) + len(stages)):
            for depth, stage in enumerate(stages):
                if 0 <= wave - depth < len(order):
                    stage(order[wave - depth])
            if wave < members:
                forward_across(([0] + near_first)[wave])
        for step in ([0] + near_first)[len(order) + len(stages) :]:
            forward_across(step)
        forward_core(0)
        forward_core(1)
        for number in order:
            finish(number)
        for copy in core_blocks:
            copy.wait_recv()
        for copy in low_blocks[members - 1 :]:
            copy.wait_recv()

    for step in near_first[1:2]:
        forward_pair(step)
    for unit in (2, 1, 0):
        dilation = DILATIONS[unit]
        number = 5 + unit
        work[...] = dot(branch[...], narrow[unit], 1, 0)
        alpha = row_of(snake_alpha, 2 * unit + 1)
        inverse = 1.0 / alpha

        def conv_back(place, carry, edge):
            at = block_rows(place)
            upstream = work[at, :]
            slope, alpha_slope = snake_slopes(conv[unit, at, :], alpha, inverse)
            lowered = (upstream * slope).astype(bf16)
            for index in range(time_count):
                shares[unit, index, 0, at, :] = lowered[
                    :, index * share : (index + 1) * share
                ]
            pad[pad_rows(place), :] = lowered.astype(f32)
            keep_edge(number, edge, lowered)
            return carry + folded(upstream * alpha_slope)

        alpha_sum, made = each_block(conv_back, zero, lambda: start_halo(number))
        shares_in[unit] = [
            remote(
                shares.at[unit, sibling(step)],
                share_all.at[unit, :, mine, own],
                share_send.at[unit, step - 1],
                share_recv.at[unit, step - 1],
                (batch, sibling(step)),
            )
            for step in range(1, time_count)
        ]
        if unit == 2:
            gather(1)
        for kind in range(2):
            share_all[unit, kind, mine, own, :] = shares[unit, time, kind]
        keep_alpha(2 * unit + 1, jnp.sum(alpha_sum, axis=0, keepdims=True))
        between_units(unit)
        fill_rims(made, number)
        result = None
        for tap in range(TAPS):
            term = dot(shifted(-(tap - 3) * dilation), wide[unit, tap], 1, 0)
            result = term if result is None else result + term
        work[...] = result
        alpha = row_of(snake_alpha, 2 * unit)
        inverse = 1.0 / alpha

        def hidden_back(place, carry, edge):
            at = block_rows(place)
            upstream = work[at, :]
            slope, alpha_slope = snake_slopes(hidden[unit, at, :], alpha, inverse)
            following = grad[at, :] + upstream * slope
            if unit > 0:
                grad[at, :] = following
                keep_branch(unit - 1, place, following.astype(bf16))
            else:
                signal_out[at, :] = following * valid_rows(place)
            return carry + folded(upstream * alpha_slope)

        alpha_sum, _ = each_block(hidden_back, zero)
        keep_alpha(2 * unit, jnp.sum(alpha_sum, axis=0, keepdims=True))

    alphas_in = [
        remote(
            alpha_out.at[sibling(step)],
            alpha_in.at[step - 1],
            small_send.at[time_count - 1 + step - 1],
            small_recv.at[time_count - 1 + step - 1],
            (batch, sibling(step)),
        )
        for step in range(1, time_count)
    ]
    relay(0)
    unit_gradient(0)
    swap_back = swap(
        4,
        lambda part: signal_out.at[pl.ds(part * length, length)],
        lambda slot: signal_back.at[slot],
        mine,
        True,
    )
    small_gradient(quantizer_gradient())
    for copy in alphas_in:
        copy.wait_recv()
    alpha_rows = alpha_out[time]
    for step in range(time_count - 1):
        alpha_rows += alpha_in[step]
    rest = [alpha_rows] + [bias_rows[unit][kind] for kind in range(2) for unit in range(3)]
    rest = jnp.concatenate(rest + [jnp.zeros((2, share), f32)], axis=0)
    small[0, small.shape[1] - 16 :, channels - share :] = rest
    for start in range(0, pieces[0][1], small.shape[1]):
        total[start : start + small.shape[1], :] = small[0].astype(bf16)
    send_pair(0)

    finish_all()
    swapped_in(swap_back)
    swapped_in(swap_commit)
    for crop in range(crops):
        signal_grad[crop] = signal_back[crop].T
    for made in swaps:
        for peer, origin, away, here, arrived in made:

            @pl.when(peer != time)
            def _():
                away.wait_send()

    for copy in local_copies:
        copy.wait()
    for copy in sent:
        copy.wait_send()


def run_block(time_count, batch_count, pieces, lengths, *arrays):
    (signal, quant_cot, coded, wide, _, narrow, _, _, down, down_bias, in_weight) = arrays[:11]
    f32, bf16 = jnp.float32, jnp.bfloat16
    crops, channels, length = signal.shape
    latents = down_bias.shape[1]
    taps = down.shape[0] // latents
    frames = crops * (length // STRIDE)
    rows = crops * length
    count = in_weight.shape[0]
    share = channels // time_count
    wide_of = latents // time_count
    members = batch_count // 2
    everywhere = crops * rows
    total_rows = pieces[-1][0] + pieces[-1][1]
    vmem = pl.BlockSpec(memory_space=pltpu.VMEM)
    hbm = pl.BlockSpec(memory_space=pl.ANY)
    in_specs = [pl.BlockSpec(memory_space=pltpu.SMEM)] + [vmem] * len(arrays)
    for place in (3, 5, 8):
        in_specs[1 + place] = hbm
    lane_tiles = channels // 128
    dma = pltpu.SemaphoreType.DMA
    slots = 2 * members
    return pl.pallas_call(
        functools.partial(block_kernel, time_count, batch_count, pieces),
        out_shape=(
            jax.ShapeDtypeStruct(quant_cot.shape, f32),
            jax.ShapeDtypeStruct(coded.shape, f32),
            jax.ShapeDtypeStruct(signal.shape, f32),
            jax.ShapeDtypeStruct((total_rows, channels), bf16),
            jax.ShapeDtypeStruct((batch_count, time_count, STRIDE, frames, channels), bf16),
            jax.ShapeDtypeStruct((batch_count, time_count, frames, wide_of), bf16),
        ),
        in_specs=in_specs,
        out_specs=(vmem, vmem, vmem, vmem, hbm, hbm),
        scratch_shapes=[
            pltpu.VMEM(wide.shape, bf16),
            pltpu.VMEM(narrow.shape, bf16),
            pltpu.VMEM((taps * latents, channels), bf16),
            pltpu.VMEM((4, rows, channels), f32),
            pltpu.VMEM((3, rows, channels), f32),
            pltpu.VMEM((3, 2, crops, everywhere, channels), bf16),
            pltpu.VMEM((rows + 2 * RIM, channels), f32),
            pltpu.VMEM((rows, channels), f32),
            pltpu.VMEM((rows, channels), f32),
            pltpu.VMEM((rows, channels), bf16),
            pltpu.VMEM((3, time_count, 2, rows, share), bf16),
            pltpu.VMEM((3, 2, crops, everywhere, share), bf16),
            pltpu.VMEM((crops, everywhere + 2 * RIM, share), f32),
            pltpu.VMEM((lane_tiles * (rows + 16), 128), f32),
            pltpu.VMEM((taps, frames, channels), bf16),
            pltpu.VMEM((frames, latents), f32),
            pltpu.VMEM((frames + 16, latents), f32),
            pltpu.VMEM((lane_tiles * (rows + 8 * STRIDE), 128), f32),
            pltpu.VMEM((frames, count), f32),
            pltpu.VMEM((frames, count), f32),
            pltpu.VMEM((frames, count), f32),
            pltpu.VMEM((time_count, 128, channels), f32),
            pltpu.VMEM((time_count, 128, channels), bf16),
            pltpu.VMEM((time_count - 1, 128, channels), bf16),
            pltpu.VMEM((time_count, 8, share), f32),
            pltpu.VMEM((time_count - 1, 8, share), f32),
            pltpu.VMEM((time_count, frames, wide_of), bf16),
            pltpu.VMEM((time_count, frames, wide_of), bf16),
            pltpu.VMEM((144, channels), bf16),
            pltpu.VMEM((144, channels), bf16),
            pltpu.VMEM((frames, latents), bf16),
            pltpu.VMEM((16, latents), bf16),
            pltpu.VMEM(signal.shape, f32),
            pltpu.VMEM(quant_cot.shape, f32),
            pltpu.VMEM(coded.shape, f32),
            pltpu.VMEM(coded.shape, f32),
            pltpu.VMEM((rows, channels), f32),
            pltpu.VMEM((crops, length, channels), f32),
            dma((5,)),
            dma((5, 2)),
            dma((5, 2)),
            pltpu.VMEM((total_rows // 2, channels), bf16),
            pltpu.VMEM((members - 1, total_rows // batch_count, channels), bf16),
            dma((8,)),
            dma((2,)),
            dma((8,)),
            dma((8,)),
            dma((3, 2)),
            dma((3, 2)),
            dma((3,)),
            dma((3,)),
            dma((3, time_count - 1)),
            dma((3, time_count - 1)),
            dma((2 * (time_count - 1),)),
            dma((2 * (time_count - 1),)),
            dma((2 + 2 * members,)),
            dma((2 + 2 * members,)),
            dma((4 * members + 2,)),
            dma((4 * members + 2,)),
            dma((len(pieces), slots)),
            dma((len(pieces), slots)),
        ],
        compiler_params=pltpu.CompilerParams(
            collective_id=1, has_side_effects=True, vmem_limit_bytes=62 * 2**20
        ),
    )(lengths, *arrays)


def down_kernel(lows, phases, out, held, columns, in_sems, out_sems):
    count = lows.shape[2]
    group, lanes = held.shape[1], held.shape[4]
    rows = group * held.shape[3]
    tiles = lanes // 128
    groups = phases.shape[0] // group
    items = [(part, at) for part in range(phases.shape[3] // lanes) for at in range(groups)]
    loads = [
        pltpu.make_async_copy(
            phases.at[pl.ds(at * group, group), :, :, pl.ds(part * lanes, lanes)],
            held.at[index % 2],
            in_sems.at[index % 2],
        )
        for index, (part, at) in enumerate(items)
    ]
    for load in loads[:2]:
        load.start()
    stores = []
    after = before = None
    for index, (part, at) in enumerate(items):
        if after is None or groups > 1:
            turned = [lows[kind, at * rows : (at + 1) * rows].T for kind in range(3)]
            after = jnp.concatenate([turned[0], turned[1]], axis=0)
            before = jnp.concatenate([turned[0], turned[2]], axis=0)
        loads[index].wait()
        for step in range(STRIDE):
            block = held[index % 2, :, step].reshape(rows, lanes)
            late = step >= STRIDE // 2
            both = dot(after if late else before, block, 1, 0)
            middle = step + STRIDE // 2
            for tap, row in ((middle, 0), (middle - STRIDE if late else middle + STRIDE, count)):
                for tile in range(tiles):
                    place = pl.ds(tap, count, stride=2 * STRIDE)
                    value = both[row : row + count, tile * 128 : (tile + 1) * 128]
                    if at > 0:
                        value = value + columns[part * tiles + tile, place, :]
                    columns[part * tiles + tile, place, :] = value
        if index + 2 < len(items):
            loads[index + 2].start()
        if at == groups - 1:
            for tile in range(part * tiles, (part + 1) * tiles):
                stores.append(
                    pltpu.make_async_copy(
                        columns.at[tile], out.at[:, pl.ds(tile * 128, 128)], out_sems.at[tile]
                    )
                )
                stores[-1].start()
    for store in stores:
        store.wait()


def down_gradient(lows, phases):
    devices, _, rows, channels = phases.shape
    count = lows.shape[2]
    lanes = 256
    hbm = pl.BlockSpec(memory_space=pl.ANY)
    return pl.pallas_call(
        down_kernel,
        out_shape=jax.ShapeDtypeStruct((count * 2 * STRIDE, channels), jnp.float32),
        in_specs=[pl.BlockSpec(memory_space=pltpu.VMEM), hbm],
        out_specs=hbm,
        scratch_shapes=[
            pltpu.VMEM((2, min(devices, 32), STRIDE, rows, lanes), phases.dtype),
            pltpu.VMEM((channels // 128, count * 2 * STRIDE, 128), jnp.float32),
            pltpu.SemaphoreType.DMA((2,)),
            pltpu.SemaphoreType.DMA((channels // 128,)),
        ],
        compiler_params=pltpu.CompilerParams(vmem_limit_bytes=60 * 2**20),
    )(lows, phases)


def body(
    signal,
    quant_cot,
    commit_cot,
    lengths,
    codes,
    wide_weight,
    wide_bias,
    narrow_weight,
    narrow_bias,
    snake_alpha,
    down_weight,
    down_bias,
    in_weight,
    in_bias,
    codebook,
    out_weight,
    out_bias,
):
    time_count = lax.axis_size("tm")
    batch_count = lax.axis_size("batch")
    crop_count, channel_count, length = signal.shape
    latent_count, tap_count, _ = down_weight.shape
    phases, dims = in_weight.shape[:2]
    count = phases * dims
    frame_count = length // STRIDE
    small_rows = 16 * batch_count
    unit_rows = (TAPS + 1) * (channel_count // time_count)
    piece = max(unit_rows // 2, small_rows)
    pieces = [(0, small_rows)]
    pieces += [(at, piece) for at in range(small_rows, small_rows + 3 * unit_rows, piece)]
    coded = [jnp.swapaxes(codes, 1, 2).astype(jnp.float32), jnp.swapaxes(commit_cot, 1, 2)]
    coded = jnp.pad(jnp.concatenate(coded, axis=2), ((0, 0), (0, 0), (0, 128 - 2 * phases)))
    quantized, commit, signal_grad, summed, all_phases, all_low = run_block(
        time_count,
        batch_count,
        tuple(pieces),
        lengths,
        signal,
        quant_cot,
        coded,
        jnp.swapaxes(wide_weight, 1, 2),
        wide_bias,
        narrow_weight,
        narrow_bias,
        snake_alpha,
        down_weight.reshape(-1, channel_count),
        down_bias.reshape(1, -1),
        in_weight.reshape(count, -1),
        in_bias.reshape(1, -1),
        codebook.reshape(count, -1),
        out_weight.reshape(count, -1),
        out_bias,
    )
    commit = jnp.swapaxes(commit[:, :, :phases], 1, 2)

    share = latent_count // time_count
    all_phases = all_phases.reshape((-1,) + all_phases.shape[2:])
    line = all_low.reshape(batch_count * crop_count, time_count * frame_count, share)
    after = jnp.pad(line[:, 1:], ((0, 0), (0, 1), (0, 0)))
    before = jnp.pad(line[:, :-1], ((0, 0), (1, 0), (0, 0)))
    lows = jnp.stack([line, after, before])
    lows = lows.reshape(3, -1, share)

    wide_of = latent_count // time_count
    small = summed[:128].astype(jnp.float32)
    small = jnp.concatenate([small[:, :wide_of], small[:, wide_of : 2 * wide_of]], axis=0)
    in_weight_out = small[:count].reshape(phases, dims, -1)
    codebook_out = small[count : 2 * count].reshape(phases, dims, -1)
    out_weight_out = small[2 * count : 3 * count].reshape(phases, dims, -1)
    row = 3 * count + phases
    out_bias_out = small[3 * count : row]
    down_bias_out = small[row]
    narrow_of = channel_count // time_count
    in_bias_all = small[row + 1, :count].reshape(phases, dims)
    part = dims // time_count
    in_bias_out = lax.dynamic_slice_in_dim(in_bias_all, lax.axis_index("tm") * part, part, axis=1)
    last = summed[112:128, -narrow_of:].astype(jnp.float32)
    alpha_out, wide_bias_out, narrow_bias_out = last[:7], last[8:11], last[11:14]
    units = summed[small_rows:].reshape(3, unit_rows, channel_count)
    wide_out = units[:, : TAPS * narrow_of].astype(jnp.float32)
    wide_out = wide_out.reshape(3, TAPS, narrow_of, channel_count)
    wide_out = jnp.swapaxes(wide_out, 1, 2)
    narrow_out = units[:, TAPS * narrow_of :].astype(jnp.float32)
    down_out = down_gradient(lows, all_phases).reshape(share, tap_count, channel_count)
    return (
        quantized,
        commit,
        signal_grad,
        wide_out,
        wide_bias_out,
        narrow_out,
        narrow_bias_out,
        alpha_out,
        down_out,
        down_bias_out,
        in_weight_out,
        in_bias_out,
        codebook_out,
        out_weight_out,
        out_bias_out,
    )


def solution(mesh):
    return jax.shard_map(
        body,
        mesh=mesh,
        in_specs=(
            P("batch", None, "tm"),
            P("batch", "tm", None),
            P("batch", None, "tm"),
            P("batch"),
            P("batch", None, "tm"),
            P(),
            P(),
            P(),
            P(),
            P(),
            P(),
            P(),
            P(),
            P(),
            P(),
            P(),
            P(),
        ),
        out_specs=(
            P("batch", "tm", None),
            P("batch", None, "tm"),
            P("batch", None, "tm"),
            P(None, "tm", None, None),
            P(None, "tm"),
            P(None, "tm", None),
            P(None, "tm"),
            P(None, "tm"),
            P("tm", None, None),
            P("tm"),
            P(None, None, "tm"),
            P(None, "tm"),
            P(None, None, "tm"),
            P(None, None, "tm"),
            P(None, "tm"),
        ),
        check_vma=False,
    )
```

time: 261 us -> 210 us (0.80); the launches traced: 257 us -> 209 us
  Pallas kernels: 222 us -> 190 us
  between operations: 14.2 us -> 0.76 us
  local copies, waits for them, and re-layouts: 17 us -> 10.3 us
  other arithmetic: 2.93 us -> 7.85 us
    pallas_call x2 -> x1, Pallas kernels: 210 us -> 178 us  [run_block(): pl.pallas_call(functools.partial(block_kernel, time_count, batch_count, p...]
    slice x7 -> x5, local copies, waits for them, and re-layouts: 7.08 us -> 1.58 us  [the longest x1 0.59 us: body(): last[:7]]
    transpose x0 -> x1, other arithmetic: none -> 3.2 us  [body(): wide_out = jnp.swapaxes(wide_out, 1, 2)]
    transpose x3 -> x1, local copies, waits for them, and re-layouts: 2.81 us -> 0.01 us  [body(): commit = jnp.swapaxes(commit[:, :, :phases], 1, 2)]
  transfers between devices with their start and end apart: 2 -> 0, of which waited for: 0 -> 0; matrix products, arithmetic and copies ran while one was open for 5% -> 0% of each run, Pallas kernels for 59% -> 0%
where the time goes in v3:
time: 210 us; the launch traced here: 209 us
  Pallas kernels  190 us (90%)
  local copies, waits for them, and re-layouts  10.3 us (5%)
  other arithmetic  7.85 us (4%)
    pallas_call x1, Pallas kernels, run_block(): pl.pallas_call(functools.partial(block_kernel, time_count, batch_count, p...  178 us
    pallas_call x1, Pallas kernels, down_gradient(): pl.pallas_call(down_kernel, out_shape=jax.ShapeDtypeStruct((count * 2 * S...  12.3 us
    unnamed x17, local copies, waits for them, and re-layouts  5.14 us

profile of v3, /device:TPU:0, one launch (start us, length us, event | category | flops | bytes accessed | tf_op | source)
XLA Modules:
  0.0 209.2 jit_solution(9368616585676841193)
XLA Ops:
  0.6 0.8 copy.37
  1.4 0.8 copy.38
  2.2 0.7 select_maximum_fusion.coded
  2.9 0.8 copy.39
  3.7 0.6 reshape.83.in_bias
  4.3 178.0 %shard_map.280 = (f32[2,16,1024]{2,1,0:T(8,128)}, f32[2,16,128]{2,1,0:T(8,128)}, f32[2,512,128]{2,1,0:T(8,128)}, bf16[3200,512]{1,0:T(8,128)(2,1)}, bf16[8,4,8,3...) custom-call(s32[2]{0:T(128)} %lengths.1, f32[2,512,128]{2,1,0:T(8,128)} %signal.1, f32[2,16,1024]{2,1,0:T(8,128)} %quant_cot.1, ...), custom_call_target="tpu_custom_call" | custom-call | tf_op jit(solution)/shard_map/pallas_call | solution.py:1090
  182.3 0.0 copy-start
  182.3 1.0 slice_convert_fusion.1
  183.3 0.7 slice_bitcast_fusion
  184.0 1.4 fusion.1
  185.5 0.2 pad.14
  185.7 0.0 copy-done
  185.7 1.3 pad_maximum_fusion.lows
  187.0 0.0 copy-start.1
  187.0 12.3 %shard_map.281 = f32[4096,512]{1,0:T(8,128)} custom-call(bf16[3,1024,256]{2,1,0:T(8,128)(2,1)} %pad_maximum_fusion.lows, bf16[32,8,32,512]{3,2,1,0:T(8,128)(2,1)} %bitcast.35), custom_call_target="tpu_custom_call" | custom-call | tf_op jit(solution)/shard_map/pallas_call | solution.py:1227
  199.3 0.1 reshape_squeeze.3
  199.4 0.1 constant_dynamic-slice_fusion
  199.4 0.7 copy.41
  200.1 0.6 slice.94
  200.7 0.6 slice.88
  201.3 0.0 copy-done.1
  201.3 0.6 fusion.3
  201.9 0.2 slice.63
  202.1 0.2 slice.81
  202.3 0.0 copy-start.4
  202.3 0.0 copy-start.3
  202.3 0.0 copy-start.2
  202.3 3.2 %convert_bitcast_fusion = f32[3,128,7,512]{3,1,2,0:T(8,128)} fusion(bf16[3,7,128,512]{3,2,1,0:T(8,128)(2,1)S(1)} %bitcast.33), kind=kLoop, calls=%fused_computation | loop fusion | flops 1376256 | bytes 8257536 | tf_op jit(solution)/shard_map/transpose | solution.py:1324
  205.5 1.0 slice_convert_fusion
  206.5 0.6 slice.85
  207.1 0.0 copy-done.4
  207.1 0.7 copy.40
  207.8 0.0 copy-done.3
  207.8 0.7 copy.44
  208.4 0.0 copy-done.2
  208.4 0.8 copy.45
  (6 shorter events, 0.1 us)
Async XLA Ops:
  182.3 3.4 %copy-start = (bf16[8,4,32,256]{3,2,1,0:T(8,128)(2,1)S(1)}, bf16[8,4,32,256]{3,2,1,0:T(8,128)(2,1)}, u32[]{:S(2)}) copy-start(bf16[8,4,32,256]{3,2,1,0:T(8,128)(2,1)} %get-tuple-element.25) | copy-start | bytes 1572868
  187.0 14.3 %copy-start.1 = (bf16[3200,512]{1,0:T(8,128)(2,1)S(1)}, bf16[3200,512]{1,0:T(8,128)(2,1)}, u32[]{:S(2)}) copy-start(bf16[3200,512]{1,0:T(8,128)(2,1)} %get-tuple-element.24) | copy-start | bytes 9830404
  202.3 4.8 %copy-start.4 = (f32[2,16,128]{2,1,0:T(8,128)S(1)}, f32[2,16,128]{2,1,0:T(8,128)}, u32[]{:S(2)}) copy-start(f32[2,16,128]{2,1,0:T(8,128)} %get-tuple-element.22) | copy-start | bytes 49156
  202.3 5.5 %copy-start.3 = (f32[2,16,1024]{2,1,0:T(8,128)S(1)}, f32[2,16,1024]{2,1,0:T(8,128)}, u32[]{:S(2)}) copy-start(f32[2,16,1024]{2,1,0:T(8,128)} %get-tuple-element.81) | copy-start | bytes 393220
  202.3 6.1 %copy-start.2 = (f32[2,512,128]{2,1,0:T(8,128)S(1)}, f32[2,512,128]{2,1,0:T(8,128)}, u32[]{:S(2)}) copy-start(f32[2,512,128]{2,1,0:T(8,128)} %get-tuple-element.83) | copy-start | bytes 1572868

commit v4 on v3

--- a/solution.py
+++ b/solution.py
@@ -145,7 +145,6 @@
     swap_send,
     swap_recv,
     from_pair,
-    from_members,
     weight_sems,
     local_sems,
     send_sems,
@@ -346,9 +345,9 @@
         return tiles[:, tap].reshape(latents, channels)
 
     pl.semaphore_wait(barrier, len(peers))
+    swap_coded = swap(2, lambda part: coded.at[part], lambda slot: coded_in.at[slot], side, False)
     swap_signal = swap(0, lambda part: signal.at[part], lambda slot: signal_in.at[slot], side, False)
     swap_quant = swap(1, lambda part: quant_cot.at[part], lambda slot: quant_in.at[slot], side, False)
-    swap_coded = swap(2, lambda part: coded.at[part], lambda slot: coded_in.at[slot], side, False)
     wide_copies[0].start()
     narrow_copy.start()
     for copy in down_copies:
@@ -379,6 +378,95 @@
         (exact(looked_rows, out_weight[...], 1, 0) + jnp.sum(out_bias[...], axis=0, keepdims=True))
         * frame_valid
     ).reshape(quantized.shape)
+    for part in range(4):
+        reorder(part)
+
+    swapped_in(swap_signal)
+    for part in range(crops):
+        places = side * rows_all + part * length + lax.broadcasted_iota(jnp.int32, (length, 1), 0)
+        keep = jnp.where(places < lengths[mine], 1.0, 0.0)
+        hidden[0, part * length : (part + 1) * length, :] = signal_in[part].T * keep
+
+    def block_rows(place):
+        return pl.ds(pl.multiple_of(place * ROWS, ROWS), ROWS)
+
+    def own_rows(place):
+        return pl.ds(pl.multiple_of(side * rows_all + place * ROWS, ROWS), ROWS)
+
+    own = pl.ds(pl.multiple_of(side * rows_all, rows_all), rows_all)
+
+    def pad_rows(place):
+        return pl.ds(pl.multiple_of(RIM + place * ROWS, ROWS), ROWS)
+
+    def shifted(offset):
+        start = RIM + offset
+        return pad[start : start + rows_all, :].astype(bf16)
+
+    gather_across, gather_core = {}, {}
+
+    def gather(unit):
+        slot = gathered.at[unit, :, mine, own]
+        gather_across[unit] = remote(
+            slot, slot, gather_send.at[unit, 0], gather_recv.at[unit, 0], (batch, across)
+        )
+        gather_core[unit] = remote(
+            slot, slot, gather_send.at[unit, 1], gather_recv.at[unit, 1], (batch, core)
+        )
+
+    for unit in range(3):
+        dilation = DILATIONS[unit]
+        alpha = row_of(snake_alpha, 2 * unit)
+        inverse = 1.0 / alpha
+
+        def first_snake(place, carry, edge):
+            low = snake_of(hidden[unit, block_rows(place), :], alpha, inverse).astype(bf16)
+            gathered[unit, 0, mine, own_rows(place), :] = low
+            pad[pad_rows(place), :] = low.astype(f32)
+            keep_edge(unit, edge, low)
+            return carry
+
+        _, made = each_block(first_snake, 0, lambda: start_halo(unit))
+        fill_rims(made, unit)
+        wide_copies[unit].wait()
+        result = None
+        for tap in range(TAPS):
+            term = dot(shifted((tap - 3) * dilation), wide[unit, tap], 1, 1)
+            result = term if result is None else result + term
+        conv[unit] = result + row_of(wide_bias, unit)
+        alpha = row_of(snake_alpha, 2 * unit + 1)
+        inverse = 1.0 / alpha
+
+        def second_snake(place, carry, edge):
+            values = snake_of(conv[unit, block_rows(place), :], alpha, inverse)
+            gathered[unit, 1, mine, own_rows(place), :] = values.astype(bf16)
+            return carry
+
+        each_block(second_snake, 0)
+        if unit == 0:
+            narrow_copy.wait()
+        if unit != 1:
+            gather(unit)
+        rounded = gathered[unit, 1, mine, own, :]
+        hidden[unit + 1] = (
+            hidden[unit] + dot(rounded, narrow[unit], 1, 1) + row_of(narrow_bias, unit)
+        )
+
+    lane_tiles = channels // 128
+    stretch = rows_all + 16
+    alpha = row_of(snake_alpha, 6)
+    inverse = 1.0 / alpha
+
+    def last_snake(place, carry, edge):
+        values = snake_of(hidden[3, block_rows(place), :], alpha, inverse)
+        low = (values * valid_rows(place)).astype(bf16)
+        keep_edge(3, edge, low)
+        wider = low.astype(f32)
+        for tile in range(lane_tiles):
+            at = pl.multiple_of(tile * stretch + 8 + place * ROWS, 8)
+            mixed_pad[pl.ds(at, ROWS), :] = wider[:, tile * 128 : (tile + 1) * 128]
+        return carry
+
+    _, made = each_block(last_snake, 0, lambda: start_halo(3))
     swapped_in(swap_coded)
     codes = coded_in[...].reshape(frames_all, -1)
     looked[...] = look_up(codes)
@@ -396,95 +484,6 @@
     bias_terms = jnp.sum(jnp.where(nine_rows < nine_columns, bias_terms, 0.0), axis=0, keepdims=True)
     correction[...] = exact(looked_rows, crossing, 1, 0) + bias_terms - in_bias[...]
 
-    for part in range(4):
-        reorder(part)
-
-    swapped_in(swap_signal)
-    for part in range(crops):
-        places = side * rows_all + part * length + lax.broadcasted_iota(jnp.int32, (length, 1), 0)
-        keep = jnp.where(places < lengths[mine], 1.0, 0.0)
-        hidden[0, part * length : (part + 1) * length, :] = signal_in[part].T * keep
-
-    def block_rows(place):
-        return pl.ds(pl.multiple_of(place * ROWS, ROWS), ROWS)
-
-    def own_rows(place):
-        return pl.ds(pl.multiple_of(side * rows_all + place * ROWS, ROWS), ROWS)
-
-    own = pl.ds(pl.multiple_of(side * rows_all, rows_all), rows_all)
-
-    def pad_rows(place):
-        return pl.ds(pl.multiple_of(RIM + place * ROWS, ROWS), ROWS)
-
-    def shifted(offset):
-        start = RIM + offset
-        return pad[start : start + rows_all, :].astype(bf16)
-
-    gather_across, gather_core = {}, {}
-
-    def gather(unit):
-        slot = gathered.at[unit, :, mine, own]
-        gather_across[unit] = remote(
-            slot, slot, gather_send.at[unit, 0], gather_recv.at[unit, 0], (batch, across)
-        )
-        gather_core[unit] = remote(
-            slot, slot, gather_send.at[unit, 1], gather_recv.at[unit, 1], (batch, core)
-        )
-
-    for unit in range(3):
-        dilation = DILATIONS[unit]
-        alpha = row_of(snake_alpha, 2 * unit)
-        inverse = 1.0 / alpha
-
-        def first_snake(place, carry, edge):
-            low = snake_of(hidden[unit, block_rows(place), :], alpha, inverse).astype(bf16)
-            gathered[unit, 0, mine, own_rows(place), :] = low
-            pad[pad_rows(place), :] = low.astype(f32)
-            keep_edge(unit, edge, low)
-            return carry
-
-        _, made = each_block(first_snake, 0, lambda: start_halo(unit))
-        fill_rims(made, unit)
-        wide_copies[unit].wait()
-        result = None
-        for tap in range(TAPS):
-            term = dot(shifted((tap - 3) * dilation), wide[unit, tap], 1, 1)
-            result = term if result is None else result + term
-        conv[unit] = result + row_of(wide_bias, unit)
-        alpha = row_of(snake_alpha, 2 * unit + 1)
-        inverse = 1.0 / alpha
-
-        def second_snake(place, carry, edge):
-            values = snake_of(conv[unit, block_rows(place), :], alpha, inverse)
-            gathered[unit, 1, mine, own_rows(place), :] = values.astype(bf16)
-            return carry
-
-        each_block(second_snake, 0)
-        if unit == 0:
-            narrow_copy.wait()
-        if unit != 1:
-            gather(unit)
-        rounded = gathered[unit, 1, mine, own, :]
-        hidden[unit + 1] = (
-            hidden[unit] + dot(rounded, narrow[unit], 1, 1) + row_of(narrow_bias, unit)
-        )
-
-    lane_tiles = channels // 128
-    stretch = rows_all + 16
-    alpha = row_of(snake_alpha, 6)
-    inverse = 1.0 / alpha
-
-    def last_snake(place, carry, edge):
-        values = snake_of(hidden[3, block_rows(place), :], alpha, inverse)
-        low = (values * valid_rows(place)).astype(bf16)
-        keep_edge(3, edge, low)
-        wider = low.astype(f32)
-        for tile in range(lane_tiles):
-            at = pl.multiple_of(tile * stretch + 8 + place * ROWS, 8)
-            mixed_pad[pl.ds(at, ROWS), :] = wider[:, tile * 128 : (tile + 1) * 128]
-        return carry
-
-    _, made = each_block(last_snake, 0, lambda: start_halo(3))
     made.wait_recv()
     begin = halo_start[3]
     rim = halo_in[begin : begin + 16, :].astype(f32)
@@ -735,83 +734,68 @@
 
     total = down.at[pl.ds(0, pieces[-1][0] + pieces[-1][1])]
 
-    chunk_of = {start: rows // batch_count for start, rows in pieces}
-    spread_z = members - 1
-    copies = {}
-
-    def add_into(target, start, sources, rows):
+    copies, regions = {}, {}
+
+    def add_into(target, start, source, begin, other, at_other, rows):
         def step(index, carry):
             at = index * 16
-            block = target[pl.ds(pl.multiple_of(start + at, 16), 16), :].astype(f32)
-            for ref, begin in sources:
-                block += ref[pl.ds(pl.multiple_of(begin + at, 16), 16), :].astype(f32)
+            block = source[pl.ds(pl.multiple_of(begin + at, 16), 16), :].astype(f32)
+            block += other[pl.ds(pl.multiple_of(at_other + at, 16), 16), :].astype(f32)
             target[pl.ds(pl.multiple_of(start + at, 16), 16), :] = block.astype(bf16)
             return carry
 
         lax.fori_loop(0, rows // 16, step, 0, unroll=min(4, rows // 16))
 
+    def partner_of(bit):
+        return batch + bit - 2 * bit * lax.rem(batch // bit, 2)
+
+    def rows_at(start, rows):
+        return pl.ds(pl.multiple_of(start, 16), rows)
+
+    def send_half(number, level):
+        begin, rows = regions[number, level]
+        bit = bits_of[number][level]
+        upper = lax.rem(batch // bit, 2)
+        rows = rows // 2
+        inbox = pieces[number][0] + pieces[number][1] - 2 * rows
+        regions[number, level + 1] = (begin + upper * rows, rows)
+        copies[number, level] = remote(
+            total.at[rows_at(begin + (1 - upper) * rows, rows)],
+            from_pair.at[pl.ds(inbox, rows)],
+            piece_send.at[number, level],
+            piece_recv.at[number, level],
+            (partner_of(bit), time),
+        )
+
+    def send_back(number, level):
+        begin, rows = regions[number, level + 1]
+        sems = 2 * len(bits_of[number]) - 1 - level
+        copies[number, sems] = remote(
+            final.at[rows_at(begin, rows)],
+            final.at[rows_at(begin, rows)],
+            piece_send.at[number, sems],
+            piece_recv.at[number, sems],
+            (partner_of(bits_of[number][level]), time),
+        )
+
     def send_pair(number):
-        start, rows = pieces[number]
-        other = pl.ds(pl.multiple_of(start + (1 - half) * (rows // 2), 16), rows // 2)
-        copies[number, 0] = remote(
-            total.at[other],
-            from_pair.at[pl.ds(start // 2, rows // 2)],
-            piece_send.at[number, 0],
-            piece_recv.at[number, 0],
-            (pair, time),
-        )
-
-    def send_members(number):
-        start, rows = pieces[number]
-        copies[number, 0].wait_recv()
-        mine = pl.multiple_of(start + half * (rows // 2), 16)
-        add_into(total, mine, [(from_pair, start // 2)], rows // 2)
-        chunk = rows // batch_count
-        for step in range(1, members):
-            at = mine + lax.rem(place_z + step, members) * chunk
-            copies[number, step] = remote(
-                total.at[pl.ds(pl.multiple_of(at, 16), chunk)],
-                from_members.at[step - 1, pl.ds(start // batch_count, chunk)],
-                piece_send.at[number, step],
-                piece_recv.at[number, step],
-                (member(step), time),
-            )
-
-    def send_back(number):
-        start, rows = pieces[number]
-        chunk = rows // batch_count
-        for step in range(1, members):
-            copies[number, step].wait_recv()
-        mine = pl.multiple_of(start + half * (rows // 2) + place_z * chunk, 16)
-        sources = [(from_members.at[step], start // batch_count) for step in range(spread_z)]
-        block = total[pl.ds(mine, chunk), :].astype(f32)
-        for ref, begin in sources:
-            block += ref[pl.ds(begin, chunk), :].astype(f32)
-        final[pl.ds(mine, chunk), :] = block.astype(bf16)
-        for step in range(1, members):
-            copies[number, spread_z + step] = remote(
-                final.at[pl.ds(mine, chunk)],
-                final.at[pl.ds(mine, chunk)],
-                piece_send.at[number, spread_z + step],
-                piece_recv.at[number, spread_z + step],
-                (member(step), time),
-            )
-
-    def send_last(number):
-        start, rows = pieces[number]
-        for step in range(1, members):
-            copies[number, spread_z + step].wait_recv()
-        mine = pl.ds(pl.multiple_of(start + half * (rows // 2), 16), rows // 2)
-        copies[number, 1 + 2 * spread_z] = remote(
-            final.at[mine],
-            final.at[mine],
-            piece_send.at[number, 1 + 2 * spread_z],
-            piece_recv.at[number, 1 + 2 * spread_z],
-            (pair, time),
-        )
-
-    def finish(number):
-        copies[number, 1 + 2 * spread_z].wait_recv()
+        regions[number, 0] = pieces[number]
+        send_half(number, 0)
+
+    def advance(stage, number):
+        levels = len(bits_of[number])
+        copies[number, stage].wait_recv()
+        if stage < levels:
+            begin, rows = regions[number, stage + 1]
+            inbox = pieces[number][0] + pieces[number][1] - 2 * rows
+            target = final if stage + 1 == levels else total
+            add_into(target, begin, total, begin, from_pair, inbox, rows)
+            if stage + 1 < levels:
+                send_half(number, stage + 1)
+            else:
+                send_back(number, stage)
+        elif stage + 1 < 2 * levels:
+            send_back(number, 2 * levels - 2 - stage)
 
     relays = {}
 
@@ -834,6 +818,12 @@
     }
     everywhere = crops * rows_all
     shifted_start = down.shape[0] // 2
+    levels = batch_count.bit_length() - 1
+    bits_of = {}
+    for number in range(len(pieces)):
+        bits_of[number] = [2**level for level in range(levels)]
+        if number in [numbers[unit][0 if unit == 0 else -1] for unit in range(3)]:
+            bits_of[number][:2] = [2, 1]
     share_pad[...] = jnp.zeros_like(share_pad)
     shares_in = {}
     bias_rows = {}
@@ -934,7 +924,7 @@
 
     def finish_all():
         order = numbers[2] + numbers[1] + numbers[0] + [0]
-        stages = [send_members, send_back, send_last]
+        stages = [functools.partial(advance, stage) for stage in range(2 * levels)]
         for wave in range(len(order) + len(stages)):
             for depth, stage in enumerate(stages):
                 if 0 <= wave - depth < len(order):
@@ -945,8 +935,6 @@
             forward_across(step)
         forward_core(0)
         forward_core(1)
-        for number in order:
-            finish(number)
         for copy in core_blocks:
             copy.wait_recv()
         for copy in low_blocks[members - 1 :]:
@@ -1082,7 +1070,7 @@
     vmem = pl.BlockSpec(memory_space=pltpu.VMEM)
     hbm = pl.BlockSpec(memory_space=pl.ANY)
     in_specs = [pl.BlockSpec(memory_space=pltpu.SMEM)] + [vmem] * len(arrays)
-    for place in (3, 5, 8):
+    for place in (0, 1, 3, 5, 8):
         in_specs[1 + place] = hbm
     lane_tiles = channels // 128
     dma = pltpu.SemaphoreType.DMA
@@ -1141,8 +1129,7 @@
             dma((5,)),
             dma((5, 2)),
             dma((5, 2)),
-            pltpu.VMEM((total_rows // 2, channels), bf16),
-            pltpu.VMEM((members - 1, total_rows // batch_count, channels), bf16),
+            pltpu.VMEM((total_rows, channels), bf16),
             dma((8,)),
             dma((2,)),
             dma((8,)),
@@ -1168,8 +1155,8 @@
     )(lengths, *arrays)
 
 
-def down_kernel(lows, phases, out, held, columns, in_sems, out_sems):
-    count = lows.shape[2]
+def down_kernel(line, lows, phases, out, held, columns, in_sems, out_sems):
+    count = lows.shape[1]
     group, lanes = held.shape[1], held.shape[4]
     rows = group * held.shape[3]
     tiles = lanes // 128
@@ -1189,9 +1176,12 @@
     after = before = None
     for index, (part, at) in enumerate(items):
         if after is None or groups > 1:
-            turned = [lows[kind, at * rows : (at + 1) * rows].T for kind in range(3)]
-            after = jnp.concatenate([turned[0], turned[1]], axis=0)
-            before = jnp.concatenate([turned[0], turned[2]], axis=0)
+            rows_here = lows[at * rows : (at + 1) * rows, :].astype(jnp.float32).T
+            place = lax.rem(lax.broadcasted_iota(jnp.int32, rows_here.shape, 1), line)
+            following = jnp.where(place < line - 1, pltpu.roll(rows_here, rows - 1, 1), 0.0)
+            preceding = jnp.where(place > 0, pltpu.roll(rows_here, 1, 1), 0.0)
+            after = jnp.concatenate([rows_here, following], axis=0).astype(lows.dtype)
+            before = jnp.concatenate([rows_here, preceding], axis=0).astype(lows.dtype)
         loads[index].wait()
         for step in range(STRIDE):
             block = held[index % 2, :, step].reshape(rows, lanes)
@@ -1219,13 +1209,13 @@
         store.wait()
 
 
-def down_gradient(lows, phases):
+def down_gradient(lows, phases, line):
     devices, _, rows, channels = phases.shape
-    count = lows.shape[2]
+    count = lows.shape[1]
     lanes = 256
     hbm = pl.BlockSpec(memory_space=pl.ANY)
     return pl.pallas_call(
-        down_kernel,
+        functools.partial(down_kernel, line),
         out_shape=jax.ShapeDtypeStruct((count * 2 * STRIDE, channels), jnp.float32),
         in_specs=[pl.BlockSpec(memory_space=pltpu.VMEM), hbm],
         out_specs=hbm,
@@ -1297,12 +1287,7 @@
 
     share = latent_count // time_count
     all_phases = all_phases.reshape((-1,) + all_phases.shape[2:])
-    line = all_low.reshape(batch_count * crop_count, time_count * frame_count, share)
-    after = jnp.pad(line[:, 1:], ((0, 0), (0, 1), (0, 0)))
-    before = jnp.pad(line[:, :-1], ((0, 0), (1, 0), (0, 0)))
-    lows = jnp.stack([line, after, before])
-    lows = lows.reshape(3, -1, share)
-
+    lows = all_low.reshape(-1, share)
     wide_of = latent_count // time_count
     small = summed[:128].astype(jnp.float32)
     small = jnp.concatenate([small[:, :wide_of], small[:, wide_of : 2 * wide_of]], axis=0)
@@ -1323,7 +1308,7 @@
     wide_out = wide_out.reshape(3, TAPS, narrow_of, channel_count)
     wide_out = jnp.swapaxes(wide_out, 1, 2)
     narrow_out = units[:, TAPS * narrow_of :].astype(jnp.float32)
-    down_out = down_gradient(lows, all_phases).reshape(share, tap_count, channel_count)
+    down_out = down_gradient(lows, all_phases, time_count * frame_count).reshape(share, tap_count, channel_count)
     return (
         quantized,
         commit,

time: 210 us -> 191 us (0.910)
  Pallas kernels: 190 us -> 175 us
    pallas_call x1, Pallas kernels: 178 us -> 163 us  [run_block(): pl.pallas_call(functools.partial(block_kernel, time_count, batch_count, p...]
    unnamed x17 -> x15, local copies, waits for them, and re-layouts: 5.14 us -> 5.13 us
where the time goes in v4:
time: 191 us
  Pallas kernels  175 us (92%)
  local copies, waits for them, and re-layouts  8.65 us (5%)
  other arithmetic  6.48 us (3%)
    pallas_call x1, Pallas kernels, run_block(): pl.pallas_call(functools.partial(block_kernel, time_count, batch_count, p...  163 us
    pallas_call x1, Pallas kernels, down_gradient(): pl.pallas_call(functools.partial(down_kernel, line), out_shape=jax.ShapeD...  11.9 us
    unnamed x15, local copies, waits for them, and re-layouts  5.13 us

profile of v4, /device:TPU:0, one launch (start us, length us, event | category | flops | bytes accessed | tf_op | source)
XLA Modules:
  0.0 190.7 jit_solution(2708848279994249902)
XLA Ops:
  0.6 0.8 copy.37
  1.4 0.8 copy.38
  2.2 0.7 select_maximum_fusion.coded
  2.9 0.8 copy.39
  3.7 0.6 reshape.76.in_bias
  4.3 162.9 %shard_map.280 = (f32[2,16,1024]{2,1,0:T(8,128)}, f32[2,16,128]{2,1,0:T(8,128)}, f32[2,512,128]{2,1,0:T(8,128)}, bf16[3200,512]{1,0:T(8,128)(2,1)}, bf16[8,4,8,3...) custom-call(s32[2]{0:T(128)} %lengths.1, f32[2,512,128]{2,1,0:T(8,128)} %signal.1, f32[2,16,1024]{2,1,0:T(8,128)} %quant_cot.1, ...), custom_call_target="tpu_custom_call" | custom-call | tf_op jit(solution)/shard_map/pallas_call | solution.py:1078
  167.2 0.9 slice_convert_fusion.1
  168.2 0.7 slice_bitcast_fusion
  168.9 0.1 reshape_squeeze.3
  168.9 0.1 constant_dynamic-slice_fusion
  169.0 0.7 copy.41
  169.7 0.6 slice.84
  170.3 0.6 slice.78
  170.9 0.0 copy-start
  170.9 11.9 %shard_map.281 = f32[4096,512]{1,0:T(8,128)} custom-call(bf16[1024,256]{1,0:T(8,128)(2,1)} %bitcast.33, bf16[32,8,32,512]{3,2,1,0:T(8,128)(2,1)} %bitcast.31), custom_call_target="tpu_custom_call" | custom-call | tf_op jit(solution)/shard_map/pallas_call | solution.py:1217
  182.8 0.0 copy-done
  182.8 0.6 fusion.2
  183.4 0.2 slice.57
  183.6 0.2 slice.73
  183.8 0.0 copy-start.3
  183.8 0.0 copy-start.2
  183.8 0.0 copy-start.1
  183.8 3.2 %convert_bitcast_fusion = f32[3,128,7,512]{3,1,2,0:T(8,128)} fusion(bf16[3,7,128,512]{3,2,1,0:T(8,128)(2,1)S(1)} %bitcast.30), kind=kLoop, calls=%fused_computation | loop fusion | flops 1376256 | bytes 8257536 | tf_op jit(solution)/shard_map/transpose | solution.py:1309
  187.0 1.0 slice_convert_fusion
  188.0 0.6 slice.77
  188.6 0.0 copy-done.3
  188.6 0.7 copy.40
  189.3 0.0 copy-done.2
  189.3 0.7 copy.44
  189.9 0.0 copy-done.1
  189.9 0.8 copy.45
  (5 shorter events, 0.1 us)
Async XLA Ops:
  170.9 11.9 %copy-start = (bf16[3200,512]{1,0:T(8,128)(2,1)S(1)}, bf16[3200,512]{1,0:T(8,128)(2,1)}, u32[]{:S(2)}) copy-start(bf16[3200,512]{1,0:T(8,128)(2,1)} %get-tuple-element.24) | copy-start | bytes 9830404
  183.8 4.8 %copy-start.3 = (f32[2,16,128]{2,1,0:T(8,128)S(1)}, f32[2,16,128]{2,1,0:T(8,128)}, u32[]{:S(2)}) copy-start(f32[2,16,128]{2,1,0:T(8,128)} %get-tuple-element.22) | copy-start | bytes 49156
  183.8 5.5 %copy-start.2 = (f32[2,16,1024]{2,1,0:T(8,128)S(1)}, f32[2,16,1024]{2,1,0:T(8,128)}, u32[]{:S(2)}) copy-start(f32[2,16,1024]{2,1,0:T(8,128)} %get-tuple-element.79) | copy-start | bytes 393220
  183.8 6.1 %copy-start.1 = (f32[2,512,128]{2,1,0:T(8,128)S(1)}, f32[2,512,128]{2,1,0:T(8,128)}, u32[]{:S(2)}) copy-start(f32[2,512,128]{2,1,0:T(8,128)} %get-tuple-element.81) | copy-start | bytes 1572868

commit v5 on v4

--- a/solution.py
+++ b/solution.py
@@ -916,19 +916,18 @@
             lows_members()
             for step in near_first[2:]:
                 forward_pair(step)
-        else:
-            relay(unit + 1)
-            if unit == 1:
-                lows_pair()
-            unit_gradient(unit + 1)
-
-    def finish_all():
+        elif unit == 1:
+            lows_pair()
+
+    def finish_all(between_waves):
         order = numbers[2] + numbers[1] + numbers[0] + [0]
         stages = [functools.partial(advance, stage) for stage in range(2 * levels)]
         for wave in range(len(order) + len(stages)):
             for depth, stage in enumerate(stages):
                 if 0 <= wave - depth < len(order):
                     stage(order[wave - depth])
+            if wave in between_waves:
+                between_waves[wave]()
             if wave < members:
                 forward_across(([0] + near_first)[wave])
         for step in ([0] + near_first)[len(order) + len(stages) :]:
@@ -1013,8 +1012,11 @@
         )
         for step in range(1, time_count)
     ]
-    relay(0)
-    unit_gradient(0)
+    relay(2)
+    unit_gradient(2)
+    smalls_in = quantizer_gradient()
+    relay(1)
+    unit_gradient(1)
     swap_back = swap(
         4,
         lambda part: signal_out.at[pl.ds(part * length, length)],
@@ -1022,20 +1024,25 @@
         mine,
         True,
     )
-    small_gradient(quantizer_gradient())
-    for copy in alphas_in:
-        copy.wait_recv()
-    alpha_rows = alpha_out[time]
-    for step in range(time_count - 1):
-        alpha_rows += alpha_in[step]
-    rest = [alpha_rows] + [bias_rows[unit][kind] for kind in range(2) for unit in range(3)]
-    rest = jnp.concatenate(rest + [jnp.zeros((2, share), f32)], axis=0)
-    small[0, small.shape[1] - 16 :, channels - share :] = rest
-    for start in range(0, pieces[0][1], small.shape[1]):
-        total[start : start + small.shape[1], :] = small[0].astype(bf16)
-    send_pair(0)
-
-    finish_all()
+    small_gradient(smalls_in)
+    def first_unit():
+        relay(0)
+        unit_gradient(0)
+
+    def last_piece():
+        for copy in alphas_in:
+            copy.wait_recv()
+        alpha_rows = alpha_out[time]
+        for step in range(time_count - 1):
+            alpha_rows += alpha_in[step]
+        rest = [alpha_rows] + [bias_rows[unit][kind] for kind in range(2) for unit in range(3)]
+        rest = jnp.concatenate(rest + [jnp.zeros((2, share), f32)], axis=0)
+        small[0, small.shape[1] - 16 :, channels - share :] = rest
+        for start in range(0, pieces[0][1], small.shape[1]):
+            total[start : start + small.shape[1], :] = small[0].astype(bf16)
+        send_pair(0)
+
+    finish_all({0: first_unit, 1: last_piece})
     swapped_in(swap_back)
     swapped_in(swap_commit)
     for crop in range(crops):
@@ -1155,7 +1162,38 @@
     )(lengths, *arrays)
 
 
-def down_kernel(line, lows, phases, out, held, columns, in_sems, out_sems):
+def down_kernel(
+    line,
+    count_small,
+    start,
+    lows,
+    phases,
+    summed,
+    quantized,
+    signal_grad,
+    out,
+    wide_out,
+    narrow_out,
+    quantized_out,
+    signal_out,
+    in_weight_out,
+    codebook_out,
+    out_weight_out,
+    bias_out,
+    down_bias,
+    in_bias,
+    alpha_out,
+    wide_bias,
+    narrow_bias,
+    held,
+    columns,
+    sums,
+    wide,
+    narrow,
+    in_sems,
+    out_sems,
+    sum_sems,
+):
     count = lows.shape[1]
     group, lanes = held.shape[1], held.shape[4]
     rows = group * held.shape[3]
@@ -1170,18 +1208,50 @@
         )
         for index, (part, at) in enumerate(items)
     ]
+    bring = pltpu.make_async_copy(summed, sums, sum_sems.at[0])
+    bring.start()
     for load in loads[:2]:
         load.start()
+    def turned_rows(at):
+        rows_here = lows[at * rows : (at + 1) * rows, :].astype(jnp.float32).T
+        place = lax.rem(lax.broadcasted_iota(jnp.int32, rows_here.shape, 1), line)
+        following = jnp.where(place < line - 1, pltpu.roll(rows_here, rows - 1, 1), 0.0)
+        preceding = jnp.where(place > 0, pltpu.roll(rows_here, 1, 1), 0.0)
+        after = jnp.concatenate([rows_here, following], axis=0).astype(lows.dtype)
+        before = jnp.concatenate([rows_here, preceding], axis=0).astype(lows.dtype)
+        return after, before
+
     stores = []
-    after = before = None
+    first_rows = turned_rows(0)
+    quantized_out[...] = quantized[...]
+    signal_out[...] = signal_grad[...]
+    bring.wait()
+    f32 = jnp.float32
+    units, share, channels = narrow.shape
+    for unit in range(units):
+        at = start + unit * (TAPS + 1) * share
+        for tap in range(TAPS):
+            wide[unit, tap] = sums[at + tap * share : at + (tap + 1) * share, :].astype(f32)
+        narrow[unit] = sums[at + TAPS * share : at + (TAPS + 1) * share, :].astype(f32)
+    stores.append(pltpu.make_async_copy(wide, wide_out, sum_sems.at[1]))
+    stores.append(pltpu.make_async_copy(narrow, narrow_out, sum_sems.at[2]))
+    for store in stores:
+        store.start()
+    small = jnp.concatenate([sums[:128, :count], sums[:128, count : 2 * count]], axis=0).astype(f32)
+    for kind, ref in enumerate((in_weight_out, codebook_out, out_weight_out)):
+        ref[...] = small[kind * count_small : (kind + 1) * count_small]
+    row = 3 * count_small + bias_out.shape[0]
+    bias_out[...] = small[3 * count_small : row]
+    down_bias[...] = small[row : row + 1]
+    in_bias[...] = small[row + 1 : row + 2]
+    last = small[240:256, count - share : count]
+    alpha_out[...] = last[:7]
+    wide_bias[...] = last[8:11]
+    narrow_bias[...] = last[11:14]
+    after, before = first_rows
     for index, (part, at) in enumerate(items):
-        if after is None or groups > 1:
-            rows_here = lows[at * rows : (at + 1) * rows, :].astype(jnp.float32).T
-            place = lax.rem(lax.broadcasted_iota(jnp.int32, rows_here.shape, 1), line)
-            following = jnp.where(place < line - 1, pltpu.roll(rows_here, rows - 1, 1), 0.0)
-            preceding = jnp.where(place > 0, pltpu.roll(rows_here, 1, 1), 0.0)
-            after = jnp.concatenate([rows_here, following], axis=0).astype(lows.dtype)
-            before = jnp.concatenate([rows_here, preceding], axis=0).astype(lows.dtype)
+        if index > 0 and groups > 1:
+            after, before = turned_rows(at)
         loads[index].wait()
         for step in range(STRIDE):
             block = held[index % 2, :, step].reshape(rows, lanes)
@@ -1209,24 +1279,47 @@
         store.wait()
 
 
-def down_gradient(lows, phases, line):
+def down_gradient(lows, phases, line, summed, start, share, count_small, phase_count, quantized, signal_grad):
     devices, _, rows, channels = phases.shape
     count = lows.shape[1]
     lanes = 256
+    f32 = jnp.float32
     hbm = pl.BlockSpec(memory_space=pl.ANY)
+    vmem = pl.BlockSpec(memory_space=pltpu.VMEM)
+    wide = (3, TAPS, share, channels)
+    shapes = [
+        (count * 2 * STRIDE, channels),
+        wide,
+        (3, share, channels),
+        quantized.shape,
+        signal_grad.shape,
+        (count_small, count),
+        (count_small, count),
+        (count_small, count),
+        (phase_count, count),
+        (1, count),
+        (1, count),
+        (7, share),
+        (3, share),
+        (3, share),
+    ]
     return pl.pallas_call(
-        functools.partial(down_kernel, line),
-        out_shape=jax.ShapeDtypeStruct((count * 2 * STRIDE, channels), jnp.float32),
-        in_specs=[pl.BlockSpec(memory_space=pltpu.VMEM), hbm],
-        out_specs=hbm,
+        functools.partial(down_kernel, line, count_small, start),
+        out_shape=[jax.ShapeDtypeStruct(shape, f32) for shape in shapes],
+        in_specs=[vmem, hbm, hbm, vmem, vmem],
+        out_specs=[hbm] * 3 + [vmem] * (len(shapes) - 3),
         scratch_shapes=[
             pltpu.VMEM((2, min(devices, 32), STRIDE, rows, lanes), phases.dtype),
-            pltpu.VMEM((channels // 128, count * 2 * STRIDE, 128), jnp.float32),
+            pltpu.VMEM((channels // 128, count * 2 * STRIDE, 128), f32),
+            pltpu.VMEM(summed.shape, summed.dtype),
+            pltpu.VMEM(wide, f32),
+            pltpu.VMEM((3, share, channels), f32),
             pltpu.SemaphoreType.DMA((2,)),
             pltpu.SemaphoreType.DMA((channels // 128,)),
+            pltpu.SemaphoreType.DMA((3,)),
         ],
         compiler_params=pltpu.CompilerParams(vmem_limit_bytes=60 * 2**20),
-    )(lows, phases)
+    )(lows, phases, summed, quantized, signal_grad)
 
 
 def body(
@@ -1288,27 +1381,29 @@
     share = latent_count // time_count
     all_phases = all_phases.reshape((-1,) + all_phases.shape[2:])
     lows = all_low.reshape(-1, share)
-    wide_of = latent_count // time_count
-    small = summed[:128].astype(jnp.float32)
-    small = jnp.concatenate([small[:, :wide_of], small[:, wide_of : 2 * wide_of]], axis=0)
-    in_weight_out = small[:count].reshape(phases, dims, -1)
-    codebook_out = small[count : 2 * count].reshape(phases, dims, -1)
-    out_weight_out = small[2 * count : 3 * count].reshape(phases, dims, -1)
-    row = 3 * count + phases
-    out_bias_out = small[3 * count : row]
-    down_bias_out = small[row]
-    narrow_of = channel_count // time_count
-    in_bias_all = small[row + 1, :count].reshape(phases, dims)
+    results = down_gradient(
+        lows,
+        all_phases,
+        time_count * frame_count,
+        summed,
+        small_rows,
+        channel_count // time_count,
+        count,
+        phases,
+        quantized,
+        signal_grad,
+    )
+    down_out, wide_out, narrow_out, quantized, signal_grad = results[:5]
+    out_bias_out, down_bias_out, in_bias_row, alpha_out, wide_bias_out, narrow_bias_out = results[8:]
+    down_out = down_out.reshape(share, tap_count, channel_count)
+    wide_out = jnp.swapaxes(wide_out, 1, 2)
+    in_weight_out, codebook_out, out_weight_out = (
+        rows.reshape(phases, dims, -1) for rows in results[5:8]
+    )
+    down_bias_out = down_bias_out.reshape(-1)
+    in_bias_all = in_bias_row[0, :count].reshape(phases, dims)
     part = dims // time_count
     in_bias_out = lax.dynamic_slice_in_dim(in_bias_all, lax.axis_index("tm") * part, part, axis=1)
-    last = summed[112:128, -narrow_of:].astype(jnp.float32)
-    alpha_out, wide_bias_out, narrow_bias_out = last[:7], last[8:11], last[11:14]
-    units = summed[small_rows:].reshape(3, unit_rows, channel_count)
-    wide_out = units[:, : TAPS * narrow_of].astype(jnp.float32)
-    wide_out = wide_out.reshape(3, TAPS, narrow_of, channel_count)
-    wide_out = jnp.swapaxes(wide_out, 1, 2)
-    narrow_out = units[:, TAPS * narrow_of :].astype(jnp.float32)
-    down_out = down_gradient(lows, all_phases, time_count * frame_count).reshape(share, tap_count, channel_count)
     return (
         quantized,
         commit,

time: 191 us -> 179 us (0.937)
  other arithmetic: 6.48 us -> 0.69 us
  Pallas kernels: 175 us -> 171 us
  local copies, waits for them, and re-layouts: 8.65 us -> 5.81 us
    pallas_call x1, Pallas kernels: 163 us -> 157 us  [run_block(): pl.pallas_call(functools.partial(block_kernel, time_count, batch_count, p...]
    transpose x1 -> x0, other arithmetic: 3.2 us -> none  [body(): wide_out = jnp.swapaxes(wide_out, 1, 2)]
    pallas_call x1, Pallas kernels: 11.9 us -> 14.4 us  [down_gradient(): pl.pallas_call(functools.partial(down_kernel, line, count_small, start),...]
    slice x8 -> x1, local copies, waits for them, and re-layouts: 2.77 us -> 0.67 us  [body(): in_bias_all = in_bias_row[0, :count].reshape(phases, dims)]
    unnamed x15 -> x5, local copies, waits for them, and re-layouts: 5.13 us -> 3.67 us
where the time goes in v5:
time: 179 us
  Pallas kernels  171 us (96%)
  local copies, waits for them, and re-layouts  5.81 us (3%)
    pallas_call x1, Pallas kernels, run_block(): pl.pallas_call(functools.partial(block_kernel, time_count, batch_count, p...  157 us
    pallas_call x1, Pallas kernels, down_gradient(): pl.pallas_call(functools.partial(down_kernel, line, count_small, start),...  14.4 us
    unnamed x5, local copies, waits for them, and re-layouts  3.67 us

profile of v5, /device:TPU:0, one launch (start us, length us, event | category | flops | bytes accessed | tf_op | source)
XLA Modules:
  0.0 178.7 jit_solution(3798469228436444714)
XLA Ops:
  0.6 0.8 copy.39
  1.4 0.6 reshape.72.in_bias
  2.0 0.8 copy.38
  2.8 0.8 copy.37
  3.6 0.7 select_maximum_fusion.coded
  4.3 157.1 %shard_map.280 = (f32[2,16,1024]{2,1,0:T(8,128)}, f32[2,16,128]{2,1,0:T(8,128)}, f32[2,512,128]{2,1,0:T(8,128)}, bf16[3200,512]{1,0:T(8,128)(2,1)}, bf16[8,4,8,3...) custom-call(s32[2]{0:T(128)} %lengths.1, f32[2,512,128]{2,1,0:T(8,128)} %signal.1, f32[2,16,1024]{2,1,0:T(8,128)} %quant_cot.1, ...), custom_call_target="tpu_custom_call" | custom-call | tf_op jit(solution)/shard_map/pallas_call | solution.py:1085
  161.3 0.7 slice_bitcast_fusion
  162.0 0.7 copy.40
  162.7 14.4 %shard_map.281 = (f32[4096,512]{1,0:T(8,128)}, f32[3,7,128,512]{3,2,1,0:T(8,128)}, f32[3,128,512]{2,1,0:T(8,128)}, f32[2,16,1024]{2,1,0:T(8,128)}, f32[2,512,128...) custom-call(bf16[1024,256]{1,0:T(8,128)(2,1)} %bitcast.22, ...), custom_call_target="tpu_custom_call" | custom-call | tf_op jit(solution)/shard_map/pallas_call | solution.py:1306
  177.2 0.7 slice_reduce_fusion
  177.9 0.1 reshape_squeeze.3
  177.9 0.1 constant_dynamic-slice_fusion
  178.0 0.7 copy.41
  (1 shorter events, 0.0 us)
